TPU v7x, 32 devices: a whole 2x2x4 slice. The times are simulated.
32 devices in a mesh: dp: 2 (over x), row: 4 (over y, core), col: 4 (over z).
Axes of the slice: x: 2, y: 2, z: 4, core: 2. Of those that a mesh axis runs over, the one named last changes fastest.
Arguments:
- tokens: bfloat16 [20, 32, 32, 768], P('dp', 'row', 'col')
- cot_tokens: bfloat16 [20, 32, 32, 768], P('dp', 'row', 'col'), may hold values from -6 to 6
- cot_merged: bfloat16 [20, 64, 64, 256], P('dp', 'row', 'col'), may hold values from -6 to 6
- image_counts: int32 [2], P('dp'), may hold values from 5 to 10, as said below
- scale_flags: int32 [20], P('dp'), may hold values from 0 to 3
- shift_flags: int32 [20], P('dp'), may hold values from -1 to 1
- qkv_w: float32 [768, 2304], P('dp'), may hold values from -0.21875 to 0.21875
- attn_out_w: float32 [768, 768], P('dp'), may hold values from -2.5 to 2.5
- fc1_w: float32 [768, 3072], P('dp'), may hold values from -0.21875 to 0.21875
- fc1_b: float32 [3072], P('dp'), may hold values from -3 to 3
- fc2_w: float32 [3072, 768], P('dp'), may hold values from -0.109375 to 0.109375
- fc2_b: float32 [768], P('dp'), may hold values from -2 to 2
- ln1_gain: float32 [768], P('dp'), may hold values from 0.25 to 1.75
- ln1_bias: float32 [768], P('dp'), may hold values from -2 to 2
- ln2_gain: float32 [768], P('dp'), may hold values from 0.25 to 1.75
- ln2_bias: float32 [768], P('dp'), may hold values from -2 to 2
- proj_w: float32 [768, 256], P('dp'), may hold values from -0.21875 to 0.21875
- conv_w: float32 [4, 3, 3, 256, 256], P(None, None, None, 'dp'), may hold values from -0.125 to 0.125
- head_w: float32 [256, 256], P('dp'), may hold values from -0.375 to 0.375
- head_b: float32 [256], P('dp'), may hold values from -3 to 3
- shift_row: float32 [256], P('dp'), may hold values from -4 to 4
Outputs:
- tokens_out: bfloat16 [20, 32, 32, 768], P('dp', 'row', 'col')
- merged_out: bfloat16 [20, 64, 64, 256], P('dp', 'row', 'col')
- grad_tokens: float32 [20, 32, 32, 768], P('dp', 'row', 'col')
- grad_qkv_w: float32 [768, 2304], P('dp')
- grad_attn_out_w: float32 [768, 768], P('dp')
- grad_fc1_w: float32 [768, 3072], P('dp')
- grad_fc1_b: float32 [3072], P('dp')
- grad_fc2_w: float32 [3072, 768], P('dp')
- grad_fc2_b: float32 [768], P('dp')
- grad_ln1_gain: float32 [768], P('dp')
- grad_ln1_bias: float32 [768], P('dp')
- grad_ln2_gain: float32 [768], P('dp')
- grad_ln2_bias: float32 [768], P('dp')
- grad_proj_w: float32 [768, 256], P('dp')
- grad_conv_w: float32 [4, 3, 3, 256, 256], P(None, None, None, 'dp')
- grad_head_w: float32 [256, 256], P('dp')
- grad_head_b: float32 [256], P('dp')
- grad_shift_row: float32 [256], P('dp')
Inputs may be any that keep to these rules, and one draw needn't show every extreme that they name: `image_counts`: slots of a group below its count hold images, the rest are empty; some group is full and another holds the least count.
All inputs are finite; a program needn't handle non-finite values.
Results may differ from a plain program's by a relative error of at most 0.024.
Values may be sent and summed in bfloat16 or wider, within the bound.
A program may use at most 384 MiB of HBM per device.

v0:
```python
import jax
import jax.numpy as jnp
from jax import lax
from jax.sharding import PartitionSpec as P

HEADS = 12
HEAD_DIM = 64


epsilon = 1e-06


def extended(value, sides, width):
    for axis, dim in sides:
        peers, length = (lax.axis_size(axis), value.shape[dim])
        up = [(i, (i + 1) % peers) for i in range(peers - 1)]
        down = [(j, i) for i, j in up]
        last = lax.slice_in_dim(value, length - width, length, axis=dim)
        leading = lax.slice_in_dim(value, 0, width, axis=dim)
        before = lax.ppermute(last, axis, up)
        after = lax.ppermute(leading, axis, down)
        value = jnp.concatenate([before, value, after], axis=dim)
    return value


def norm_rows(stream, gain_row, bias_row):
    centre = stream - jnp.mean(stream, -1, keepdims=True)
    spread = jnp.mean(centre * centre, -1, keepdims=True)
    factor = lax.rsqrt(spread + epsilon)
    scaled = centre * factor
    return (scaled * gain_row + bias_row, scaled, factor)


def norm_back(cotangent, scaled, factor, gain_row):
    gained = cotangent * gain_row
    inner = (
        gained
        - jnp.mean(gained, -1, keepdims=True)
        - scaled * jnp.mean(gained * scaled, -1, keepdims=True)
    )
    return (factor * inner, jnp.sum(cotangent * scaled, 0), jnp.sum(cotangent, 0))


def gelu_grad(inputs, cotangent):
    return jax.vjp(jax.nn.gelu, inputs)[1](cotangent)[0]


def outer_product(first_op, second_op):
    return lax.dot_general(
        first_op, second_op, (((0,), (0,)), ((), ())), preferred_element_type=jnp.float32
    )


def back_product(first_op, weight):
    return lax.dot_general(
        first_op, weight, (((1,), (1,)), ((), ())), preferred_element_type=jnp.float32
    )


def add_rims(tile_map):
    return extended(tile_map, (("row", 1), ("col", 2)), 1)


def clamp_edges(padded):
    first_row = lax.axis_index("row") == 0
    last_row = lax.axis_index("row") == lax.axis_size("row") - 1
    upper = jnp.where(first_row, padded[:, 1:2], padded[:, 0:1])
    lower = jnp.where(last_row, padded[:, -2:-1], padded[:, -1:])
    padded = jnp.concatenate([upper, padded[:, 1:-1], lower], 1)
    first_col = lax.axis_index("col") == 0
    last_col = lax.axis_index("col") == lax.axis_size("col") - 1
    left_side = jnp.where(first_col, padded[:, :, 1:2], padded[:, :, 0:1])
    right_side = jnp.where(last_col, padded[:, :, -2:-1], padded[:, :, -1:])
    return jnp.concatenate([left_side, padded[:, :, 1:-1], right_side], 2)


def patches(padded):
    tall = padded.shape[1] - 2
    broad = padded.shape[2] - 2
    pieces = [
        padded[:, row_shift : row_shift + tall, col_shift : col_shift + broad]
        for row_shift in range(3)
        for col_shift in range(3)
    ]
    return jnp.concatenate(pieces, -1).reshape(-1, 9 * padded.shape[3])


def conv_apply(padded, kernel):
    result = jnp.dot(
        patches(padded), kernel.reshape(-1, kernel.shape[3]), preferred_element_type=jnp.float32
    )
    return result.reshape(padded.shape[0], padded.shape[1] - 2, padded.shape[2] - 2, -1)


def flip_kernel(kernel):
    return jnp.transpose(kernel[::-1, ::-1], (0, 1, 3, 2))


def double_axis(padded, axis_index):
    leading = jnp.moveaxis(padded, axis_index, 0)
    middle_part = leading[1:-1]
    even_part = 0.75 * middle_part + 0.25 * leading[:-2]
    odd_part = 0.75 * middle_part + 0.25 * leading[2:]
    joined = jnp.stack([even_part, odd_part], 1).reshape(
        (2 * middle_part.shape[0],) + middle_part.shape[1:]
    )
    return jnp.moveaxis(joined, 0, axis_index)


def halve_axis(padded, axis_index):
    leading = jnp.moveaxis(padded, axis_index, 0)
    even_part = leading[1:-1:2]
    odd_part = leading[2:-1:2]
    before_part = leading[0:-2:2]
    after_part = leading[3::2]
    joined = 0.75 * (even_part + odd_part) + 0.25 * (before_part + after_part)
    return jnp.moveaxis(joined, 0, axis_index)


def on_device(
    tokens,
    cot_tokens,
    cot_merged,
    image_counts,
    scale_flags,
    shift_flags,
    qkv_w,
    attn_out_w,
    fc1_w,
    fc1_b,
    fc2_w,
    fc2_b,
    ln1_gain,
    ln1_bias,
    ln2_gain,
    ln2_bias,
    proj_w,
    conv_w,
    head_w,
    head_b,
    shift_row,
):
    lowered = [
        master.astype(jnp.bfloat16)
        for master in (
            qkv_w,
            attn_out_w,
            fc1_w,
            fc1_b,
            fc2_w,
            fc2_b,
            ln1_gain,
            ln1_bias,
            ln2_gain,
            ln2_bias,
            proj_w,
            conv_w,
            head_w,
            head_b,
            shift_row,
        )
    ]
    gathered = (
        lax.all_gather(lowered[0], "dp", axis=0, tiled=True),
        lax.all_gather(lowered[1], "dp", axis=0, tiled=True),
        lax.all_gather(lowered[2], "dp", axis=0, tiled=True),
        lax.all_gather(lowered[3], "dp", axis=0, tiled=True),
        lax.all_gather(lowered[4], "dp", axis=0, tiled=True),
        lax.all_gather(lowered[5], "dp", axis=0, tiled=True),
        lax.all_gather(lowered[6], "dp", axis=0, tiled=True),
        lax.all_gather(lowered[7], "dp", axis=0, tiled=True),
        lax.all_gather(lowered[8], "dp", axis=0, tiled=True),
        lax.all_gather(lowered[9], "dp", axis=0, tiled=True),
        lax.all_gather(lowered[10], "dp", axis=0, tiled=True),
        lax.all_gather(lowered[11], "dp", axis=3, tiled=True),
        lax.all_gather(lowered[12], "dp", axis=0, tiled=True),
        lax.all_gather(lowered[13], "dp", axis=0, tiled=True),
        lax.all_gather(lowered[14], "dp", axis=0, tiled=True),
    )
    (
        w_qkv,
        w_out,
        w_up,
        b_up,
        w_down,
        b_down,
        gain_one,
        bias_one,
        gain_two,
        bias_two,
        w_proj,
        w_conv,
        w_head,
        b_head,
        w_shift,
    ) = gathered
    images = tokens.shape[0]
    tile_rows = tokens.shape[1]
    tile_cols = tokens.shape[2]
    tile_size = tile_rows * tile_cols
    model_width = tokens.shape[3]
    temper = HEAD_DIM ** (-0.5)
    present = (jnp.arange(images) < image_counts[0]).astype(jnp.float32)
    factor = 0.5 + 0.5 * scale_flags.astype(jnp.float32)
    shift_sign = shift_flags.astype(jnp.float32)
    present_rows = jnp.repeat(present, tile_size)[:, None]
    stream = tokens.astype(jnp.float32).reshape(-1, model_width)
    normed, scaled_one, factor_one = norm_rows(
        stream, gain_one.astype(jnp.float32), bias_one.astype(jnp.float32)
    )
    normed_low = normed.astype(jnp.bfloat16)
    projected = jnp.dot(normed_low, w_qkv, preferred_element_type=jnp.float32).astype(jnp.bfloat16)
    queries = projected[:, :model_width].reshape(images, tile_size, HEADS, HEAD_DIM)
    keys_own = projected[:, model_width : 2 * model_width].reshape(images, tile_size, model_width)
    values_own = projected[:, 2 * model_width :].reshape(images, tile_size, model_width)
    keys_all, values_all = (
        lax.all_gather(keys_own, ("row", "col"), axis=1, tiled=True),
        lax.all_gather(values_own, ("row", "col"), axis=1, tiled=True),
    )
    keys_heads = keys_all.reshape(images, -1, HEADS, HEAD_DIM)
    values_heads = values_all.reshape(images, -1, HEADS, HEAD_DIM)
    scores = (
        jnp.einsum("nqhd,nkhd->nhqk", queries, keys_heads, preferred_element_type=jnp.float32)
        * temper
    )
    highest_score = jnp.max(scores, -1, keepdims=True)
    exponent = jnp.exp(scores - highest_score)
    denominator = jnp.sum(exponent, -1, keepdims=True)
    log_total = highest_score + jnp.log(denominator)
    attention_low = (exponent / denominator).astype(jnp.bfloat16)
    attended = jnp.einsum(
        "nhqk,nkhd->nqhd", attention_low, values_heads, preferred_element_type=jnp.float32
    )
    attended = attended.reshape(-1, model_width).astype(jnp.bfloat16)
    after_attn = stream + jnp.dot(attended, w_out, preferred_element_type=jnp.float32)
    normed_two, scaled_two, factor_two = norm_rows(
        after_attn, gain_two.astype(jnp.float32), bias_two.astype(jnp.float32)
    )
    normed_two_low = normed_two.astype(jnp.bfloat16)
    hidden = jnp.dot(normed_two_low, w_up, preferred_element_type=jnp.float32) + b_up.astype(
        jnp.float32
    )
    hidden_low = jax.nn.gelu(hidden).astype(jnp.bfloat16)
    after_mlp = after_attn + (
        jnp.dot(hidden_low, w_down, preferred_element_type=jnp.float32) + b_down.astype(jnp.float32)
    )
    tokens_low = after_mlp.astype(jnp.bfloat16)
    tokens_out = (
        (tokens_low.astype(jnp.float32) * present_rows).astype(jnp.bfloat16).reshape(tokens.shape)
    )
    feature = jnp.dot(tokens_low, w_proj, preferred_element_type=jnp.float32).reshape(
        images, tile_rows, tile_cols, -1
    )
    channels = feature.shape[3]
    stored = []
    for unit_index in range(2):
        first_in = add_rims(jax.nn.gelu(feature).astype(jnp.bfloat16))
        first_out = conv_apply(first_in, w_conv[2 * unit_index])
        second_in = add_rims(jax.nn.gelu(first_out).astype(jnp.bfloat16))
        second_out = conv_apply(second_in, w_conv[2 * unit_index + 1])
        stored.append((feature, first_in, first_out, second_in))
        feature = feature + second_out
    coarse_map = clamp_edges(add_rims(feature.astype(jnp.bfloat16))).astype(jnp.float32)
    upsampled = double_axis(double_axis(coarse_map, 1), 2).astype(jnp.bfloat16)
    fine_rows = upsampled.reshape(-1, channels)
    head_out = jnp.dot(fine_rows, w_head, preferred_element_type=jnp.float32) + b_head.astype(
        jnp.float32
    )
    head_out = head_out.reshape(images, -1, channels)
    merged = (
        head_out * factor[:, None, None] + shift_sign[:, None, None] * w_shift.astype(jnp.float32)
    ) * present[:, None, None]
    merged_out = merged.astype(jnp.bfloat16).reshape(cot_merged.shape)
    gathered = (
        lax.all_gather(lowered[0], "dp", axis=0, tiled=True),
        lax.all_gather(lowered[1], "dp", axis=0, tiled=True),
        lax.all_gather(lowered[2], "dp", axis=0, tiled=True),
        lax.all_gather(lowered[3], "dp", axis=0, tiled=True),
        lax.all_gather(lowered[4], "dp", axis=0, tiled=True),
        lax.all_gather(lowered[5], "dp", axis=0, tiled=True),
        lax.all_gather(lowered[6], "dp", axis=0, tiled=True),
        lax.all_gather(lowered[7], "dp", axis=0, tiled=True),
        lax.all_gather(lowered[8], "dp", axis=0, tiled=True),
        lax.all_gather(lowered[9], "dp", axis=0, tiled=True),
        lax.all_gather(lowered[10], "dp", axis=0, tiled=True),
        lax.all_gather(lowered[11], "dp", axis=3, tiled=True),
        lax.all_gather(lowered[12], "dp", axis=0, tiled=True),
        lax.all_gather(lowered[13], "dp", axis=0, tiled=True),
        lax.all_gather(lowered[14], "dp", axis=0, tiled=True),
    )
    (
        w_qkv,
        w_out,
        w_up,
        b_up,
        w_down,
        b_down,
        gain_one,
        bias_one,
        gain_two,
        bias_two,
        w_proj,
        w_conv,
        w_head,
        b_head,
        w_shift,
    ) = gathered
    merged_grad = (
        cot_merged.astype(jnp.float32).reshape(images, -1, channels) * present[:, None, None]
    )
    grad_shift = jnp.sum(merged_grad * shift_sign[:, None, None], (0, 1))
    head_grad = (merged_grad * factor[:, None, None]).astype(jnp.bfloat16).reshape(-1, channels)
    grad_head_b = jnp.sum(head_grad.astype(jnp.float32), 0)
    grad_head_w = outer_product(fine_rows, head_grad)
    fine_grad = back_product(head_grad, w_head).astype(jnp.bfloat16).reshape(upsampled.shape)
    spread_grad = clamp_edges(extended(fine_grad, (("row", 1), ("col", 2)), 1)).astype(jnp.float32)
    feature_grad = halve_axis(halve_axis(spread_grad, 1), 2)
    conv_grads = [None, None, None, None]
    for unit_index in (1, 0):
        unit_input, first_in, first_out, second_in = stored[unit_index]
        second_grad = feature_grad.astype(jnp.bfloat16)
        conv_grads[2 * unit_index + 1] = outer_product(
            patches(second_in), second_grad.reshape(-1, channels)
        )
        middle_grad = conv_apply(add_rims(second_grad), flip_kernel(w_conv[2 * unit_index + 1]))
        first_grad = gelu_grad(first_out, middle_grad).astype(jnp.bfloat16)
        conv_grads[2 * unit_index] = outer_product(
            patches(first_in), first_grad.reshape(-1, channels)
        )
        inner_grad = conv_apply(add_rims(first_grad), flip_kernel(w_conv[2 * unit_index]))
        feature_grad = feature_grad + gelu_grad(unit_input, inner_grad)
    grad_conv = jnp.stack(conv_grads).reshape(4, 3, 3, channels, channels)
    proj_grad = feature_grad.astype(jnp.bfloat16).reshape(-1, channels)
    grad_proj = outer_product(tokens_low, proj_grad)
    stream_grad = cot_tokens.astype(jnp.float32).reshape(
        -1, model_width
    ) * present_rows + back_product(proj_grad, w_proj)
    down_grad = stream_grad.astype(jnp.bfloat16)
    grad_down_b = jnp.sum(down_grad.astype(jnp.float32), 0)
    grad_down_w = outer_product(hidden_low, down_grad)
    up_grad = gelu_grad(hidden, back_product(down_grad, w_down)).astype(jnp.bfloat16)
    grad_up_b = jnp.sum(up_grad.astype(jnp.float32), 0)
    grad_up_w = outer_product(normed_two_low, up_grad)
    norm_grad, grad_gain_two, grad_bias_two = norm_back(
        back_product(up_grad, w_up), scaled_two, factor_two, gain_two.astype(jnp.float32)
    )
    stream_grad = stream_grad + norm_grad
    branch_grad = stream_grad.astype(jnp.bfloat16)
    grad_out_w = outer_product(attended, branch_grad)
    attended_grad = (
        back_product(branch_grad, w_out)
        .astype(jnp.bfloat16)
        .reshape(images, tile_size, HEADS, HEAD_DIM)
    )
    keys_heads = keys_all.reshape(images, -1, HEADS, HEAD_DIM)
    values_heads = values_all.reshape(images, -1, HEADS, HEAD_DIM)
    scores = (
        jnp.einsum("nqhd,nkhd->nhqk", queries, keys_heads, preferred_element_type=jnp.float32)
        * temper
    )
    attention_full = jnp.exp(scores - log_total)
    attention_low = attention_full.astype(jnp.bfloat16)
    prob_grad = jnp.einsum(
        "nqhd,nkhd->nhqk", attended_grad, values_heads, preferred_element_type=jnp.float32
    )
    centre = jnp.sum(attention_full * prob_grad, -1, keepdims=True)
    score_grad = (attention_full * (prob_grad - centre)).astype(jnp.bfloat16)
    query_grad = (
        jnp.einsum("nhqk,nkhd->nqhd", score_grad, keys_heads, preferred_element_type=jnp.float32)
        * temper
    )
    key_part = (
        jnp.einsum("nhqk,nqhd->knhd", score_grad, queries, preferred_element_type=jnp.float32)
        * temper
    )
    value_part = jnp.einsum(
        "nhqk,nqhd->knhd", attention_low, attended_grad, preferred_element_type=jnp.float32
    )
    pair_grad = lax.psum_scatter(
        jnp.concatenate(
            [
                key_part.reshape(lax.axis_size(("row", "col")) * tile_size, images, model_width),
                value_part.reshape(lax.axis_size(("row", "col")) * tile_size, images, model_width),
            ],
            2,
        ).astype(jnp.bfloat16),
        ("row", "col"),
        scatter_dimension=0,
        tiled=True,
    ).astype(jnp.float32)
    pair_grad = jnp.transpose(pair_grad, (1, 0, 2))
    mixed_grad = jnp.concatenate([query_grad.reshape(images, tile_size, model_width), pair_grad], 2)
    mixed_grad = mixed_grad.astype(jnp.bfloat16).reshape(-1, 3 * model_width)
    grad_qkv = outer_product(normed_low, mixed_grad)
    norm_grad, grad_gain_one, grad_bias_one = norm_back(
        back_product(mixed_grad, w_qkv), scaled_one, factor_one, gain_one.astype(jnp.float32)
    )
    input_grad = (stream_grad + norm_grad).reshape(tokens.shape)
    shards = (
        lax.psum_scatter(
            grad_qkv.astype(jnp.bfloat16), "dp", scatter_dimension=0, tiled=True
        ).astype(jnp.float32),
        lax.psum_scatter(
            grad_out_w.astype(jnp.bfloat16), "dp", scatter_dimension=0, tiled=True
        ).astype(jnp.float32),
        lax.psum_scatter(
            grad_up_w.astype(jnp.bfloat16), "dp", scatter_dimension=0, tiled=True
        ).astype(jnp.float32),
        lax.psum_scatter(
            grad_up_b.astype(jnp.bfloat16), "dp", scatter_dimension=0, tiled=True
        ).astype(jnp.float32),
        lax.psum_scatter(
            grad_down_w.astype(jnp.bfloat16), "dp", scatter_dimension=0, tiled=True
        ).astype(jnp.float32),
        lax.psum_scatter(
            grad_down_b.astype(jnp.bfloat16), "dp", scatter_dimension=0, tiled=True
        ).astype(jnp.float32),
        lax.psum_scatter(
            grad_gain_one.astype(jnp.bfloat16), "dp", scatter_dimension=0, tiled=True
        ).astype(jnp.float32),
        lax.psum_scatter(
            grad_bias_one.astype(jnp.bfloat16), "dp", scatter_dimension=0, tiled=True
        ).astype(jnp.float32),
        lax.psum_scatter(
            grad_gain_two.astype(jnp.bfloat16), "dp", scatter_dimension=0, tiled=True
        ).astype(jnp.float32),
        lax.psum_scatter(
            grad_bias_two.astype(jnp.bfloat16), "dp", scatter_dimension=0, tiled=True
        ).astype(jnp.float32),
        lax.psum_scatter(
            grad_proj.astype(jnp.bfloat16), "dp", scatter_dimension=0, tiled=True
        ).astype(jnp.float32),
        lax.psum_scatter(
            grad_conv.astype(jnp.bfloat16), "dp", scatter_dimension=3, tiled=True
        ).astype(jnp.float32),
        lax.psum_scatter(
            grad_head_w.astype(jnp.bfloat16), "dp", scatter_dimension=0, tiled=True
        ).astype(jnp.float32),
        lax.psum_scatter(
            grad_head_b.astype(jnp.bfloat16), "dp", scatter_dimension=0, tiled=True
        ).astype(jnp.float32),
        lax.psum_scatter(
            grad_shift.astype(jnp.bfloat16), "dp", scatter_dimension=0, tiled=True
        ).astype(jnp.float32),
    )
    totals = (
        lax.psum(shards[0].astype(jnp.bfloat16), ("row", "col")).astype(jnp.float32),
        lax.psum(shards[1].astype(jnp.bfloat16), ("row", "col")).astype(jnp.float32),
        lax.psum(shards[2].astype(jnp.bfloat16), ("row", "col")).astype(jnp.float32),
        lax.psum(shards[3].astype(jnp.bfloat16), ("row", "col")).astype(jnp.float32),
        lax.psum(shards[4].astype(jnp.bfloat16), ("row", "col")).astype(jnp.float32),
        lax.psum(shards[5].astype(jnp.bfloat16), ("row", "col")).astype(jnp.float32),
        lax.psum(shards[6].astype(jnp.bfloat16), ("row", "col")).astype(jnp.float32),
        lax.psum(shards[7].astype(jnp.bfloat16), ("row", "col")).astype(jnp.float32),
        lax.psum(shards[8].astype(jnp.bfloat16), ("row", "col")).astype(jnp.float32),
        lax.psum(shards[9].astype(jnp.bfloat16), ("row", "col")).astype(jnp.float32),
        lax.psum(shards[10].astype(jnp.bfloat16), ("row", "col")).astype(jnp.float32),
        lax.psum(shards[11].astype(jnp.bfloat16), ("row", "col")).astype(jnp.float32),
        lax.psum(shards[12].astype(jnp.bfloat16), ("row", "col")).astype(jnp.float32),
        lax.psum(shards[13].astype(jnp.bfloat16), ("row", "col")).astype(jnp.float32),
        lax.psum(shards[14].astype(jnp.bfloat16), ("row", "col")).astype(jnp.float32),
    )
    return (
        tokens_out,
        merged_out,
        input_grad,
        totals[0],
        totals[1],
        totals[2],
        totals[3],
        totals[4],
        totals[5],
        totals[6],
        totals[7],
        totals[8],
        totals[9],
        totals[10],
        totals[11],
        totals[12],
        totals[13],
        totals[14],
    )


def solution(mesh):
    placed = (
        P("dp", "row", "col", None),
        P("dp", "row", "col", None),
        P("dp", "row", "col", None),
        P("dp"),
        P("dp"),
        P("dp"),
        P("dp", None),
        P("dp", None),
        P("dp", None),
        P("dp"),
        P("dp", None),
        P("dp"),
        P("dp"),
        P("dp"),
        P("dp"),
        P("dp"),
        P("dp", None),
        P(None, None, None, "dp", None),
        P("dp", None),
        P("dp"),
        P("dp"),
    )
    return jax.shard_map(
        on_device,
        mesh=mesh,
        in_specs=placed,
        out_specs=(
            P("dp", "row", "col", None),
            P("dp", "row", "col", None),
            P("dp", "row", "col", None),
            P("dp", None),
            P("dp", None),
            P("dp", None),
            P("dp"),
            P("dp", None),
            P("dp"),
            P("dp"),
            P("dp"),
            P("dp"),
            P("dp"),
            P("dp", None),
            P(None, None, None, "dp", None),
            P("dp", None),
            P("dp"),
            P("dp"),
        ),
        check_vma=False,
    )
```

profile of v0, /device:TPU:0, one launch (start us, length us, event | category | flops | bytes accessed | tf_op | source)
XLA Modules:
  0.0 1635.2 jit_solution(16031658393236253364)
XLA Ops:
  10.9 5.2 all-gather.1
  21.8 41.2 %all-gather.16.cloned.1.call-done = bf16[768,2304]{1,0:T(8,128)(2,1)} async-done(((bf16[384,2304]{1,0:T(8,128)(2,1)}), bf16[768,2304]{1,0:T(8,128)(2,1)}) %all-gather.16.cloned.1.call-update) | async-done | bytes 3538960 | tf_op jit(solution)/shard_map/all_gather | solution.py:164
  80.9 4.9 all_gather.74
  90.6 4.9 copy.85
  150.1 7.5 collective-permute-done.25
  159.0 5.6 collective-permute-start.26
  164.6 6.7 all_gather.72
  181.2 10.2 all-gather.20.cloned.1.call-done
  191.4 20.8 %copy.82 = bf16[10,1024,768]{1,2,0:T(8,128)(2,1)} copy(bf16[10,1024,768]{2,1,0:T(8,128)(2,1)} %all-gather.20.cloned.1.call-done) | data formatting | bytes 31457280 | tf_op jit(solution)/shard_map/all_gather | solution.py:217
  212.1 15.8 multiply_reduce_fusion.1
  227.9 13.7 fusion
  241.7 72.1 %all-gather.18.cloned.1.call-done = bf16[10,1024,768]{2,1,0:T(8,128)(2,1)} async-done(((bf16[10,64,768]{2,1,0:T(8,128)(2,1)}), bf16[10,1024,768]{2,1,0:T(8,128)(2,1)}) %all-gather.18.cloned.1.call-update) | async-done | bytes 15728656 | tf_op jit(solution)/shard_map/all_gather | solution.py:218
  313.7 20.7 %copy.81 = bf16[10,1024,768]{1,2,0:T(8,128)(2,1)} copy(bf16[10,1024,768]{2,1,0:T(8,128)(2,1)} %all-gather.18.cloned.1.call-done) | data formatting | bytes 31457280 | tf_op jit(solution)/shard_map/all_gather | solution.py:218
  334.4 19.7 %convert_bitcast_fusion.1 = bf16[10,64,12,64]{1,3,2,0:T(8,128)(2,1)S(1)} fusion(bf16[10,1024,12,64]{1,3,2,0:T(8,128)(2,1)} %bitcast.247, f32[10,12,64,1024]{3,2,1,0:T(8,128)} %get-tuple-element.129, f32[10,12,64]{2,1,0:T(8,128)S(1)} %fusion, f32[10,12,64]{2,1,0:T(8,128)S(1)} %get-tuple-element.128), kind=kOutput, calls=%fused_computation.81 | convolution fusion | flops 1038581760 | bytes 48230400 | tf_op jit(solution)/shard_map/nhqk,nkhd->nqhd/dot_general | solution.py:231
  364.6 36.1 %all-gather.24.cloned.1.call-done = bf16[768,3072]{1,0:T(8,128)(2,1)} async-done(((bf16[384,3072]{1,0:T(8,128)(2,1)}), bf16[768,3072]{1,0:T(8,128)(2,1)}) %all-gather.24.cloned.1.call-update) | async-done | bytes 4718608 | tf_op jit(solution)/shard_map/all_gather | solution.py:166
  400.8 8.3 fusion.116
  409.1 56.3 %all-gather.26.cloned.1.call-done = bf16[3072,768]{1,0:T(8,128)(2,1)} async-done(((bf16[1536,768]{1,0:T(8,128)(2,1)}), bf16[3072,768]{1,0:T(8,128)(2,1)}) %all-gather.26.cloned.1.call-update) | async-done | bytes 4718608 | tf_op jit(solution)/shard_map/all_gather | solution.py:168
  465.4 10.5 multiply_convert_fusion.6
  489.2 40.4 %all-gather.28.cloned.1.call-done = bf16[4,3,3,256,256]{3,4,2,1,0:T(8,128)(2,1)} async-done(((bf16[4,3,3,128,256]{3,4,2,1,0:T(8,128)(2,1)}), bf16[4,3,3,256,256]{3,4,2,1,0:T(8,128)(2,1)}) %all-gather.28.cloned.1.call-update) | async-done | bytes 4718608 | tf_op jit(solution)/shard_map/all_gather | solution.py:175
  529.6 5.9 slice_bitcast_fusion.3
  571.1 5.3 collective-permute-start.10
  598.9 5.2 collective-permute-start.30
  620.5 5.6 collective-permute-start.34
  641.4 5.2 collective-permute-start.38
  655.5 8.7 fusion.130
  677.8 18.3 %fusion.7 = bf16[10,12,64,1024]{3,2,1,0:T(8,128)(2,1)} fusion(bf16[10,64,12,64]{1,3,2,0:T(8,128)(2,1)S(1)} %copy.97, f32[10,12,64,1024]{3,2,1,0:T(8,128)} %get-tuple-element.129, f32[10,12,64]{2,1,0:T(8,128)S(1)} %log_add_fusion), kind=kOutput, calls=%fused_computation.16 | convolution fusion | flops 1038090240 | bytes 48199680 | tf_op jit(solution)/shard_map/nhqk,nqhd->knhd/dot_general | solution.py:376
  696.1 30.0 %multiply_reduce_fusion = (f32[10,12,64]{2,1,0:T(8,128)S(1)}, f32[10,12,64,1024]{3,2,1,0:T(8,128)}) fusion(f32[10,12,64,1024]{3,2,1,0:T(8,128)} %get-tuple-element.129, f32[10,12,64]{2,1,0:T(8,128)S(1)} %log_add_fusion, bf16[10,64,12,64]{1,3,2,0:T(8,128)(2,1)S(1)} %copy.97, bf16[10,1024,12,64]{1,3,2,0:T(8,128)(2,1)} %bitcast.248), kind=kOutput, calls=%fused_computation.3 | convolution fusion | flops 1038082560 | bytes 79687680 | tf_op jit(solution)/shard_map/nqhd,nkhd->nhqk/dot_general | solution.py:363
  726.1 19.2 %copy.99 = bf16[1024,10,768]{2,0,1:T(8,128)(2,1)} copy(bf16[1024,10,768]{0,2,1:T(8,128)(2,1)} %bitcast.249) | data formatting | bytes 31457280 | tf_op jit(solution)/shard_map/reshape | solution.py:383
  745.3 26.1 %multiply_convert_fusion.1 = bf16[10,12,64,1024]{3,2,1,0:T(8,128)(2,1)} fusion(f32[10,12,64,1024]{3,2,1,0:T(8,128)} %get-tuple-element.144, f32[10,12,64,1024]{3,2,1,0:T(8,128)} %get-tuple-element.129, f32[10,12,64]{2,1,0:T(8,128)S(1)} %get-tuple-element.143, f32[10,12,64]{2,1,0:T(8,128)S(1)} %log_add_fusion), kind=kLoop, calls=%fused_computation.2 | loop fusion | flops 39321600 | bytes 78704640 | tf_op jit(solution)/shard_map/convert_element_type | solution.py:367
  771.4 10.9 multiply_convert_fusion
  782.4 20.7 %copy.98 = bf16[1024,10,768]{2,0,1:T(8,128)(2,1)} copy(bf16[1024,10,768]{0,2,1:T(8,128)(2,1)} %bitcast.252) | data formatting | bytes 31457280 | tf_op jit(solution)/shard_map/reshape | solution.py:382
  803.0 21.2 %pad_maximum_fusion = bf16[1024,10,1536]{2,0,1:T(8,128)(2,1)} fusion(bf16[1024,10,768]{2,0,1:T(8,128)(2,1)} %copy.99, bf16[1024,10,768]{2,0,1:T(8,128)(2,1)} %copy.98), kind=kLoop, calls=%fused_computation | loop fusion | flops 62914560 | bytes 62914560 | tf_op jit(solution)/shard_map/concatenate | solution.py:380
  833.9 5.0 collective-permute-start.14
  892.3 11.3 convolution_convert_fusion
  904.3 9.1 convolution_convert_fusion.1
  913.5 14.0 fusion.23
  935.5 186.8 %reduce-scatter.9.cloned.1.call-done = bf16[64,10,1536]{2,0,1:T(8,128)(2,1)} async-done(((bf16[1024,10,1536]{2,0,1:T(8,128)(2,1)}), bf16[64,10,1536]{2,0,1:T(8,128)(2,1)}) %reduce-scatter.9.cloned.1.call-update) | async-done | bytes 1966096 | tf_op jit(solution)/shard_map/reduce_scatter | solution.py:379
  1122.4 5.9 convolution_convert_fusion.2
  1128.4 5.6 reduce-scatter.23.cloned.1.call-done
  1134.0 15.8 reduce-scatter.19.cloned.1.call-done
  1149.8 24.7 %reduce-scatter.13.cloned.1.call-done = bf16[384,768]{1,0:T(8,128)(2,1)} async-done(((bf16[768,768]{1,0:T(8,128)(2,1)}), bf16[384,768]{1,0:T(8,128)(2,1)}) %reduce-scatter.13.cloned.1.call-update) | async-done | bytes 589840 | tf_op jit(solution)/shard_map/reduce_scatter | solution.py:403
  1174.5 62.7 %reduce-scatter.21.cloned.1.call-done = bf16[4,3,3,128,256]{4,3,2,1,0:T(8,128)(2,1)} async-done(((bf16[4,3,3,256,256]{4,3,2,1,0:T(8,128)(2,1)}), bf16[4,3,3,128,256]{4,3,2,1,0:T(8,128)(2,1)}) %reduce-scatter.21.cloned.1.call-update) | async-done | bytes 2359312 | tf_op jit(solution)/shard_map/reduce_scatter | solution.py:433
  1237.3 63.0 %reduce-scatter.17.cloned.1.call-done = bf16[1536,768]{1,0:T(8,128)(2,1)} async-done(((bf16[3072,768]{1,0:T(8,128)(2,1)}), bf16[1536,768]{1,0:T(8,128)(2,1)}) %reduce-scatter.17.cloned.1.call-update) | async-done | bytes 2359312 | tf_op jit(solution)/shard_map/reduce_scatter | solution.py:412
  1300.3 62.8 %reduce-scatter.15.cloned.1.call-done = bf16[384,3072]{1,0:T(8,128)(2,1)} async-done(((bf16[768,3072]{1,0:T(8,128)(2,1)}), bf16[384,3072]{1,0:T(8,128)(2,1)}) %reduce-scatter.15.cloned.1.call-update) | async-done | bytes 2359312 | tf_op jit(solution)/shard_map/reduce_scatter | solution.py:406
  1363.1 50.5 %reduce-scatter.11.cloned.1.call-done = bf16[384,2304]{1,0:T(8,128)(2,1)} async-done(((bf16[768,2304]{1,0:T(8,128)(2,1)}), bf16[384,2304]{1,0:T(8,128)(2,1)}) %reduce-scatter.11.cloned.1.call-update) | async-done | bytes 1769488 | tf_op jit(solution)/shard_map/reduce_scatter | solution.py:400
  1434.9 7.1 all-reduce.10
  1442.7 63.2 %all-reduce.8 = (bf16[1536]{0:T(1024)(128)(2,1)S(1)}, bf16[384]{0:T(512)(128)(2,1)S(1)}, bf16[384]{0:T(512)(128)(2,1)S(1)}, bf16[384]{0:T(512)(128)(2,1)S(1)}, b...) all-reduce(bf16[1536]{0:T(1024)(128)(2,1)S(1)} %dynamic-slice.1, ...), channel_id=1, replica_groups=mesh['dp'=2,'row'=4,'col'=4] {'row','col'}, use_global_device_ids=true, to_apply=%region_20.21 | all-reduce | flops 3712 | bytes 14848 | tf_op jit(solution)/shard_map/psum | solution.py:450
  1513.8 97.9 %all-reduce.13.cloned.1.call-done = (bf16[384,2304]{1,0:T(8,128)(2,1)}, bf16[384,768]{1,0:T(8,128)(2,1)}, bf16[384,3072]{1,0:T(8,128)(2,1)}, bf16[1536,768]{1,0:...) async-done(((bf16[384,2304]{1,0:T(8,128)(2,1)}, bf16[384,768]{1,0:T(8,128)(2,1)}, ...) | async-done | bytes 9699344 | tf_op jit(solution)/shard_map/psum | solution.py:447
  (603 shorter events, 347.1 us)
Async XLA Ops:
  7.2 55.7 %all-gather.16.cloned.1.call-start = ((), (), s32[]{:S(2)}) async-start(), calls=%async_computation.8 | async-start | bytes 5308416 | tf_op jit(solution)/shard_map/all_gather | solution.py:164
  10.8 180.6 %all-gather.20.cloned.1.call-start = ((), (), s32[]{:S(2)}) async-start(), calls=%async_computation.10 | async-start | bytes 16711680 | tf_op jit(solution)/shard_map/all_gather | solution.py:217
  69.1 244.6 %all-gather.18.cloned.1.call-start = ((), (), s32[]{:S(2)}) async-start(), calls=%async_computation.9 | async-start | bytes 16711680 | tf_op jit(solution)/shard_map/all_gather | solution.py:218
  69.9 291.8 %all-gather.22.cloned.1.call-start = ((), (), s32[]{:S(2)}) async-start(), calls=%async_computation.11 | async-start | bytes 1769472 | tf_op jit(solution)/shard_map/all_gather | solution.py:165
  70.8 329.9 %all-gather.24.cloned.1.call-start = ((), (), s32[]{:S(2)}) async-start(), calls=%async_computation.12 | async-start | bytes 7077888 | tf_op jit(solution)/shard_map/all_gather | solution.py:166
  75.0 390.4 %all-gather.26.cloned.1.call-start = ((), (), s32[]{:S(2)}) async-start(), calls=%async_computation.13 | async-start | bytes 7077888 | tf_op jit(solution)/shard_map/all_gather | solution.py:168
  79.6 450.0 %all-gather.28.cloned.1.call-start = ((), (), s32[]{:S(2)}) async-start(), calls=%async_computation.14 | async-start | bytes 7077888 | tf_op jit(solution)/shard_map/all_gather | solution.py:175
  87.8 20.9 %collective-permute-start.20 = (bf16[10,1,16,256]{3,2,1,0:T(8,128)(2,1)S(1)}, bf16[10,1,16,256]{3,2,1,0:T(8,128)(2,1)S(1)}, u32[]{:S(2)}, u32[]{:S(2)}) collective-permute-start(bf16[10,1,16,256]{3,2,1,0:T(8,128)(2,1)S(1)} %get-tuple-element.70), channel_id=1, source_target_pairs={{0,4},{4,8},{8,12},{1,5},{5,9},{9,13},{2,6},{6,10},{10,14},{3,7},{... | collective-permute-start | bytes 245768 | tf_op jit(solution)/shard_map/ppermute | solution.py:20
  89.2 19.6 %collective-permute-start.21 = (bf16[10,1,16,256]{3,2,1,0:T(8,128)(2,1)S(1)}, bf16[10,1,16,256]{3,2,1,0:T(8,128)(2,1)S(1)}, u32[]{:S(2)}, u32[]{:S(2)}) collective-permute-start(bf16[10,1,16,256]{3,2,1,0:T(8,128)(2,1)S(1)} %get-tuple-element.71), channel_id=1, source_target_pairs={{4,0},{8,4},{12,8},{5,1},{9,5},{13,9},{6,2},{10,6},{14,10},{7,3},{... | collective-permute-start | bytes 245768 | tf_op jit(solution)/shard_map/ppermute | solution.py:21
  95.6 1026.8 %reduce-scatter.9.cloned.1.call-start = ((), (), s32[]{:S(2)}) async-start(), calls=%async_computation.15 | async-start | bytes 33423360 | tf_op jit(solution)/shard_map/reduce_scatter | solution.py:379
  109.0 7.3 collective-permute-start.22
  112.3 8.2 collective-permute-start.23
  141.7 8.3 collective-permute-start.24
  143.0 14.5 collective-permute-start.25
  157.7 13.5 collective-permute-start.27
  159.0 12.2 collective-permute-start.26
  478.9 4.4 collective-permute-start.1
  483.4 54.5 %collective-permute-start.3 = (bf16[10,10,1,256]{3,2,1,0:T(2,128)(2,1)S(1)}, bf16[10,10,1,256]{3,2,1,0:T(2,128)(2,1)S(1)}, u32[]{:S(2)}, u32[]{:S(2)}) collective-permute-start(bf16[10,10,1,256]{3,2,1,0:T(2,128)(2,1)S(1)} %get-tuple-element.106), channel_id=1, source_target_pairs={{1,0},{2,1},{3,2},{5,4},{6,5},{7,6},{9,8},{10,9},{11,10},{13,12},{... | collective-permute-start | bytes 153608 | tf_op jit(solution)/shard_map/ppermute | solution.py:21
  484.7 53.2 %collective-permute-start.2 = (bf16[10,10,1,256]{3,2,1,0:T(2,128)(2,1)S(1)}, bf16[10,10,1,256]{3,2,1,0:T(2,128)(2,1)S(1)}, u32[]{:S(2)}, u32[]{:S(2)}) collective-permute-start(bf16[10,10,1,256]{3,2,1,0:T(2,128)(2,1)S(1)} %get-tuple-element.107), channel_id=1, source_target_pairs={{0,1},{1,2},{2,3},{4,5},{5,6},{6,7},{8,9},{9,10},{10,11},{12,13},{... | collective-permute-start | bytes 153608 | tf_op jit(solution)/shard_map/ppermute | solution.py:20
  541.6 5.0 collective-permute-start.4
  547.8 10.0 collective-permute-start.7
  549.1 8.7 collective-permute-start.6
  561.5 6.1 collective-permute-start.8
  569.8 12.5 collective-permute-start.11
  571.1 11.2 collective-permute-start.10
  589.6 5.4 collective-permute-start.28
  597.6 7.6 collective-permute-start.31
  598.9 7.1 collective-permute-start.30
  611.2 4.8 collective-permute-start.32
  619.2 8.0 collective-permute-start.35
  620.5 7.5 collective-permute-start.34
  632.8 5.1 collective-permute-start.36
  640.1 7.4 collective-permute-start.39
  641.4 7.2 collective-permute-start.38
  824.3 309.7 %reduce-scatter.23.cloned.1.call-start = ((), (), s32[]{:S(2)}) async-start(), calls=%async_computation.22 | async-start | bytes 196608 | tf_op jit(solution)/shard_map/reduce_scatter | solution.py:436
  825.3 5.1 collective-permute-start.12
  832.6 7.0 collective-permute-start.15
  833.9 7.2 collective-permute-start.14
  843.8 7.7 collective-permute-start.16
  851.7 7.9 collective-permute-start.18
  855.8 6.7 collective-permute-start.19
  877.4 272.5 %reduce-scatter.19.cloned.1.call-start = ((), (), s32[]{:S(2)}) async-start(), calls=%async_computation.20 | async-start | bytes 589824 | tf_op jit(solution)/shard_map/reduce_scatter | solution.py:430
  878.7 295.8 %reduce-scatter.13.cloned.1.call-start = ((), (), s32[]{:S(2)}) async-start(), calls=%async_computation.17 | async-start | bytes 1769472 | tf_op jit(solution)/shard_map/reduce_scatter | solution.py:403
  885.6 351.6 %reduce-scatter.21.cloned.1.call-start = ((), (), s32[]{:S(2)}) async-start(), calls=%async_computation.21 | async-start | bytes 7077888 | tf_op jit(solution)/shard_map/reduce_scatter | solution.py:433
  891.6 408.7 %reduce-scatter.17.cloned.1.call-start = ((), (), s32[]{:S(2)}) async-start(), calls=%async_computation.19 | async-start | bytes 7077888 | tf_op jit(solution)/shard_map/reduce_scatter | solution.py:412
  903.6 459.5 %reduce-scatter.15.cloned.1.call-start = ((), (), s32[]{:S(2)}) async-start(), calls=%async_computation.18 | async-start | bytes 7077888 | tf_op jit(solution)/shard_map/reduce_scatter | solution.py:406
  913.4 500.1 %reduce-scatter.11.cloned.1.call-start = ((), (), s32[]{:S(2)}) async-start(), calls=%async_computation.16 | async-start | bytes 5308416 | tf_op jit(solution)/shard_map/reduce_scatter | solution.py:400
  1128.4 483.4 %all-reduce.13.cloned.1.call-start = ((), (), s32[]{:S(2)}) async-start(), calls=%async_computation.23 | async-start | bytes 19398656 | tf_op jit(solution)/shard_map/psum | solution.py:447
  (122 other events, 3661.3 us)
Sparse Core Ops, SparseCore 0:
  10.9 52.0 all-gather.15
  69.3 122.0 all-gather.19
  194.3 119.3 all-gather.17
  315.1 20.9 all-gather.21
  338.1 62.6 all-gather.23
  402.7 62.6 all-gather.25
  467.0 62.6 all-gather.27
  824.5 297.8 reduce-scatter.8
  1124.6 9.3 reduce-scatter.22
  1136.7 13.1 reduce-scatter.18
  1152.7 21.7 reduce-scatter.12
  1177.3 59.9 reduce-scatter.20
  1240.3 59.9 reduce-scatter.16
  1303.0 59.9 reduce-scatter.14
  1365.8 47.6 reduce-scatter.10
  1418.0 193.6 all-reduce.12
where the time goes:
time: 1650 us; the launch traced here: 1640 us
  waiting for transfers between devices  862 us (52%)
  matrix products  215 us (13%)
  local copies, waits for them, and re-layouts  185 us (11%)
  other arithmetic  131 us (8%)
  blocking collectives  118 us (7%)
  starting transfers between devices  105 us (6%)
  between operations  19.7 us (1%)
    reduce_scatter x1, waiting for transfers between devices, on_device(): lax.psum_scatter(jnp.concatenate([key_part.reshape(lax.axis_size(('row',...  187 us
    psum x1, waiting for transfers between devices, on_device(): lax.psum(shards[0].astype(jnp.bfloat16), ('row', 'col')).astype(jnp.float32)  97.9 us
    ppermute x20, starting transfers between devices, extended(): before = lax.ppermute(last, axis, up)  77.2 us
    all_gather x1, waiting for transfers between devices, on_device(): lax.all_gather(values_own, ('row', 'col'), axis=1, tiled=True)  72.1 us
    psum x1, blocking collectives, on_device(): lax.psum(shards[3].astype(jnp.bfloat16), ('row', 'col')).astype(jnp.float32)  63.2 us
    reduce_scatter x1, waiting for transfers between devices, on_device(): lax.psum_scatter(grad_down_w.astype(jnp.bfloat16), 'dp', scatter_dimensio...  63 us
    reduce_scatter x1, waiting for transfers between devices, on_device(): lax.psum_scatter(grad_up_w.astype(jnp.bfloat16), 'dp', scatter_dimension=...  62.8 us
    reduce_scatter x1, waiting for transfers between devices, on_device(): lax.psum_scatter(grad_conv.astype(jnp.bfloat16), 'dp', scatter_dimension=...  62.7 us
  transfers between devices with their start and end apart: 56, of which 30 were waited for; matrix products, arithmetic and copies ran while one was open for 18% of the time, Pallas kernels for 0%

commit v1 on v0

--- a/solution.py
+++ b/solution.py
@@ -1,6 +1,10 @@
+import functools
+
 import jax
 import jax.numpy as jnp
 from jax import lax
+from jax.experimental import pallas as pl
+from jax.experimental.pallas import tpu as pltpu
 from jax.sharding import PartitionSpec as P
 
 HEADS = 12
@@ -482,7 +486,1038 @@
     )
 
 
+LOG2E = 1.4426950408889634
+MESH = pl.DeviceIdType.MESH
+HALO = 6
+PATCH = 112
+VMEM_LIMIT = 58 << 20
+
+
+def place():
+    dp, row, col = (lax.axis_index(axis) for axis in ("dp", "row", "col"))
+    return dp, lax.div(row, 2), lax.rem(row, 2), col
+
+
+def flip(bit):
+    return 1 - bit
+
+
+def send(src, dst, send_sem, recv_sem, dp, y, core, z):
+    return pltpu.make_async_remote_copy(
+        src_ref=src,
+        dst_ref=dst,
+        send_sem=send_sem,
+        recv_sem=recv_sem,
+        device_id={"dp": dp, "row": y * 2 + core, "col": z},
+        device_id_type=MESH,
+    )
+
+
+def landed(ref, sem):
+    return pltpu.make_async_copy(ref, ref, sem)
+
+
+def to_images_start(src, dst, send_sem, recv_sem, sizes):
+    chips, slots, cols = sizes
+    dp, y, core, z = place()
+    own = core * cols + z
+    for step in range(chips):
+        far_y = lax.rem(y + step // cols, 2)
+        far_z = lax.rem(z + step % cols, cols)
+        slot = far_y * cols + far_z
+        copy = send(
+            src.at[slot], dst.at[0, own], send_sem.at[step], recv_sem.at[own], dp, far_y, y, far_z
+        )
+        if step == 0:
+            local = pltpu.make_async_copy(src.at[slot], dst.at[0, own], recv_sem.at[own])
+            pl.when(core == y)(local.start)
+            pl.when(core != y)(copy.start)
+        else:
+            copy.start()
+    for extra in range(slots - chips):
+        chip = 2 * chips - slots + extra
+        send(
+            src.at[chips + extra],
+            dst.at[1, own],
+            send_sem.at[chips + extra],
+            recv_sem.at[chips + own],
+            1 - dp,
+            chip // cols,
+            y,
+            chip % cols,
+        ).start()
+
+
+def to_images_wait(src, dst, send_sem, recv_sem, sizes):
+    chips, slots, cols = sizes
+    dp, y, core, z = place()
+    for step in range(slots):
+        left = landed(src.at[0], send_sem.at[step])
+        if step == 0:
+            pl.when(core != y)(left.wait)
+        else:
+            left.wait()
+    for tile in range(chips):
+        landed(dst.at[0, tile], recv_sem.at[tile]).wait()
+
+    @pl.when(y * cols + z >= 2 * chips - slots)
+    def _():
+        for tile in range(chips):
+            landed(dst.at[1, tile], recv_sem.at[chips + tile]).wait()
+
+
+def to_tiles_start(src, dst, send_sem, recv_sem, sizes):
+    chips, slots, cols = sizes
+    dp, y, core, z = place()
+    slot = y * cols + z
+    for step in range(chips):
+        far_core = lax.rem(core + step // cols, 2)
+        far_z = lax.rem(z + step % cols, cols)
+        tile = far_core * cols + far_z
+        copy = send(
+            src.at[tile], dst.at[slot], send_sem.at[step], recv_sem.at[slot], dp, core, far_core, far_z
+        )
+        if step == 0:
+            local = pltpu.make_async_copy(src.at[tile], dst.at[slot], recv_sem.at[slot])
+            pl.when(core == y)(local.start)
+            pl.when(core != y)(copy.start)
+        else:
+            copy.start()
+
+    @pl.when(slot >= 2 * chips - slots)
+    def _():
+        for step in range(chips):
+            far_core = step // cols
+            far_z = step % cols
+            other = slot + slots - chips
+            send(
+                src.at[step],
+                dst.at[other],
+                send_sem.at[chips + step],
+                recv_sem.at[other],
+                1 - dp,
+                core,
+                far_core,
+                far_z,
+            ).start()
+
+
+def to_tiles_wait(src, dst, send_sem, recv_sem, sizes):
+    chips, slots, cols = sizes
+    dp, y, core, z = place()
+    for step in range(chips):
+        left = landed(src.at[0], send_sem.at[step])
+        if step == 0:
+            pl.when(core != y)(left.wait)
+        else:
+            left.wait()
+
+    @pl.when(y * cols + z >= 2 * chips - slots)
+    def _():
+        for step in range(chips):
+            landed(src.at[0], send_sem.at[chips + step]).wait()
+
+    for slot in range(slots):
+        landed(dst.at[slot], recv_sem.at[slot]).wait()
+
+
+BITS = ("dp", "y", "z1", "z2")
+
+
+def mate(bit):
+    dp, y, core, z = place()
+    low, high = lax.rem(z, 2), lax.div(z, 2)
+    if bit == "core":
+        return dp, y, 1 - core, z
+    if bit == "dp":
+        return 1 - dp, y, core, z
+    if bit == "y":
+        return dp, 1 - y, core, z
+    if bit == "z1":
+        return dp, y, core, high * 2 + 1 - low
+    return dp, y, core, (1 - high) * 2 + low
+
+
+def bit_of(bit):
+    dp, y, core, z = place()
+    return {
+        "dp": dp,
+        "y": y,
+        "core": core,
+        "z1": lax.rem(z, 2),
+        "z2": lax.div(z, 2),
+    }[bit]
+
+
+PIECE_BITS = ("y", "z1", "core")
+GATHER_ORDERS = (("dp", "z1", "y", "core"), ("dp", "y", "z1", "core"))
+
+
+def gather_steps(half, whole, local_sem, send_sem, recv_sem, order):
+    held = {bit: bit_of(bit) for bit in PIECE_BITS}
+    dp = bit_of("dp")
+    copies = []
+
+    def start(step):
+        bit = order[step]
+        at = tuple(held[b] if held[b] is not None else slice(None) for b in PIECE_BITS)
+        if bit == "dp":
+            src = half.at[(slice(None),) + at]
+            far = whole.at[(slice(None), dp) + at]
+            for piece in range(8):
+                of = (slice(None), piece // 4, piece // 2 % 2, piece % 2)
+                local = pltpu.make_async_copy(
+                    half.at[of], whole.at[of[:1] + (dp,) + of[1:]], local_sem.at[piece]
+                )
+                local.start()
+                copies.append(local)
+        else:
+            src = whole.at[(slice(None), 1 - dp) + at]
+            far = src
+        copy = send(src, far, send_sem.at[step], recv_sem.at[step], *mate(bit))
+        copy.start()
+        copies.append(copy)
+
+    def wait(step):
+        while copies:
+            copies.pop().wait()
+        if order[step] != "dp":
+            held[order[step]] = None
+
+    return len(order), start, wait
+
+
+def pipeline(jobs):
+    for slot in range(max(delay + steps for delay, steps, _, _ in jobs) + 1):
+        for delay, steps, start, wait in jobs:
+            step = slot - delay
+            if 0 < step <= steps:
+                wait(step - 1)
+            if 0 <= step < steps:
+                start(step)
+
+
+def in_kernel(sizes, names, *refs):
+    n = len(names)
+    tiles, refs = refs[:3], refs[3:]
+    halves, refs = refs[:n], refs[n:]
+    images, refs = refs[:3], refs[3:]
+    wholes, refs = refs[:n], refs[n:]
+    tile_send, tile_recv, local_sem, send_sem, recv_sem = refs
+    for i in range(3):
+        to_images_start(tiles[i], images[i], tile_send.at[i], tile_recv.at[i], sizes)
+    jobs = []
+    for i in range(n):
+        steps, start, wait = gather_steps(
+            halves[i],
+            wholes[i],
+            local_sem.at[i],
+            send_sem.at[i],
+            recv_sem.at[i],
+            GATHER_ORDERS[i % 2],
+        )
+        jobs.append((i // 2, steps, start, wait))
+    pipeline(jobs)
+    for i in range(3):
+        to_images_wait(tiles[i], images[i], tile_send.at[i], tile_recv.at[i], sizes)
+
+
+def bring_in(tiles, halves, sizes):
+    chips, slots, cols = sizes
+    names = list(halves)
+    cut = {}
+    for name, half in halves.items():
+        lead, rows, width = half.shape
+        cut[name] = half.reshape(lead, 2, 2, 2, rows // 8, width)
+    out_shape = [
+        jax.ShapeDtypeStruct((2, chips) + tile.shape[1:], tile.dtype) for tile in tiles
+    ] + [
+        jax.ShapeDtypeStruct((cut[name].shape[0], 2) + cut[name].shape[1:], jnp.bfloat16)
+        for name in names
+    ]
+    n = len(names)
+    outs = pl.pallas_call(
+        functools.partial(in_kernel, sizes, names),
+        out_shape=out_shape,
+        in_specs=[pl.BlockSpec(memory_space=pltpu.HBM)] * (3 + n),
+        out_specs=[pl.BlockSpec(memory_space=pltpu.HBM)] * (3 + n),
+        scratch_shapes=[
+            pltpu.SemaphoreType.DMA((3, slots)),
+            pltpu.SemaphoreType.DMA((3, 2 * chips)),
+            pltpu.SemaphoreType.DMA((n, 8)),
+            pltpu.SemaphoreType.DMA((n, 4)),
+            pltpu.SemaphoreType.DMA((n, 4)),
+        ],
+        compiler_params=pltpu.CompilerParams(
+            has_side_effects=True, vmem_limit_bytes=VMEM_LIMIT
+        ),
+    )(*tiles, *(cut[name] for name in names))
+    wholes = {}
+    for name, whole in zip(names, outs[3:]):
+        lead, rows, width = halves[name].shape
+        wholes[name] = whole.reshape(lead, 2 * rows, width)
+    return outs[:3], wholes
+
+
+def patch_kernel(sizes, src, dst, send_sem, recv_sem):
+    to_tiles_start(src, dst, send_sem, recv_sem, sizes)
+    to_tiles_wait(src, dst, send_sem, recv_sem, sizes)
+
+
+def patches_out(patch, sizes):
+    chips, slots, cols = sizes
+    return pl.pallas_call(
+        functools.partial(patch_kernel, sizes),
+        out_shape=jax.ShapeDtypeStruct((slots,) + patch.shape[1:], patch.dtype),
+        in_specs=[pl.BlockSpec(memory_space=pltpu.HBM)],
+        out_specs=pl.BlockSpec(memory_space=pltpu.HBM),
+        scratch_shapes=[
+            pltpu.SemaphoreType.DMA((2 * chips,)),
+            pltpu.SemaphoreType.DMA((slots,)),
+        ],
+        compiler_params=pltpu.CompilerParams(
+            has_side_effects=True, vmem_limit_bytes=VMEM_LIMIT
+        ),
+    )(patch)
+
+
+SUM_ORDERS = (
+    ("dp", "y", "z1", "z2"),
+    ("y", "dp", "z1", "z2"),
+    ("z1", "dp", "y", "z2"),
+)
+BACK_ORDERS = (
+    ("z2", "z1", "y", "core"),
+    ("z2", "y", "z1", "core"),
+    ("z2", "y", "z1", "core"),
+)
+
+
+def reduce_steps(grad, out, acc, recvs, sems, orders):
+    local_sem, send_sem, recv_sem = sems
+    sum_order, back_order = orders
+    half = grad.shape[-1] // 2
+    core = bit_of("core")
+    mine = pl.ds(pl.multiple_of(core * half, 128), half)
+    theirs = pl.ds(pl.multiple_of((1 - core) * half, 128), half)
+    kept = {bit: None for bit in BITS}
+    whole = slice(None)
+    copies = []
+    forward = 1 + len(sum_order)
+
+    def index():
+        return tuple(whole if kept[b] is None else kept[b] for b in BITS)
+
+    def add(recv):
+        free = [b for b in BITS if kept[b] is None]
+
+        def body(i, _):
+            bits, left = {}, i
+            for b in reversed(free):
+                bits[b] = lax.rem(left, 2)
+                left = lax.div(left, 2)
+            at = tuple(bits[b] if b in bits else kept[b] for b in BITS)
+            here = (whole,) + at
+            there = (whole,) + tuple(bits[b] for b in free)
+            total = acc[here].astype(jnp.float32) + recv[there].astype(jnp.float32)
+            acc[here] = total.astype(acc.dtype)
+            return 0
+
+        lax.fori_loop(0, 2 ** len(free), body, 0)
+
+    def start(step):
+        if step == 0:
+            local = pltpu.make_async_copy(grad.at[..., mine], acc, local_sem.at[0])
+            local.start()
+            copies.append(local)
+            copy = send(
+                grad.at[..., theirs], recvs[0], send_sem.at[0], recv_sem.at[0], *mate("core")
+            )
+        elif step < forward:
+            bit = sum_order[step - 1]
+            kept[bit] = 1 - bit_of(bit)
+            src = acc.at[(whole,) + index()]
+            kept[bit] = bit_of(bit)
+            copy = send(src, recvs[step], send_sem.at[step], recv_sem.at[step], *mate(bit))
+        elif step == forward:
+            at = (whole,) + index()[1:] + (whole, mine)
+            copy = pltpu.make_async_copy(acc.at[(whole,) + index()], out.at[at], local_sem.at[1])
+            kept.pop("dp")
+            kept["core"] = mine
+        else:
+            bit = back_order[step - forward - 1]
+            at = (whole,) + tuple(whole if kept[b] is None else kept[b] for b in BITS[1:])
+            at = at + (whole, mine)
+            copy = send(
+                out.at[at], out.at[at], send_sem.at[step - 1], recv_sem.at[step - 1], *mate(bit)
+            )
+        copy.start()
+        copies.append(copy)
+
+    def wait(step):
+        while copies:
+            copies.pop().wait()
+        if step < forward:
+            add(recvs[step])
+        elif step > forward:
+            kept[back_order[step - forward - 1]] = None
+
+    return forward + 1 + len(back_order), start, wait
+
+
+def recv_shapes(shape, order):
+    lead, rows, width = shape[0], shape[5], shape[6]
+    free, out = 4, []
+    for step in range(1 + len(order)):
+        out.append((lead,) + (2,) * (4 - step) + (rows, width // 2))
+    return out
+
+
+def out_kernel(sizes, n, delays, *refs):
+    tiles, refs = refs[:2], refs[2:]
+    grads, refs = refs[:n], refs[n:]
+    slots, refs = refs[:2], refs[2:]
+    outs, refs = refs[:n], refs[n:]
+    accs, refs = refs[:n], refs[n:]
+    recvs, refs = refs[: 5 * n], refs[5 * n :]
+    tile_send, tile_recv, local_sem, send_sem, recv_sem = refs
+    for i in range(2):
+        to_tiles_start(tiles[i], slots[i], tile_send.at[i], tile_recv.at[i], sizes)
+    jobs = []
+    for i in range(n):
+        steps, start, wait = reduce_steps(
+            grads[i],
+            outs[i],
+            accs[i],
+            recvs[5 * i : 5 * i + 5],
+            (local_sem.at[i], send_sem.at[i], recv_sem.at[i]),
+            (SUM_ORDERS[i % 3], BACK_ORDERS[i % 3]),
+        )
+        jobs.append((delays[i], steps, start, wait))
+    pipeline(jobs)
+    for i in range(2):
+        to_tiles_wait(tiles[i], slots[i], tile_send.at[i], tile_recv.at[i], sizes)
+
+
+def bring_out(tiles, grads, sizes):
+    chips, slots, cols = sizes
+    names = list(grads)
+    n = len(names)
+    cut = []
+    for name in names:
+        lead, rows, width = grads[name].shape
+        cut.append(grads[name].reshape(lead, 2, 2, 2, 2, rows // 16, width))
+    accs = [pltpu.VMEM(g.shape[:-1] + (g.shape[-1] // 2,), jnp.bfloat16) for g in cut]
+    recvs = [
+        pltpu.VMEM(shape, jnp.bfloat16)
+        for i, g in enumerate(cut)
+        for shape in recv_shapes(g.shape, SUM_ORDERS[i % 3])
+    ]
+    outs = pl.pallas_call(
+        functools.partial(out_kernel, sizes, n, [i // 2 for i in range(n)]),
+        out_shape=[
+            jax.ShapeDtypeStruct((slots,) + tile.shape[1:], tile.dtype) for tile in tiles
+        ]
+        + [jax.ShapeDtypeStruct(g.shape[:1] + g.shape[2:], jnp.bfloat16) for g in cut],
+        in_specs=[pl.BlockSpec(memory_space=pltpu.HBM)] * (2 + n),
+        out_specs=[pl.BlockSpec(memory_space=pltpu.HBM)] * (2 + n),
+        scratch_shapes=accs
+        + recvs
+        + [
+            pltpu.SemaphoreType.DMA((2, 2 * chips)),
+            pltpu.SemaphoreType.DMA((2, slots)),
+            pltpu.SemaphoreType.DMA((n, 2)),
+            pltpu.SemaphoreType.DMA((n, 9)),
+            pltpu.SemaphoreType.DMA((n, 9)),
+        ],
+        compiler_params=pltpu.CompilerParams(
+            has_side_effects=True, vmem_limit_bytes=VMEM_LIMIT
+        ),
+    )(*tiles, *cut)
+    sums = {}
+    for name, out in zip(names, outs[2:]):
+        lead, rows, width = grads[name].shape
+        sums[name] = out.reshape(lead, rows // 2, width)
+    return outs[:2], sums
+
+
+SCALE = HEAD_DIM**-0.5
+
+
+def attend_kernel(q_ref, k_ref, v_ref, o_ref, log_ref):
+    lane = lax.broadcasted_iota(jnp.int32, (1, 128), 1)
+    sub = lax.broadcasted_iota(jnp.int32, (128, 1), 0)
+    k, v, q = k_ref[...], v_ref[...], q_ref[...]
+    out = jnp.zeros((128, q.shape[0]), jnp.float32)
+    for h in range(2):
+        mine = (lane >= 64) == (h == 1)
+        scores = lax.dot_general(
+            k, jnp.where(mine, q, 0), (((1,), (1,)), ((), ())), preferred_element_type=jnp.float32
+        )
+        top = jnp.max(scores, 0, keepdims=True) * (SCALE * LOG2E)
+        e = jnp.exp2(scores * (SCALE * LOG2E) - top)
+        total = jnp.sum(e, 0, keepdims=True)
+        part = lax.dot_general(
+            v, e.astype(jnp.bfloat16), (((0,), (0,)), ((), ())), preferred_element_type=jnp.float32
+        )
+        out = jnp.where((sub >= 64) == (h == 1), part / total, out)
+        log_ref[0, h : h + 1, :] = top + jnp.log2(total)
+    o_ref[...] = out.T
+
+
+def attend_back_kernel(q_ref, k_ref, v_ref, o_ref, log_ref, g_ref, dq_ref, dk_ref, dv_ref):
+    lane = lax.broadcasted_iota(jnp.int32, (1, 128), 1)
+    sub = lax.broadcasted_iota(jnp.int32, (128, 1), 0)
+    k, v, q, g = k_ref[...], v_ref[...], q_ref[...], g_ref[...]
+    product = (g.astype(jnp.float32) * o_ref[...]).T
+    dq = jnp.zeros((128, q.shape[0]), jnp.float32)
+    for h in range(2):
+        mine = (lane >= 64) == (h == 1)
+        q_own, g_own = jnp.where(mine, q, 0), jnp.where(mine, g, 0)
+        centre = jnp.sum(product[h * 64 : (h + 1) * 64], 0, keepdims=True)
+        scores = lax.dot_general(
+            k, q_own, (((1,), (1,)), ((), ())), preferred_element_type=jnp.float32
+        )
+        p = jnp.exp2(scores * (SCALE * LOG2E) - log_ref[0, h : h + 1, :])
+        dp = lax.dot_general(
+            v, g_own, (((1,), (1,)), ((), ())), preferred_element_type=jnp.float32
+        )
+        ds = (p * (dp - centre)).astype(jnp.bfloat16)
+        dq_own = lax.dot_general(
+            k, ds, (((0,), (0,)), ((), ())), preferred_element_type=jnp.float32
+        )
+        dq = jnp.where((sub >= 64) == (h == 1), dq_own * SCALE, dq)
+        dk = jnp.dot(ds, q_own, preferred_element_type=jnp.float32) * SCALE
+        dv = jnp.dot(p.astype(jnp.bfloat16), g_own, preferred_element_type=jnp.float32)
+        if h == 0:
+            dk_ref[...], dv_ref[...] = dk, dv
+        else:
+            dk_ref[...] += dk
+            dv_ref[...] += dv
+    dq_ref[...] = dq.T
+
+
+def pair_block(rows):
+    return pl.BlockSpec((rows, 128), lambda i: (0, i))
+
+
+def attend(q, k, v):
+    rows, width = q.shape
+    logs = pl.BlockSpec((1, 2, rows), lambda i: (i, 0, 0))
+    return pl.pallas_call(
+        attend_kernel,
+        grid=(width // 128,),
+        in_specs=[pair_block(rows), pair_block(k.shape[0]), pair_block(k.shape[0])],
+        out_specs=[pair_block(rows), logs],
+        out_shape=[
+            jax.ShapeDtypeStruct((rows, width), jnp.float32),
+            jax.ShapeDtypeStruct((width // 128, 2, rows), jnp.float32),
+        ],
+        compiler_params=pltpu.CompilerParams(vmem_limit_bytes=VMEM_LIMIT),
+    )(q, k, v)
+
+
+def attend_back(q, k, v, o, logs, g):
+    rows, width = q.shape
+    keys = k.shape[0]
+    own, both = pair_block(rows), pair_block(keys)
+    return pl.pallas_call(
+        attend_back_kernel,
+        grid=(width // 128,),
+        in_specs=[own, both, both, own, pl.BlockSpec((1, 2, rows), lambda i: (i, 0, 0)), own],
+        out_specs=[own, both, both],
+        out_shape=[jax.ShapeDtypeStruct((n, width), jnp.float32) for n in (rows, keys, keys)],
+        compiler_params=pltpu.CompilerParams(vmem_limit_bytes=VMEM_LIMIT),
+    )(q, k, v, o, logs, g)
+
+
+GELU_K, GELU_C = 0.7978845608028654, 0.044715
+
+
+def gelu_slope(v):
+    t = jnp.tanh(GELU_K * (v + GELU_C * v * v * v))
+    return 0.5 * (1.0 + t) + 0.5 * v * (1.0 - t * t) * (GELU_K * (1.0 + 3.0 * GELU_C * v * v))
+
+
+def block(row, size):
+    return pl.ds(pl.multiple_of(row * size, size), size)
+
+
+def turned(core, row, last):
+    return core * (last - 2 * row) + row
+
+
+def triple(dst, value, cols):
+    rows, feat = value.shape
+    col = lax.rem(lax.broadcasted_iota(jnp.int32, (rows, 1), 0), cols)
+    left = jnp.where(col == 0, 0.0, pltpu.roll(value, 1, 0))
+    right = jnp.where(col == cols - 1, 0.0, pltpu.roll(value, rows - 1, 0))
+    body = pl.ds(cols, rows)
+    dst[body, 0:feat] = left.astype(dst.dtype)
+    dst[body, feat : 2 * feat] = value.astype(dst.dtype)
+    dst[body, 2 * feat :] = right.astype(dst.dtype)
+
+
+def clear_ends(dst, cols):
+    zero = jnp.zeros((cols, dst.shape[1]), dst.dtype)
+    dst[0:cols, :] = zero
+    dst[dst.shape[0] - cols :, :] = zero
+
+
+def project_kernel(tiles, cols, token_ref, w_ref, out_ref, scratch):
+    tile_rows, tile_cols = tiles
+    core = place()[2]
+    scratch[...] = jnp.dot(token_ref[...], w_ref[...], preferred_element_type=jnp.float32)
+    for r in range(2 * tile_rows):
+        row = turned(core, r, 2 * tile_rows - 1)
+        for z in range(cols):
+            at = ((r // tile_rows) * cols + z) * tile_rows + r % tile_rows
+            out_ref[block(row * cols + z, tile_cols), :] = scratch[
+                at * tile_cols : (at + 1) * tile_cols, :
+            ]
+
+
+def conv_rows(src, w_ref, first, core, cols):
+    rows = src.shape[0] - 2 * cols
+    total = 0.0
+    for a in range(3):
+        total = total + jnp.dot(
+            src[a * cols : a * cols + rows, :],
+            w_ref[first + turned(core, a, 2)],
+            preferred_element_type=jnp.float32,
+        )
+    return total
+
+
+def maps_kernel(
+    cols, f_ref, beyond_ref, w_ref, f0_ref, first0_ref, f1_ref, first1_ref, out_ref, wide
+):
+    core = place()[2]
+    own = f_ref.shape[0]
+    f0_ref[0:own, :] = f_ref[...]
+    for i in range(HALO):
+        f0_ref[own + i * cols : own + (i + 1) * cols, :] = beyond_ref[
+            (HALO - 1 - i) * cols : (HALO - i) * cols, :
+        ]
+    clear_ends(wide, cols)
+    for unit, (f, first, after) in enumerate(
+        ((f0_ref, first0_ref, f1_ref), (f1_ref, first1_ref, None))
+    ):
+        triple(wide, jax.nn.gelu(f[...]), cols)
+        first[...] = conv_rows(wide, w_ref, 6 * unit, core, cols)
+        triple(wide, jax.nn.gelu(first[...]), cols)
+        result = f[...] + conv_rows(wide, w_ref, 6 * unit + 3, core, cols)
+        if after is not None:
+            after[...] = result
+    result = result.astype(out_ref.dtype)
+    rows = own // cols + 2
+    for j in range(rows):
+        i = max(j - 1, 0)
+        out_ref[block(turned(core, j, rows - 1), cols), :] = result[i * cols : (i + 1) * cols]
+
+
+def kernel_grads(wide, grad, out_ref, first, core, cols):
+    own = grad.shape[0]
+    for a in range(3):
+        out_ref[first + turned(core, a, 2)] = outer_product(
+            wide[a * cols : a * cols + own, :], grad
+        ).astype(out_ref.dtype)
+
+
+def conv_back_rows(src, w_ref, first, core, cols):
+    rows, feat = src.shape[0] - 2 * cols, w_ref.shape[2]
+    total = 0.0
+    for a in range(3):
+        tap = w_ref[first + turned(core, 2 - a, 2)]
+        for b in range(3):
+            total = total + back_product(
+                src[a * cols : a * cols + rows, b * feat : (b + 1) * feat],
+                tap[(2 - b) * feat : (3 - b) * feat],
+            )
+    return total
+
+
+def maps_back_kernel(
+    tiles,
+    cols,
+    tall_ref,
+    far_ref,
+    f0_ref,
+    first0_ref,
+    f1_ref,
+    first1_ref,
+    w_ref,
+    g_ref,
+    out_ref,
+    wide,
+    wide_g,
+    total,
+    parted,
+):
+    tile_rows, tile_cols = tiles
+    core = place()[2]
+    own_rows = 2 * tile_rows
+    own = own_rows * cols * tile_cols
+    line = cols * tile_cols
+    edge = own_rows + 1
+
+    def near(i):
+        return tall_ref[block(turned(core, i, edge), line), :]
+
+    def far(i):
+        return far_ref[block(turned(1 - core, i, edge), line), :]
+
+    for i in range(own_rows + 4):
+        at = i * line
+        if i < own_rows:
+            value = near(i + 1)
+            if i == 0:
+                value = value + near(0)
+            if i == own_rows - 1:
+                value = value + far(edge)
+        else:
+            value = far(2 * own_rows - i)
+            if i == own_rows:
+                value = value + near(edge)
+        total[at : at + line, :] = value
+    rest = (own_rows + 4) * line
+    total[rest:, :] = jnp.zeros((total.shape[0] - rest, total.shape[1]), jnp.float32)
+    clear_ends(wide, line)
+    clear_ends(wide_g, line)
+    for unit, (f, first) in ((1, (f1_ref, first1_ref)), (0, (f0_ref, first0_ref))):
+        triple(wide, jax.nn.gelu(first[...]), line)
+        triple(wide_g, total[...], line)
+        kernel_grads(
+            wide, total[0:own, :].astype(wide.dtype), g_ref, 6 * unit + 3, core, line
+        )
+        middle = conv_back_rows(wide_g, w_ref, 6 * unit + 3, core, line)
+        middle = gelu_slope(first[...]) * middle
+        triple(wide, jax.nn.gelu(f[...]), line)
+        triple(wide_g, middle, line)
+        kernel_grads(wide, middle[0:own].astype(wide.dtype), g_ref, 6 * unit, core, line)
+        inner = conv_back_rows(wide_g, w_ref, 6 * unit, core, line)
+        total[...] += gelu_slope(f[...]) * inner
+    for r in range(own_rows):
+        row = turned(core, r, own_rows - 1)
+        for z in range(cols):
+            at = ((r // tile_rows) * cols + z) * tile_rows + r % tile_rows
+            parted[at * tile_cols : (at + 1) * tile_cols, :] = total[
+                block(row * cols + z, tile_cols), :
+            ]
+    out_ref[...] = parted[...].astype(out_ref.dtype)
+
+
+def in_vmem(count):
+    return [pl.BlockSpec(memory_space=pltpu.VMEM)] * count
+
+
+def plain_call(kernel, inputs, out_shape, scratch):
+    return pl.pallas_call(
+        kernel,
+        out_shape=out_shape,
+        in_specs=in_vmem(len(inputs)),
+        out_specs=in_vmem(len(out_shape)),
+        scratch_shapes=scratch,
+        compiler_params=pltpu.CompilerParams(vmem_limit_bytes=VMEM_LIMIT),
+    )(*inputs)
+
+
+def project(tokens_low, w_proj, tiles, cols):
+    shape = (tokens_low.shape[0], w_proj.shape[1])
+    return plain_call(
+        functools.partial(project_kernel, tiles, cols),
+        (tokens_low, w_proj),
+        [jax.ShapeDtypeStruct(shape, jnp.float32)],
+        [pltpu.VMEM(shape, jnp.float32)],
+    )[0]
+
+
+def maps_forward(feature, beyond, w_conv, line):
+    rows, feat = feature.shape
+    ext = jax.ShapeDtypeStruct((rows + HALO * line, feat), jnp.float32)
+    return plain_call(
+        functools.partial(maps_kernel, line),
+        (feature, beyond, w_conv),
+        [ext] * 4 + [jax.ShapeDtypeStruct((rows + 2 * line, feat), jnp.bfloat16)],
+        [pltpu.VMEM((rows + (HALO + 2) * line, 3 * feat), jnp.bfloat16)],
+    )
+
+
+def maps_backward(tall, far, saved, w_conv, tiles, cols):
+    rows, feat = saved[0].shape
+    line = cols * tiles[1]
+    own = 2 * tiles[0] * line
+    return plain_call(
+        functools.partial(maps_back_kernel, tiles, cols),
+        (tall, far, *saved, w_conv),
+        [
+            jax.ShapeDtypeStruct(w_conv.shape, jnp.bfloat16),
+            jax.ShapeDtypeStruct((own, feat), jnp.bfloat16),
+        ],
+        [pltpu.VMEM((rows + 2 * line, 3 * feat), jnp.bfloat16)] * 2
+        + [pltpu.VMEM((rows, feat), jnp.float32), pltpu.VMEM((own, feat), jnp.float32)],
+    )
+
+
+def swap_cores(value):
+    return lax.ppermute(value, "row", [(0, 1), (1, 0), (2, 3), (3, 2)])
+
+
+def halve_patch(grad, axis):
+    grad = jnp.moveaxis(grad, axis, 0)
+    even, odd = grad[0::2], grad[1::2]
+    zero = jnp.zeros_like(even[:1])
+    middle = jnp.concatenate([zero, 0.75 * (even + odd), zero])
+    before = jnp.concatenate([0.25 * even, zero, zero])
+    after = jnp.concatenate([zero, zero, 0.25 * odd])
+    return jnp.moveaxis(middle + before + after, 0, axis)
+
+
+def on_chip(
+    chips,
+    tokens,
+    cot_tokens,
+    cot_merged,
+    image_counts,
+    scale_flags,
+    shift_flags,
+    qkv_w,
+    attn_out_w,
+    fc1_w,
+    fc1_b,
+    fc2_w,
+    fc2_b,
+    ln1_gain,
+    ln1_bias,
+    ln2_gain,
+    ln2_bias,
+    proj_w,
+    conv_w,
+    head_w,
+    head_b,
+    shift_row,
+):
+    slots, tile_rows, tile_cols, width = tokens.shape
+    cols = lax.axis_size("col")
+    sizes = (chips, slots, cols)
+    tile = tile_rows * tile_cols
+    feat = proj_w.shape[1]
+    half_rows, all_cols = 2 * tile_rows, cols * tile_cols
+    dp, y, core, z = place()
+    low = jnp.bfloat16
+    count = image_counts[0]
+    present = (jnp.arange(slots) < count).astype(jnp.float32)
+    factor = 0.5 + 0.5 * scale_flags.astype(jnp.float32)
+    shift_sign = shift_flags.astype(jnp.float32)
+    full_group = count == slots
+    chip = y * cols + z
+    borrowed = jnp.logical_and(jnp.logical_not(full_group), chip >= 2 * chips - slots)
+    image_present = jnp.where(
+        jnp.logical_or(jnp.logical_or(full_group, borrowed), chip < count), 1.0, 0.0
+    )
+
+    vectors = (fc1_b, fc2_b, ln1_gain, ln1_bias, ln2_gain, ln2_bias, head_b, shift_row)
+    lengths = [v.shape[0] for v in vectors]
+    own_small = jnp.concatenate([v.astype(low) for v in vectors] + [head_w.astype(low).reshape(-1)])
+    far_small = lax.ppermute(own_small, "dp", [(0, 1), (1, 0)])
+    lower = jnp.where(dp == 0, own_small, far_small).astype(jnp.float32)
+    upper = jnp.where(dp == 0, far_small, own_small).astype(jnp.float32)
+    small, at = [], 0
+    for length in lengths:
+        small.append(jnp.concatenate([lower[at : at + length], upper[at : at + length]]))
+        at += length
+    b_up, b_down, gain_one, bias_one, gain_two, bias_two, b_head, w_shift = small
+    w_head = jnp.concatenate([lower[at:], upper[at:]]).reshape(feat, feat).astype(low)
+
+    merged_grad = cot_merged.astype(jnp.float32).reshape(slots, -1, feat) * present[:, None, None]
+    grad_shift = jnp.sum(merged_grad * shift_sign[:, None, None], (0, 1))
+    head_grad = (merged_grad * factor[:, None, None]).astype(low).reshape(-1, feat)
+    grad_head_b = jnp.sum(head_grad.astype(jnp.float32), 0)
+    fine_grad = back_product(head_grad, w_head).astype(low).reshape(cot_merged.shape)
+    patch_grad = halve_patch(halve_patch(fine_grad.astype(jnp.float32), 1), 2).astype(low)
+    cells = (tile_rows + 2) * (tile_cols + 2)
+    patch_grad = jnp.pad(
+        patch_grad.reshape(slots, cells, feat), ((0, 0), (0, PATCH - cells), (0, 0))
+    )
+
+    halves = {
+        "qkv": qkv_w[None],
+        "out": attn_out_w[None],
+        "fc1": fc1_w[None],
+        "fc2": fc2_w[None],
+        "conv": conv_w.reshape((36,) + conv_w.shape[3:]),
+        "proj": proj_w[None],
+    }
+    halves = {name: half.astype(low) for name, half in halves.items()}
+    (images, image_cots, image_patches), weights = bring_in(
+        (tokens.reshape(slots, tile, width), cot_tokens.reshape(slots, tile, width), patch_grad),
+        halves,
+        sizes,
+    )
+    w_qkv, w_out, w_up, w_down, w_proj = (
+        weights[name][0] for name in ("qkv", "out", "fc1", "fc2", "proj")
+    )
+    w_conv = weights["conv"].reshape(12, 3 * feat, feat)
+
+    def chosen(pair):
+        return jnp.where(borrowed, pair[1], pair[0])
+
+    stream = chosen(images).reshape(-1, width).astype(jnp.float32)
+    rows = stream.shape[0]
+
+    normed, scaled_one, factor_one = norm_rows(stream, gain_one, bias_one)
+    normed_low = normed.astype(low)
+    projected = jnp.dot(normed_low, w_qkv, preferred_element_type=jnp.float32).astype(low)
+    queries, pair_own = projected[:, :width], projected[:, width:]
+    pair_far = swap_cores(pair_own)
+    keys = jnp.concatenate([pair_own[:, :width], pair_far[:, :width]])
+    values = jnp.concatenate([pair_own[:, width:], pair_far[:, width:]])
+    attended_wide, logs = attend(queries, keys, values)
+    attended = attended_wide.astype(low)
+    after_attn = stream + jnp.dot(attended, w_out, preferred_element_type=jnp.float32)
+    normed_two, scaled_two, factor_two = norm_rows(after_attn, gain_two, bias_two)
+    normed_two_low = normed_two.astype(low)
+    hidden = jnp.dot(normed_two_low, w_up, preferred_element_type=jnp.float32) + b_up
+    hidden_low = jax.nn.gelu(hidden).astype(low)
+    after_mlp = after_attn + (
+        jnp.dot(hidden_low, w_down, preferred_element_type=jnp.float32) + b_down
+    )
+    tokens_low = after_mlp.astype(low)
+    tiles = (tile_rows, tile_cols)
+    feature = project(tokens_low, w_proj, tiles, cols)
+    beyond = swap_cores(feature[(half_rows - HALO) * all_cols :])
+    *saved, coarse = maps_forward(feature, beyond, w_conv, all_cols)
+
+    coarse = coarse.reshape(half_rows + 2, all_cols, feat)
+    coarse = jnp.concatenate([coarse[:, :1], coarse, coarse[:, -1:]], 1)
+    cuts = [
+        coarse[
+            r * tile_rows : (r + 1) * tile_rows + 2, c * tile_cols : (c + 1) * tile_cols + 2
+        ].reshape(cells, feat)
+        for r in range(2)
+        for c in range(cols)
+    ]
+    patch = jnp.pad(jnp.stack(cuts), ((0, 0), (0, PATCH - cells), (0, 0)))
+    patch = patches_out(patch, sizes)[:, :cells]
+    patch = patch.reshape(slots, tile_rows + 2, tile_cols + 2, feat).astype(jnp.float32)
+    patch = jnp.where(present[:, None, None, None] > 0, patch, 0.0)
+    upsampled = double_axis(double_axis(patch, 1), 2).astype(low)
+    fine_rows = upsampled.reshape(-1, feat)
+    head_out = jnp.dot(fine_rows, w_head, preferred_element_type=jnp.float32) + b_head
+    head_out = head_out.reshape(slots, -1, feat)
+    merged = (head_out * factor[:, None, None] + shift_sign[:, None, None] * w_shift) * present[
+        :, None, None
+    ]
+    merged_out = merged.astype(low).reshape(cot_merged.shape)
+    grad_head_w = outer_product(fine_rows, head_grad)
+
+    parts = chosen(image_patches)[:, :cells].astype(jnp.float32)
+    parts = parts.reshape(2, cols, tile_rows + 2, tile_cols + 2, feat)
+    wide = sum(
+        jnp.pad(parts[:, c], ((0, 0), (0, 0), (c * tile_cols, (cols - 1 - c) * tile_cols), (0, 0)))
+        for c in range(cols)
+    )
+    wide = jnp.concatenate(
+        [wide[:, :, 1:2] + wide[:, :, :1], wide[:, :, 2:-2], wide[:, :, -2:-1] + wide[:, :, -1:]], 2
+    )
+    tall = jnp.pad(wide[0], ((0, tile_rows), (0, 0), (0, 0))) + jnp.pad(
+        wide[1], ((tile_rows, 0), (0, 0), (0, 0))
+    )
+    tall = tall.reshape(-1, feat)
+    grad_conv, proj_grad = maps_backward(tall, swap_cores(tall), saved, w_conv, tiles, cols)
+    grad_conv = grad_conv.reshape(36, feat, feat)
+
+    grad_proj = outer_product(tokens_low, proj_grad)
+    stream_grad = chosen(image_cots).reshape(rows, width).astype(jnp.float32)
+    stream_grad = jnp.where(image_present > 0, stream_grad, 0.0) + back_product(proj_grad, w_proj)
+    down_grad = stream_grad.astype(low)
+    grad_down_b = jnp.sum(down_grad.astype(jnp.float32), 0)
+    grad_down_w = outer_product(hidden_low, down_grad)
+    up_grad = gelu_grad(hidden, back_product(down_grad, w_down)).astype(low)
+    grad_up_b = jnp.sum(up_grad.astype(jnp.float32), 0)
+    grad_up_w = outer_product(normed_two_low, up_grad)
+    norm_grad, grad_gain_two, grad_bias_two = norm_back(
+        back_product(up_grad, w_up), scaled_two, factor_two, gain_two
+    )
+    stream_grad = stream_grad + norm_grad
+    branch_grad = stream_grad.astype(low)
+    grad_out_w = outer_product(attended, branch_grad)
+    attended_grad = back_product(branch_grad, w_out).astype(low)
+    query_grad, key_grad, value_grad = attend_back(
+        queries, keys, values, attended_wide, logs, attended_grad
+    )
+    pair_grad = jnp.concatenate([key_grad, value_grad], 1)
+    pair_grad = pair_grad[:rows] + swap_cores(pair_grad[rows:].astype(low)).astype(jnp.float32)
+    mixed_grad = jnp.concatenate([query_grad, pair_grad], 1).astype(low)
+    grad_qkv = outer_product(normed_low, mixed_grad)
+    norm_grad, grad_gain_one, grad_bias_one = norm_back(
+        back_product(mixed_grad, w_qkv), scaled_one, factor_one, gain_one
+    )
+    input_grad = (stream_grad + norm_grad).astype(low)
+
+    vector_grads = (
+        grad_up_b,
+        grad_down_b,
+        grad_gain_one,
+        grad_bias_one,
+        grad_gain_two,
+        grad_bias_two,
+        grad_head_b,
+        grad_shift,
+    )
+    packed = jnp.concatenate([v.reshape(2, -1) for v in vector_grads], 1).astype(low)
+    room = 128 * feat
+    packed = jnp.pad(packed, ((0, 0), (0, room - packed.shape[1]))).reshape(256, feat)
+    grads = {
+        "conv": grad_conv,
+        "fc2": grad_down_w.astype(low)[None],
+        "fc1": grad_up_w.astype(low)[None],
+        "qkv": grad_qkv.astype(low)[None],
+        "out": grad_out_w.astype(low)[None],
+        "proj": grad_proj.astype(low)[None],
+        "head": grad_head_w.astype(low)[None],
+        "small": packed[None],
+    }
+    (slot_tokens, slot_grads), sums = bring_out(
+        (tokens_low.reshape(chips, tile, width), input_grad.reshape(chips, tile, width)),
+        grads,
+        sizes,
+    )
+    here = present[:, None, None] > 0
+    tokens_out = jnp.where(here, slot_tokens, 0).reshape(tokens.shape)
+    grad_tokens = jnp.where(here, slot_grads.astype(jnp.float32), 0.0).reshape(tokens.shape)
+    sums = {name: value.astype(jnp.float32) for name, value in sums.items()}
+    packed = sums["small"].reshape(-1)
+    pieces, at = [], 0
+    for length in lengths:
+        pieces.append(packed[at : at + length])
+        at += length
+    return (
+        tokens_out,
+        merged_out,
+        grad_tokens,
+        sums["qkv"][0],
+        sums["out"][0],
+        sums["fc1"][0],
+        pieces[0],
+        sums["fc2"][0],
+        pieces[1],
+        pieces[2],
+        pieces[3],
+        pieces[4],
+        pieces[5],
+        sums["proj"][0],
+        sums["conv"].reshape(conv_w.shape),
+        sums["head"][0],
+        pieces[6],
+        pieces[7],
+    )
+
+
 def solution(mesh):
+    groups, tile_rows, tile_cols = (mesh.shape[axis] for axis in ("dp", "row", "col"))
+    chips = tile_rows // 2 * tile_cols
+    fits = groups == 2 and tile_rows == 4 and tile_cols == 4
     placed = (
         P("dp", "row", "col", None),
         P("dp", "row", "col", None),
@@ -507,7 +1542,7 @@
         P("dp"),
     )
     return jax.shard_map(
-        on_device,
+        functools.partial(on_chip, chips) if fits else on_device,
         mesh=mesh,
         in_specs=placed,
         out_specs=(

time: 1650 us -> 798 us (0.48)
  waiting for transfers between devices: 862 us -> 2.04 us
  Pallas kernels: 0 us -> 613 us
  matrix products: 215 us -> 61.6 us
  local copies, waits for them, and re-layouts: 185 us -> 39 us
  blocking collectives: 118 us -> 0 us
  starting transfers between devices: 105 us -> 6.12 us
  other arithmetic: 131 us -> 65.1 us
  between operations: 19.7 us -> 3.01 us
    pallas_call x0 -> x8, Pallas kernels: none -> 613 us  [the longest x1 322 us: bring_in(): pl.pallas_call(functools.partial(in_kernel, sizes, names), out_shape=out_...]
    reduce_scatter x8 -> x0, waiting for transfers between devices: 472 us -> none  [the longest x1 187 us: on_device(): lax.psum_scatter(jnp.concatenate([key_part.reshape(lax.axis_size(('row',...]
    all_gather x7 -> x0, waiting for transfers between devices: 256 us -> none  [the longest x1 72.1 us: on_device(): lax.all_gather(values_own, ('row', 'col'), axis=1, tiled=True)]
    dot_general x20 -> x5, matrix products: 151 us -> 15.6 us  [the longest x1 5.65 us: on_chip(): jnp.dot(normed_two_low, w_up, preferred_element_type=jnp.float32) + b_up]
    psum x1 -> x0, waiting for transfers between devices: 97.9 us -> none  [on_device(): lax.psum(shards[0].astype(jnp.bfloat16), ('row', 'col')).astype(jnp.float32)]
    ppermute x40 -> x5, starting transfers between devices: 104 us -> 6.12 us  [the longest x4 3.12 us: swap_cores(): return lax.ppermute(value, 'row', [(0, 1), (1, 0), (2, 3), (3, 2)])]
    psum x1 -> x0, blocking collectives: 63.2 us -> none  [on_device(): lax.psum(shards[3].astype(jnp.bfloat16), ('row', 'col')).astype(jnp.float32)]
    reshape x6 -> x9, local copies, waits for them, and re-layouts: 52.4 us -> 1.33 us  [the longest x6 0.66 us: on_chip(): v.reshape(2, -1)]
  transfers between devices with their start and end apart: 56 -> 5, of which waited for: 30 -> 2; matrix products, arithmetic and copies ran while one was open for 18% -> 7% of each run, Pallas kernels for 0% -> 4%
where the time goes in v1:
time: 798 us; the launch traced here: 790 us
  Pallas kernels  613 us (77%)
  other arithmetic  65.1 us (8%)
  matrix products  61.6 us (8%)
  local copies, waits for them, and re-layouts  39 us (5%)
    pallas_call x1, Pallas kernels, bring_in(): pl.pallas_call(functools.partial(in_kernel, sizes, names), out_shape=out_...  322 us
    pallas_call x1, Pallas kernels, bring_out(): pl.pallas_call(functools.partial(out_kernel, sizes, n, [i // 2 for i in r...  197 us
    pallas_call x3, Pallas kernels, plain_call(): pl.pallas_call(kernel, out_shape=out_shape, in_specs=in_vmem(len(inputs))...  33.4 us
    pallas_call x1, Pallas kernels, patches_out(): pl.pallas_call(functools.partial(patch_kernel, sizes), out_shape=jax.Shap...  27.9 us
    dot_general x6, matrix products, outer_product(): lax.dot_general(first_op, second_op, (((0,), (0,)), ((), ())), preferred_...  26.2 us
    dot_general x6, matrix products, back_product(): lax.dot_general(first_op, weight, (((1,), (1,)), ((), ())), preferred_ele...  19.8 us
    pallas_call x1, Pallas kernels, attend_back(): pl.pallas_call(attend_back_kernel, grid=(width // 128,), in_specs=[own, b...  18.9 us
  transfers between devices with their start and end apart: 5, of which 2 were waited for; matrix products, arithmetic and copies ran while one was open for 7% of the time, Pallas kernels for 4%

profile of v1, /device:TPU:0, one launch (start us, length us, event | category | flops | bytes accessed | tf_op | source)
XLA Modules:
  0.0 790.3 jit_solution(10110411545311805710)
XLA Ops:
  9.7 3.0 collective-permute-start
  14.7 2.6 fusion.9
  19.2 2.1 convert_element_type.330
  21.4 3.5 convert_element_type.329
  25.1 1.7 convert_element_type.331
  26.9 4.0 convert_element_type.332
  30.8 1.7 convert_element_type.333
  35.3 3.3 slice.241
  38.6 1.4 add_multiply_fusion.1
  41.8 321.8 %shard_map.340 = (bf16[2,8,64,768]{3,2,1,0:T(8,128)(2,1)}, bf16[2,8,64,768]{3,2,1,0:T(8,128)(2,1)}, bf16[2,8,112,256]{3,2,1,0:T(8,128)(2,1)}, bf16[1,2,2,2,2,48,...) custom-call(bf16[10,64,768]{2,1,0:T(8,128)(2,1)} %bitcast.226, ...), custom_call_target="tpu_custom_call" | custom-call | tf_op jit(solution)/shard_map/pallas_call | solution.py:739
  371.5 2.0 convolution_convert_fusion.3
  379.7 14.1 %shard_map.341 = (f32[512,768]{1,0:T(8,128)}, f32[6,2,512]{2,1,0:T(2,128)}) custom-call(bf16[512,768]{1,0:T(8,128)(2,1)} %get-tuple-element.95.q_ref, bf16[1024,768]{1,0:T(8,128)(2,1)} %pad_maximum_fusion.2.k_ref, bf16[1024,768]{1,0:T(8,128)(2,1)} %pad_maximum_fusion.3.v_ref), custom_call_target="tpu_custom_call" | custom-call | tf_op jit(solution)/shard_map/pallas_call | solution.py:1007
  393.9 2.6 fusion.78
  396.8 5.7 fusion.66
  402.5 4.9 add_convert_fusion.token_ref
  407.4 2.4 shard_map.342.f_ref
  412.9 11.5 %shard_map.343 = (f32[704,256]{1,0:T(8,128)}, f32[704,256]{1,0:T(8,128)}, f32[704,256]{1,0:T(8,128)}, f32[704,256]{1,0:T(8,128)}, bf16[576,256]{1,0:T(8,128)(2,1)}) custom-call(f32[512,256]{1,0:T(8,128)} %shard_map.342.f_ref, f32[192,256]{1,0:T(8,128)} %copy-done.32, bf16[12,768,256]{2,1,0:T(8,128)(2,1)} %bitcast.186), custom_call_target="tpu_custom_call" | custom-call | tf_op jit(solution)/shard_map/pallas_call | solution.py:1215
  425.3 19.5 %shard_map.344 = (bf16[12,768,256]{2,1,0:T(8,128)(2,1)}, bf16[512,256]{1,0:T(8,128)(2,1)}) custom-call(f32[576,256]{1,0:T(8,128)} %bitcast.208, f32[576,256]{1,0:T(8,128)} %copy-done.27, f32[704,256]{1,0:T(8,128)} %get-tuple-element.59.f0_ref, f32[704,256]{1,0:T(8,128)} %get-tuple-element.60.first0_ref, f32[704,256]{1,0:T(8,128)} %get-tuple-element.61.f1_ref, ...), custom_call_target="tpu_custom_call" | custom-call | tf_op jit(solution)/shard_map/pallas_call | solution.py:1215
  444.8 2.2 convolution_convert_fusion.7
  447.4 10.0 %fusion.79 = (bf16[3072]{0:T(1024)(128)(2,1)S(1)}, bf16[512,3072]{1,0:T(8,128)(2,1)S(1)}) fusion(f32[512,3072]{1,0:T(8,128)} %copy-done.54, f32[3072]{0:T(1024)S(1)} %pad_maximum_fusion.12, bf16[3072,768]{1,0:T(8,128)(2,1)} %bitcast.243, f32[512,768]{1,0:T(8,128)S(1)} %get-tuple-element.158), kind=kOutput, calls=%fused_computation.199 | convolution fusion | flops 2450912256 | bytes 15747072 | tf_op jit(solution)/shard_map/dot_general | solution.py:59
  457.4 3.5 multiply_reduce_fusion.1
  462.3 1.8 convolution_convert_fusion.6.g_ref
  464.5 1.8 convolution_convert_fusion.5
  468.4 27.9 %shard_map.346 = bf16[10,112,256]{2,1,0:T(8,128)(2,1)} custom-call(bf16[8,112,256]{2,1,0:T(8,128)(2,1)} %pad.47.src), custom_call_target="tpu_custom_call" | custom-call | tf_op jit(solution)/shard_map/pallas_call | solution.py:769
  497.6 1.5 fusion.14
  499.4 2.4 copy.60
  501.9 2.6 reshape.424
  505.0 2.4 copy.61
  507.4 3.3 convert_element_type.363
  512.1 18.9 %shard_map.345 = (f32[512,768]{1,0:T(8,128)}, f32[1024,768]{1,0:T(8,128)}, f32[1024,768]{1,0:T(8,128)}) custom-call(bf16[512,768]{1,0:T(8,128)(2,1)} %get-tuple-element.95.q_ref, bf16[1024,768]{1,0:T(8,128)(2,1)} %pad_maximum_fusion.2.k_ref, bf16[1024,768]{1,0:T(8,128)(2,1)} %pad_maximum_fusion.3.v_ref, f32[512,768]{1,0:T(8,128)} %get-tuple-element.51.o_ref, ...), custom_call_target="tpu_custom_call" | custom-call | tf_op jit(solution)/shard_map/pallas_call | solution.py:1024
  531.0 2.5 constant_dynamic-update-slice_fusion.3
  534.3 1.5 slice.425
  535.8 2.3 collective-permute-start.4
  538.8 1.9 multiply_convert_fusion.1
  540.7 1.6 convert.71
  542.5 6.8 convolution_convert_fusion.1
  549.4 8.9 %convolution_convert_fusion.2 = bf16[3072,768]{1,0:T(8,128)(2,1)} fusion(f32[512,768]{1,0:T(8,128)S(1)} %copy-done.9, f32[512,3072]{1,0:T(8,128)} %copy-done.54, f32[3072]{0:T(1024)S(1)} %pad_maximum_fusion.12), kind=kOutput, calls=%fused_computation.12 | convolution fusion | flops 2434400256 | bytes 12595200 | tf_op jit(solution)/shard_map/dot_general | solution.py:53
  558.4 2.1 fusion.7
  560.8 3.6 fusion.33
  565.3 5.1 convolution_convert_fusion
  570.4 1.4 fusion.30
  571.9 197.2 %shard_map.347 = (bf16[10,64,768]{2,1,0:T(8,128)(2,1)}, bf16[10,64,768]{2,1,0:T(8,128)(2,1)}, bf16[36,2,2,2,16,256]{5,4,3,2,1,0:T(8,128)(2,1)}, bf16[1,2,2,2,192...) custom-call(bf16[8,64,768]{2,1,0:T(8,128)(2,1)} %bitcast.204, ...), custom_call_target="tpu_custom_call" | custom-call | tf_op jit(solution)/shard_map/pallas_call | solution.py:916
  771.2 2.3 select_bitcast_fusion.1
  776.2 1.5 select_bitcast_fusion
  778.9 2.1 bitcast_convert_fusion.2
  781.4 2.9 bitcast_convert_fusion.1
  784.3 2.7 bitcast_convert_fusion
  787.0 2.8 convert.93
  (292 shorter events, 51.8 us)
Async XLA Ops:
  5.4 11.9 %copy-start.5 = (bf16[10,16,16,256]{3,2,1,0:T(8,128)(2,1)S(1)}, bf16[10,16,16,256]{3,2,1,0:T(8,128)(2,1)}, u32[]{:S(2)}) copy-start(bf16[10,16,16,256]{3,2,1,0:T(8,128)(2,1)} %param.23) | copy-start | bytes 3932164
  9.7 22.9 %collective-permute-start = (bf16[36480]{0:T(1024)(128)(2,1)S(1)}, bf16[36480]{0:T(1024)(128)(2,1)S(1)}, u32[]{:S(2)}, u32[]{:S(2)}) collective-permute-start(bf16[36480]{0:T(1024)(128)(2,1)S(1)} %dynamic-update-slice.28), channel_id=1, source_target_pairs={{0,16},{16,0},{1,17},{17,1},{2,18},{18,2},{3,19},{19,3},{4,20},{20... | collective-permute-start | bytes 218888 | tf_op jit(solution)/shard_map/ppermute | solution.py:1322
  14.0 4.5 copy-start.38
  14.6 3.9 copy-start.40
  14.7 3.8 copy-start.53
  14.7 3.8 copy-start.29
  18.5 392.4 %copy-start.46 = (f32[10]{0:T(128)}, f32[10]{0:T(128)S(1)}, u32[]{:S(2)}) copy-start(f32[10]{0:T(128)S(1)} %convert_element_type.370) | copy-start | bytes 124
  21.4 3.8 copy-start.10
  21.4 9.5 %slice-start.2 = ((s8[4718592]{0:T(1024)(128)(4,1)}), s8[4194304]{0:T(1024)(128)(4,1)S(1)}, s32[]{:S(2)}) async-start(s8[4718592]{0:T(1024)(128)(4,1)} %bitcast.201), calls=%async_computation.2 | async-start | bytes 8388608
  25.1 5.7 slice-start.3
  373.7 3.5 collective-permute-start.1
  374.0 50.5 %collective-permute-start.2 = (f32[576,256]{1,0:T(8,128)S(1)}, f32[576,256]{1,0:T(8,128)S(1)}, u32[]{:S(2)}, u32[]{:S(2)}) collective-permute-start(f32[576,256]{1,0:T(8,128)S(1)} %bitcast.207), channel_id=1, source_target_pairs={{0,4},{4,0},{8,12},{12,8},{1,5},{5,1},{9,13},{13,9},{2,6},{6,2},{1... | collective-permute-start | bytes 1769480 | tf_op jit(solution)/shard_map/ppermute | solution.py:1263
  375.0 21.8 %copy-start.44 = (f32[768]{0:T(1024)}, f32[768]{0:T(1024)S(1)}, u32[]{:S(2)}) copy-start(f32[768]{0:T(1024)S(1)} %pad_maximum_fusion.16) | copy-start | bytes 9220
  396.5 64.5 %copy-start = (f32[512,768]{1,0:T(8,128)}, f32[512,768]{1,0:T(8,128)S(1)}, u32[]{:S(2)}) copy-start(f32[512,768]{1,0:T(8,128)S(1)} %get-tuple-element.152) | copy-start | bytes 4718596
  396.5 6.0 slice-start.6
  396.8 64.2 %copy-start.35 = (f32[512]{0:T(512)}, f32[512]{0:T(512)S(1)}, u32[]{:S(2)}) copy-start(f32[512]{0:T(512)S(1)} %add_rsqrt_fusion.1) | copy-start | bytes 6148
  396.8 5.7 slice-start.7
  402.5 4.9 copy-start.54
  410.7 1.5 collective-permute-start.3
  425.3 19.5 %copy-start.11 = (bf16[512,768]{1,0:T(8,128)(2,1)S(1)}, bf16[512,768]{1,0:T(8,128)(2,1)}, u32[]{:S(2)}) copy-start(bf16[512,768]{1,0:T(8,128)(2,1)} %add_convert_fusion.token_ref) | copy-start | bytes 2359300
  447.0 10.4 %slice-start.4 = ((s8[4718592]{0:T(1024)(128)(4,1)}), s8[4194304]{0:T(1024)(128)(4,1)S(1)}, s32[]{:S(2)}) async-start(s8[4718592]{0:T(1024)(128)(4,1)} %bitcast.240), calls=%async_computation.4 | async-start | bytes 8388608
  447.4 13.6 %copy-start.8 = (f32[512,768]{1,0:T(8,128)}, f32[512,768]{1,0:T(8,128)S(1)}, u32[]{:S(2)}) copy-start(f32[512,768]{1,0:T(8,128)S(1)} %get-tuple-element.158) | copy-start | bytes 4718596
  447.4 10.0 %slice-start.5 = ((s8[4718592]{0:T(1024)(128)(4,1)}), s8[524288]{0:T(1024)(128)(4,1)S(1)}, s32[]{:S(2)}) async-start(s8[4718592]{0:T(1024)(128)(4,1)} %bitcast.240), calls=%async_computation.5 | async-start | bytes 1048576
  457.4 3.6 copy-start.55
  464.5 2.5 copy-start.22
  507.4 3.3 copy-start.6
  507.4 3.3 copy-start.39
  507.4 3.3 copy-start.41
  531.0 2.8 copy-start.12
  534.3 3.8 copy-start.7
  534.3 3.8 copy-start.26
  534.3 3.8 copy-start.43
  535.8 22.5 %collective-permute-start.4 = (bf16[512,1536]{1,0:T(8,128)(2,1)}, bf16[512,1536]{1,0:T(8,128)(2,1)}, u32[]{:S(2)}, u32[]{:S(2)}) collective-permute-start(bf16[512,1536]{1,0:T(8,128)(2,1)} %slice.425), channel_id=1, source_target_pairs={{0,4},{4,0},{8,12},{12,8},{1,5},{5,1},{9,13},{13,9},{2,6},{6,2},{1... | collective-permute-start | bytes 4718600 | tf_op jit(solution)/shard_map/ppermute | solution.py:1263
  542.5 6.8 copy-start.9
  542.5 15.8 %slice-start = ((s8[6291456]{0:T(1024)(128)(4,1)}), s8[4194304]{0:T(1024)(128)(4,1)S(1)}, s32[]{:S(2)}) async-start(s8[6291456]{0:T(1024)(128)(4,1)} %bitcast.189), calls=%async_computation | async-start | bytes 8388608
  549.4 9.0 %slice-start.1 = ((s8[6291456]{0:T(1024)(128)(4,1)}), s8[2097152]{0:T(1024)(128)(4,1)S(1)}, s32[]{:S(2)}) async-start(s8[6291456]{0:T(1024)(128)(4,1)} %bitcast.189), calls=%async_computation.1 | async-start | bytes 4194304
  558.3 2.5 copy-start.52
  560.8 3.7 copy-start.50
  565.3 5.1 copy-start.3
  565.3 5.1 copy-start.20
  571.9 199.4 %copy-start.42 = (pred[10]{0:T(512)(128)(4,1)S(1)}, pred[10]{0:T(512)(128)(4,1)}, u32[]{:S(2)}) copy-start(pred[10]{0:T(512)(128)(4,1)} %get-tuple-element.160) | copy-start | bytes 34
  769.0 5.7 copy-start.33
  769.0 6.4 copy-start.31
  769.0 7.2 copy-start.24
  776.2 2.6 copy-start.17
  778.9 2.5 copy-start.16
  781.4 2.9 copy-start.15
  784.3 2.7 copy-start.14
  (21 other events, 36.1 us)

commit v2 on v1

--- a/solution.py
+++ b/solution.py
@@ -649,42 +649,39 @@
     }[bit]
 
 
-PIECE_BITS = ("y", "z1", "core")
-GATHER_ORDERS = (("dp", "z1", "y", "core"), ("dp", "y", "z1", "core"))
-
-
-def gather_steps(half, whole, local_sem, send_sem, recv_sem, order):
-    held = {bit: bit_of(bit) for bit in PIECE_BITS}
-    dp = bit_of("dp")
-    copies = []
-
-    def start(step):
-        bit = order[step]
-        at = tuple(held[b] if held[b] is not None else slice(None) for b in PIECE_BITS)
-        if bit == "dp":
-            src = half.at[(slice(None),) + at]
-            far = whole.at[(slice(None), dp) + at]
-            for piece in range(8):
-                of = (slice(None), piece // 4, piece // 2 % 2, piece % 2)
-                local = pltpu.make_async_copy(
-                    half.at[of], whole.at[of[:1] + (dp,) + of[1:]], local_sem.at[piece]
-                )
-                local.start()
-                copies.append(local)
+class Gather:
+    def __init__(self, whole, send_sem, recv_sem, order):
+        self.whole, self.sems, self.order = whole, (send_sem, recv_sem), order + ("core",)
+        self.rows = whole.shape[-2] // 16
+        self.next, self.copy = 0, None
+
+    def at(self, step):
+        dp, core = bit_of("dp"), bit_of("core")
+        first, second = (bit_of(bit) for bit in self.order[:2])
+        start = (core * 4, core * 4 + second * 2, core * 4 + second * 2 + first)
+        if step == 0:
+            piece, size = dp * 8 + start[2], 1
         else:
-            src = whole.at[(slice(None), 1 - dp) + at]
-            far = src
-        copy = send(src, far, send_sem.at[step], recv_sem.at[step], *mate(bit))
-        copy.start()
-        copies.append(copy)
-
-    def wait(step):
-        while copies:
-            copies.pop().wait()
-        if order[step] != "dp":
-            held[order[step]] = None
-
-    return len(order), start, wait
+            piece, size = (1 - dp) * 8 + start[3 - step], 2 ** (step - 1)
+        rows = pl.ds(pl.multiple_of(piece * self.rows, 16), size * self.rows)
+        return self.whole.at[(slice(None),) * (len(self.whole.shape) - 2) + (rows,)]
+
+    def tick(self):
+        if self.copy is not None:
+            self.copy.wait()
+            self.copy = None
+        if self.next < 4:
+            bit = (("dp",) + self.order)[self.next]
+            part = self.at(self.next)
+            self.copy = send(
+                part, part, self.sems[0].at[self.next], self.sems[1].at[self.next], *mate(bit)
+            )
+            self.copy.start()
+            self.next += 1
+
+    def finish(self):
+        while self.copy is not None:
+            self.tick()
 
 
 def pipeline(jobs):
@@ -695,68 +692,6 @@
                 wait(step - 1)
             if 0 <= step < steps:
                 start(step)
-
-
-def in_kernel(sizes, names, *refs):
-    n = len(names)
-    tiles, refs = refs[:3], refs[3:]
-    halves, refs = refs[:n], refs[n:]
-    images, refs = refs[:3], refs[3:]
-    wholes, refs = refs[:n], refs[n:]
-    tile_send, tile_recv, local_sem, send_sem, recv_sem = refs
-    for i in range(3):
-        to_images_start(tiles[i], images[i], tile_send.at[i], tile_recv.at[i], sizes)
-    jobs = []
-    for i in range(n):
-        steps, start, wait = gather_steps(
-            halves[i],
-            wholes[i],
-            local_sem.at[i],
-            send_sem.at[i],
-            recv_sem.at[i],
-            GATHER_ORDERS[i % 2],
-        )
-        jobs.append((i // 2, steps, start, wait))
-    pipeline(jobs)
-    for i in range(3):
-        to_images_wait(tiles[i], images[i], tile_send.at[i], tile_recv.at[i], sizes)
-
-
-def bring_in(tiles, halves, sizes):
-    chips, slots, cols = sizes
-    names = list(halves)
-    cut = {}
-    for name, half in halves.items():
-        lead, rows, width = half.shape
-        cut[name] = half.reshape(lead, 2, 2, 2, rows // 8, width)
-    out_shape = [
-        jax.ShapeDtypeStruct((2, chips) + tile.shape[1:], tile.dtype) for tile in tiles
-    ] + [
-        jax.ShapeDtypeStruct((cut[name].shape[0], 2) + cut[name].shape[1:], jnp.bfloat16)
-        for name in names
-    ]
-    n = len(names)
-    outs = pl.pallas_call(
-        functools.partial(in_kernel, sizes, names),
-        out_shape=out_shape,
-        in_specs=[pl.BlockSpec(memory_space=pltpu.HBM)] * (3 + n),
-        out_specs=[pl.BlockSpec(memory_space=pltpu.HBM)] * (3 + n),
-        scratch_shapes=[
-            pltpu.SemaphoreType.DMA((3, slots)),
-            pltpu.SemaphoreType.DMA((3, 2 * chips)),
-            pltpu.SemaphoreType.DMA((n, 8)),
-            pltpu.SemaphoreType.DMA((n, 4)),
-            pltpu.SemaphoreType.DMA((n, 4)),
-        ],
-        compiler_params=pltpu.CompilerParams(
-            has_side_effects=True, vmem_limit_bytes=VMEM_LIMIT
-        ),
-    )(*tiles, *(cut[name] for name in names))
-    wholes = {}
-    for name, whole in zip(names, outs[3:]):
-        lead, rows, width = halves[name].shape
-        wholes[name] = whole.reshape(lead, 2 * rows, width)
-    return outs[:3], wholes
 
 
 def patch_kernel(sizes, src, dst, send_sem, recv_sem):
@@ -783,14 +718,24 @@
 
 SUM_ORDERS = (
     ("dp", "y", "z1", "z2"),
-    ("y", "dp", "z1", "z2"),
+    ("y", "z1", "dp", "z2"),
     ("z1", "dp", "y", "z2"),
 )
 BACK_ORDERS = (
     ("z2", "z1", "y", "core"),
     ("z2", "y", "z1", "core"),
-    ("z2", "y", "z1", "core"),
+    ("z2", "z1", "y", "core"),
 )
+TURNS = {
+    "conv": (0, 0),
+    "fc2": (1, 0),
+    "fc1": (2, 0),
+    "qkv": (2, 1),
+    "out": (1, 1),
+    "proj": (0, 1),
+    "head": (0, 1),
+    "small": (0, 1),
+}
 
 
 def reduce_steps(grad, out, acc, recvs, sems, orders):
@@ -865,15 +810,13 @@
     return forward + 1 + len(back_order), start, wait
 
 
-def recv_shapes(shape, order):
+def recv_shapes(shape):
     lead, rows, width = shape[0], shape[5], shape[6]
-    free, out = 4, []
-    for step in range(1 + len(order)):
-        out.append((lead,) + (2,) * (4 - step) + (rows, width // 2))
-    return out
-
-
-def out_kernel(sizes, n, delays, *refs):
+    return [(lead,) + (2,) * free + (rows, width // 2) for free in (4, 3, 2, 1, 0)]
+
+
+def out_kernel(sizes, turns, *refs):
+    n = len(turns)
     tiles, refs = refs[:2], refs[2:]
     grads, refs = refs[:n], refs[n:]
     slots, refs = refs[:2], refs[2:]
@@ -891,9 +834,9 @@
             accs[i],
             recvs[5 * i : 5 * i + 5],
             (local_sem.at[i], send_sem.at[i], recv_sem.at[i]),
-            (SUM_ORDERS[i % 3], BACK_ORDERS[i % 3]),
+            (SUM_ORDERS[turns[i][0]], BACK_ORDERS[turns[i][0]]),
         )
-        jobs.append((delays[i], steps, start, wait))
+        jobs.append((turns[i][1], steps, start, wait))
     pipeline(jobs)
     for i in range(2):
         to_tiles_wait(tiles[i], slots[i], tile_send.at[i], tile_recv.at[i], sizes)
@@ -910,11 +853,11 @@
     accs = [pltpu.VMEM(g.shape[:-1] + (g.shape[-1] // 2,), jnp.bfloat16) for g in cut]
     recvs = [
         pltpu.VMEM(shape, jnp.bfloat16)
-        for i, g in enumerate(cut)
-        for shape in recv_shapes(g.shape, SUM_ORDERS[i % 3])
+        for g in cut
+        for shape in recv_shapes(g.shape)
     ]
     outs = pl.pallas_call(
-        functools.partial(out_kernel, sizes, n, [i // 2 for i in range(n)]),
+        functools.partial(out_kernel, sizes, [TURNS[name] for name in names]),
         out_shape=[
             jax.ShapeDtypeStruct((slots,) + tile.shape[1:], tile.dtype) for tile in tiles
         ]
@@ -944,11 +887,11 @@
 SCALE = HEAD_DIM**-0.5
 
 
-def attend_kernel(q_ref, k_ref, v_ref, o_ref, log_ref):
+def attend_pair(q, k, v):
     lane = lax.broadcasted_iota(jnp.int32, (1, 128), 1)
     sub = lax.broadcasted_iota(jnp.int32, (128, 1), 0)
-    k, v, q = k_ref[...], v_ref[...], q_ref[...]
     out = jnp.zeros((128, q.shape[0]), jnp.float32)
+    logs = []
     for h in range(2):
         mine = (lane >= 64) == (h == 1)
         scores = lax.dot_general(
@@ -961,8 +904,8 @@
             v, e.astype(jnp.bfloat16), (((0,), (0,)), ((), ())), preferred_element_type=jnp.float32
         )
         out = jnp.where((sub >= 64) == (h == 1), part / total, out)
-        log_ref[0, h : h + 1, :] = top + jnp.log2(total)
-    o_ref[...] = out.T
+        logs.append(top + jnp.log2(total))
+    return out.T, logs
 
 
 def attend_back_kernel(q_ref, k_ref, v_ref, o_ref, log_ref, g_ref, dq_ref, dk_ref, dv_ref):
@@ -1001,22 +944,6 @@
     return pl.BlockSpec((rows, 128), lambda i: (0, i))
 
 
-def attend(q, k, v):
-    rows, width = q.shape
-    logs = pl.BlockSpec((1, 2, rows), lambda i: (i, 0, 0))
-    return pl.pallas_call(
-        attend_kernel,
-        grid=(width // 128,),
-        in_specs=[pair_block(rows), pair_block(k.shape[0]), pair_block(k.shape[0])],
-        out_specs=[pair_block(rows), logs],
-        out_shape=[
-            jax.ShapeDtypeStruct((rows, width), jnp.float32),
-            jax.ShapeDtypeStruct((width // 128, 2, rows), jnp.float32),
-        ],
-        compiler_params=pltpu.CompilerParams(vmem_limit_bytes=VMEM_LIMIT),
-    )(q, k, v)
-
-
 def attend_back(q, k, v, o, logs, g):
     rows, width = q.shape
     keys = k.shape[0]
@@ -1064,17 +991,9 @@
     dst[dst.shape[0] - cols :, :] = zero
 
 
-def project_kernel(tiles, cols, token_ref, w_ref, out_ref, scratch):
-    tile_rows, tile_cols = tiles
-    core = place()[2]
-    scratch[...] = jnp.dot(token_ref[...], w_ref[...], preferred_element_type=jnp.float32)
-    for r in range(2 * tile_rows):
-        row = turned(core, r, 2 * tile_rows - 1)
-        for z in range(cols):
-            at = ((r // tile_rows) * cols + z) * tile_rows + r % tile_rows
-            out_ref[block(row * cols + z, tile_cols), :] = scratch[
-                at * tile_cols : (at + 1) * tile_cols, :
-            ]
+def taps(w_ref, line):
+    value = w_ref[pl.ds(line * 3, 3)]
+    return value.reshape(3 * value.shape[1], value.shape[2])
 
 
 def conv_rows(src, w_ref, first, core, cols):
@@ -1083,22 +1002,14 @@
     for a in range(3):
         total = total + jnp.dot(
             src[a * cols : a * cols + rows, :],
-            w_ref[first + turned(core, a, 2)],
+            taps(w_ref, first + turned(core, a, 2)),
             preferred_element_type=jnp.float32,
         )
     return total
 
 
-def maps_kernel(
-    cols, f_ref, beyond_ref, w_ref, f0_ref, first0_ref, f1_ref, first1_ref, out_ref, wide
-):
+def maps_forward(cols, own, f0_ref, first0_ref, f1_ref, first1_ref, w_ref, out_ref, wide):
     core = place()[2]
-    own = f_ref.shape[0]
-    f0_ref[0:own, :] = f_ref[...]
-    for i in range(HALO):
-        f0_ref[own + i * cols : own + (i + 1) * cols, :] = beyond_ref[
-            (HALO - 1 - i) * cols : (HALO - i) * cols, :
-        ]
     clear_ends(wide, cols)
     for unit, (f, first, after) in enumerate(
         ((f0_ref, first0_ref, f1_ref), (f1_ref, first1_ref, None))
@@ -1128,7 +1039,7 @@
     rows, feat = src.shape[0] - 2 * cols, w_ref.shape[2]
     total = 0.0
     for a in range(3):
-        tap = w_ref[first + turned(core, 2 - a, 2)]
+        tap = taps(w_ref, first + turned(core, 2 - a, 2))
         for b in range(3):
             total = total + back_product(
                 src[a * cols : a * cols + rows, b * feat : (b + 1) * feat],
@@ -1222,27 +1133,6 @@
     )(*inputs)
 
 
-def project(tokens_low, w_proj, tiles, cols):
-    shape = (tokens_low.shape[0], w_proj.shape[1])
-    return plain_call(
-        functools.partial(project_kernel, tiles, cols),
-        (tokens_low, w_proj),
-        [jax.ShapeDtypeStruct(shape, jnp.float32)],
-        [pltpu.VMEM(shape, jnp.float32)],
-    )[0]
-
-
-def maps_forward(feature, beyond, w_conv, line):
-    rows, feat = feature.shape
-    ext = jax.ShapeDtypeStruct((rows + HALO * line, feat), jnp.float32)
-    return plain_call(
-        functools.partial(maps_kernel, line),
-        (feature, beyond, w_conv),
-        [ext] * 4 + [jax.ShapeDtypeStruct((rows + 2 * line, feat), jnp.bfloat16)],
-        [pltpu.VMEM((rows + (HALO + 2) * line, 3 * feat), jnp.bfloat16)],
-    )
-
-
 def maps_backward(tall, far, saved, w_conv, tiles, cols):
     rows, feat = saved[0].shape
     line = cols * tiles[1]
@@ -1251,11 +1141,313 @@
         functools.partial(maps_back_kernel, tiles, cols),
         (tall, far, *saved, w_conv),
         [
-            jax.ShapeDtypeStruct(w_conv.shape, jnp.bfloat16),
+            jax.ShapeDtypeStruct((12, 3 * feat, feat), jnp.bfloat16),
             jax.ShapeDtypeStruct((own, feat), jnp.bfloat16),
         ],
         [pltpu.VMEM((rows + 2 * line, 3 * feat), jnp.bfloat16)] * 2
         + [pltpu.VMEM((rows, feat), jnp.float32), pltpu.VMEM((own, feat), jnp.float32)],
+    )
+
+
+WEIGHTS = ("qkv", "out", "fc1", "fc2", "proj", "conv")
+GATHER_ORDERS = (("z1", "y"), ("y", "z1"), ("z1", "y"), ("y", "z1"), ("z1", "y"), ("y", "z1"))
+VECTORS = ("fc1_b", "fc2_b", "ln1_gain", "ln1_bias", "ln2_gain", "ln2_bias")
+SAVED = ("x", "q", "k", "v", "o", "logs", "after_attn", "hidden", "tokens_low")
+MAPS = ("f0", "first0", "f1", "first1", "coarse")
+STAGES = 4
+
+
+def chunks_of(name, master, whole, dp):
+    if name == "conv":
+        half = master.shape[1]
+        rows = pl.ds(pl.multiple_of(dp * half, 16), half)
+        return [(master.at[t], whole.at[t, rows]) for t in range(master.shape[0])]
+    half, width = master.shape
+    step = half if width > 1024 or half <= 512 else 384
+    wide = min(width, 768)
+    out = []
+    for r in range(0, half, step):
+        for c in range(0, width, wide):
+            rows = pl.ds(pl.multiple_of(dp * half + r, 16), step)
+            out.append((master.at[pl.ds(r, step), pl.ds(c, wide)], whole.at[rows, pl.ds(c, wide)]))
+    return out
+
+
+def forward_kernel(sizes, tiles, *refs):
+    chips, slots, cols = sizes
+    tile_rows, tile_cols = tiles
+    refs = list(refs)
+
+    def take(names):
+        taken = {name: refs.pop(0) for name in names}
+        return taken
+
+    tile_in = take(("tokens", "cots", "patches"))
+    masters = take(WEIGHTS)
+    vectors = take(VECTORS)
+    flag = refs.pop(0)
+    image_out = take(("cots", "patches"))
+    whole_out = take(WEIGHTS)
+    vector_out = take(VECTORS)
+    saved = take(SAVED)
+    maps = take(MAPS)
+    image = refs.pop(0)
+    whole = take(WEIGHTS)
+    far_vectors = take(VECTORS)
+    keys, values, f0, hidden_low, flat, wide, stage = (refs.pop(0) for _ in range(7))
+    tile_send, tile_recv, gather_send, gather_recv, vec_send, vec_recv, stage_sem, core_sem, out_sem = refs
+    dp, y, core, z = place()
+    low, f32 = jnp.bfloat16, jnp.float32
+
+    to_images_start(tile_in["tokens"], image, tile_send.at[0], tile_recv.at[0], sizes)
+    vector_copies = []
+    for i, name in enumerate(VECTORS):
+        copy = send(
+            vectors[name], far_vectors[name], vec_send.at[i], vec_recv.at[i], *mate("dp")
+        )
+        copy.start()
+        vector_copies.append(copy)
+
+    work = [(name, c) for name in WEIGHTS for c in chunks_of(name, masters[name], whole[name], dp)]
+    incoming = {}
+
+    def fetch(i):
+        if i < len(work):
+            source = work[i][1][0]
+            slot = stage.at[i % STAGES, pl.ds(0, source.shape[0]), pl.ds(0, source.shape[1])]
+            incoming[i] = pltpu.make_async_copy(source, slot, stage_sem.at[i % STAGES])
+            incoming[i].start()
+
+    gathers = {
+        name: Gather(whole[name], gather_send.at[i], gather_recv.at[i], GATHER_ORDERS[i])
+        for i, name in enumerate(WEIGHTS)
+    }
+    begun = []
+    done = [0]
+    for i in range(STAGES - 1):
+        fetch(i)
+
+    def round_next(name):
+        while done[0] < len(work) and work[done[0]][0] == name:
+            i = done[0]
+            fetch(i + STAGES - 1)
+            incoming.pop(i).wait()
+            target = work[i][1][1]
+            target[...] = stage[i % STAGES, : target.shape[0], : target.shape[1]].astype(low)
+            done[0] += 1
+        gathers[name].tick()
+        begun.append(gathers[name])
+
+    def tick():
+        for gather in begun:
+            gather.tick()
+
+    out_copies = []
+
+    def keep(src, dst):
+        copy = pltpu.make_async_copy(src, dst, out_sem.at[len(out_copies)])
+        copy.start()
+        out_copies.append(copy)
+
+    round_next("qkv")
+    round_next("out")
+    round_next("fc1")
+    tick()
+    round_next("fc2")
+    tick()
+    round_next("proj")
+    gathers["qkv"].tick()
+    gathers["out"].tick()
+    round_next("conv")
+    gathers["qkv"].finish()
+    for copy in vector_copies:
+        copy.wait()
+    vec = {}
+    for name in VECTORS:
+        own, far = vectors[name][...], far_vectors[name][...]
+        row = jnp.concatenate(
+            [jnp.where(dp == 0, own, far), jnp.where(dp == 0, far, own)], axis=1
+        )
+        vec[name] = row.astype(low).astype(f32)
+        vector_out[name][...] = vec[name]
+    to_images_wait(tile_in["tokens"], image, tile_send.at[0], tile_recv.at[0], sizes)
+    to_images_start(tile_in["patches"], image_out["patches"], tile_send.at[1], tile_recv.at[1], sizes)
+    to_images_start(tile_in["cots"], image_out["cots"], tile_send.at[2], tile_recv.at[2], sizes)
+
+    width = image.shape[3]
+    x = jnp.where(flag[0:1, 0:1] > 0, image[1].astype(f32), image[0].astype(f32))
+    x = x.reshape(-1, width)
+    rows = x.shape[0]
+    saved["x"][...] = x.astype(low)
+    normed = norm_rows(x, vec["ln1_gain"], vec["ln1_bias"])[0].astype(low)
+    mine = pl.ds(0, rows)
+    theirs = pl.ds(rows, rows)
+    core_copies = []
+    for i, ref in ((1, keys), (2, values), (0, None)):
+        part = jnp.dot(
+            normed, whole["qkv"][:, i * width : (i + 1) * width], preferred_element_type=f32
+        ).astype(low)
+        if ref is None:
+            saved["q"][...] = part
+        else:
+            ref[mine, :] = part
+            copy = send(
+                ref.at[mine], ref.at[theirs], core_sem.at[0, i], core_sem.at[1, i], *mate("core")
+            )
+            copy.start()
+            core_copies.append(copy)
+    tick()
+    for copy in core_copies:
+        copy.wait()
+    keep(keys, saved["k"])
+    keep(values, saved["v"])
+    for name in ("qkv",):
+        keep(whole[name], whole_out[name])
+
+    for pair in range(width // 128):
+        lanes = pl.ds(pair * 128, 128)
+        out, logs = attend_pair(saved["q"][:, lanes], keys[:, lanes], values[:, lanes])
+        saved["o"][:, lanes] = out
+        for h in range(2):
+            saved["logs"][pair, h : h + 1, :] = logs[h]
+        if pair % 2 == 1:
+            tick()
+    gathers["out"].finish()
+    after_attn = saved["x"][...].astype(f32) + jnp.dot(
+        saved["o"][...].astype(low), whole["out"][...], preferred_element_type=f32
+    )
+    saved["after_attn"][...] = after_attn
+    normed_two = norm_rows(after_attn, vec["ln2_gain"], vec["ln2_bias"])[0].astype(low)
+    gathers["fc1"].finish()
+    for c in range(0, hidden_low.shape[1], width):
+        part = pl.ds(c, width)
+        hidden = jnp.dot(normed_two, whole["fc1"][:, part], preferred_element_type=f32)
+        hidden = hidden + vec["fc1_b"][:, c : c + width]
+        saved["hidden"][:, part] = hidden
+        hidden_low[:, part] = jax.nn.gelu(hidden).astype(low)
+    gathers["fc2"].finish()
+    after_mlp = saved["after_attn"][...] + (
+        jnp.dot(hidden_low[...], whole["fc2"][...], preferred_element_type=f32) + vec["fc2_b"]
+    )
+    tokens_low = after_mlp.astype(low)
+    saved["tokens_low"][...] = tokens_low
+    gathers["proj"].finish()
+
+    flat[...] = jnp.dot(tokens_low, whole["proj"][...], preferred_element_type=f32)
+    half_rows, line = 2 * tile_rows, cols * tile_cols
+    for r in range(half_rows):
+        row = turned(core, r, half_rows - 1)
+        for zz in range(cols):
+            at = ((r // tile_rows) * cols + zz) * tile_rows + r % tile_rows
+            f0[block(row * cols + zz, tile_cols), :] = flat[at * tile_cols : (at + 1) * tile_cols, :]
+    core_copies = []
+    for i in range(HALO):
+        copy = send(
+            f0.at[pl.ds((half_rows - 1 - i) * line, line)],
+            f0.at[pl.ds((half_rows + i) * line, line)],
+            core_sem.at[0, 3 + i],
+            core_sem.at[1, 3 + i],
+            *mate("core"),
+        )
+        copy.start()
+        core_copies.append(copy)
+    gathers["conv"].finish()
+    for copy in core_copies:
+        copy.wait()
+    for name in WEIGHTS[1:]:
+        keep(whole[name], whole_out[name])
+    keep(f0, maps["f0"])
+    maps_forward(
+        line, rows, f0, maps["first0"], maps["f1"], maps["first1"], whole["conv"], maps["coarse"], wide
+    )
+    for copy in out_copies:
+        copy.wait()
+    to_images_wait(
+        tile_in["patches"], image_out["patches"], tile_send.at[1], tile_recv.at[1], sizes
+    )
+    to_images_wait(tile_in["cots"], image_out["cots"], tile_send.at[2], tile_recv.at[2], sizes)
+
+
+def run_forward(tile_in, masters, vectors, flag, sizes, tiles):
+    chips, slots, cols = sizes
+    low, f32 = jnp.bfloat16, jnp.float32
+    shape = jax.ShapeDtypeStruct
+    tile, width = tile_in[0].shape[1:]
+    feat = masters["proj"].shape[1]
+    hidden = masters["fc1"].shape[1]
+    rows, line = chips * tile, cols * tiles[1]
+    ext = rows + HALO * line
+    wholes = {
+        name: shape(m.shape[:-2] + (2 * m.shape[-2], m.shape[-1]), low) for name, m in masters.items()
+    }
+    saved = {
+        "x": shape((rows, width), low),
+        "q": shape((rows, width), low),
+        "k": shape((2 * rows, width), low),
+        "v": shape((2 * rows, width), low),
+        "o": shape((rows, width), f32),
+        "logs": shape((width // 128, 2, rows), f32),
+        "after_attn": shape((rows, width), f32),
+        "hidden": shape((rows, hidden), f32),
+        "tokens_low": shape((rows, width), low),
+    }
+    maps = {name: shape((ext, feat), f32) for name in MAPS[:-1]}
+    maps["coarse"] = shape((rows + 2 * line, feat), low)
+    far = [shape((2, chips) + t.shape[1:], t.dtype) for t in tile_in]
+    hbm, vmem = pl.BlockSpec(memory_space=pltpu.HBM), pl.BlockSpec(memory_space=pltpu.VMEM)
+    out_shape = (
+        far[1:]
+        + [wholes[name] for name in WEIGHTS]
+        + [shape((1, 2 * vectors[name].shape[1]), f32) for name in VECTORS]
+        + [saved[name] for name in SAVED]
+        + [maps[name] for name in MAPS]
+    )
+    out_specs = (
+        [hbm] * (2 + len(WEIGHTS))
+        + [vmem] * len(VECTORS)
+        + [hbm if name in ("k", "v") else vmem for name in SAVED]
+        + [hbm if name == "f0" else vmem for name in MAPS]
+    )
+    n = len(WEIGHTS)
+    outs = pl.pallas_call(
+        functools.partial(forward_kernel, sizes, tiles),
+        out_shape=out_shape,
+        in_specs=[hbm] * (3 + n) + [vmem] * (len(VECTORS) + 1),
+        out_specs=out_specs,
+        scratch_shapes=[pltpu.VMEM(far[0].shape, low)]
+        + [pltpu.VMEM(wholes[name].shape, low) for name in WEIGHTS]
+        + [pltpu.VMEM(vectors[name].shape, f32) for name in VECTORS]
+        + [
+            pltpu.VMEM((2 * rows, width), low),
+            pltpu.VMEM((2 * rows, width), low),
+            pltpu.VMEM((ext, feat), f32),
+            pltpu.VMEM((rows, hidden), low),
+            pltpu.VMEM((rows, feat), f32),
+            pltpu.VMEM((ext + 2 * line, 3 * feat), low),
+            pltpu.VMEM((STAGES, 384, 768), f32),
+            pltpu.SemaphoreType.DMA((3, slots)),
+            pltpu.SemaphoreType.DMA((3, 2 * chips)),
+            pltpu.SemaphoreType.DMA((n, 4)),
+            pltpu.SemaphoreType.DMA((n, 4)),
+            pltpu.SemaphoreType.DMA((len(VECTORS),)),
+            pltpu.SemaphoreType.DMA((len(VECTORS),)),
+            pltpu.SemaphoreType.DMA((STAGES,)),
+            pltpu.SemaphoreType.DMA((2, 3 + HALO)),
+            pltpu.SemaphoreType.DMA((n + 3,)),
+        ],
+        compiler_params=pltpu.CompilerParams(
+            has_side_effects=True, vmem_limit_bytes=VMEM_LIMIT
+        ),
+    )(
+        *tile_in,
+        *(masters[name] for name in WEIGHTS),
+        *(vectors[name] for name in VECTORS),
+        flag,
+    )
+    outs = list(outs)
+    images = [outs.pop(0) for _ in range(2)]
+    return (images,) + tuple(
+        {name: outs.pop(0) for name in names} for names in (WEIGHTS, VECTORS, SAVED, MAPS)
     )
 
 
@@ -1316,18 +1508,15 @@
         jnp.logical_or(jnp.logical_or(full_group, borrowed), chip < count), 1.0, 0.0
     )
 
-    vectors = (fc1_b, fc2_b, ln1_gain, ln1_bias, ln2_gain, ln2_bias, head_b, shift_row)
-    lengths = [v.shape[0] for v in vectors]
-    own_small = jnp.concatenate([v.astype(low) for v in vectors] + [head_w.astype(low).reshape(-1)])
-    far_small = lax.ppermute(own_small, "dp", [(0, 1), (1, 0)])
-    lower = jnp.where(dp == 0, own_small, far_small).astype(jnp.float32)
-    upper = jnp.where(dp == 0, far_small, own_small).astype(jnp.float32)
-    small, at = [], 0
-    for length in lengths:
-        small.append(jnp.concatenate([lower[at : at + length], upper[at : at + length]]))
-        at += length
-    b_up, b_down, gain_one, bias_one, gain_two, bias_two, b_head, w_shift = small
-    w_head = jnp.concatenate([lower[at:], upper[at:]]).reshape(feat, feat).astype(low)
+    def both_halves(value):
+        far = lax.ppermute(value, "dp", [(0, 1), (1, 0)])
+        return jnp.where(dp == 0, jnp.stack([value, far]), jnp.stack([far, value]))
+
+    w_head = both_halves(head_w.astype(low)).reshape(feat, feat)
+    rows_small = both_halves(jnp.stack([head_b, shift_row]))
+    b_head, w_shift = (
+        rows_small[:, i].reshape(-1).astype(low).astype(jnp.float32) for i in range(2)
+    )
 
     merged_grad = cot_merged.astype(jnp.float32).reshape(slots, -1, feat) * present[:, None, None]
     grad_shift = jnp.sum(merged_grad * shift_sign[:, None, None], (0, 1))
@@ -1340,55 +1529,33 @@
         patch_grad.reshape(slots, cells, feat), ((0, 0), (0, PATCH - cells), (0, 0))
     )
 
-    halves = {
-        "qkv": qkv_w[None],
-        "out": attn_out_w[None],
-        "fc1": fc1_w[None],
-        "fc2": fc2_w[None],
-        "conv": conv_w.reshape((36,) + conv_w.shape[3:]),
-        "proj": proj_w[None],
-    }
-    halves = {name: half.astype(low) for name, half in halves.items()}
-    (images, image_cots, image_patches), weights = bring_in(
+    vectors = (fc1_b, fc2_b, ln1_gain, ln1_bias, ln2_gain, ln2_bias)
+    (image_cots, image_patches), weights, vec, saved, maps = run_forward(
         (tokens.reshape(slots, tile, width), cot_tokens.reshape(slots, tile, width), patch_grad),
-        halves,
+        {
+            "qkv": qkv_w,
+            "out": attn_out_w,
+            "fc1": fc1_w,
+            "fc2": fc2_w,
+            "proj": proj_w,
+            "conv": conv_w.reshape((36,) + conv_w.shape[3:]),
+        },
+        {name: v[None] for name, v in zip(VECTORS, vectors)},
+        jnp.full((8, 128), borrowed.astype(jnp.float32)),
         sizes,
-    )
-    w_qkv, w_out, w_up, w_down, w_proj = (
-        weights[name][0] for name in ("qkv", "out", "fc1", "fc2", "proj")
-    )
-    w_conv = weights["conv"].reshape(12, 3 * feat, feat)
+        (tile_rows, tile_cols),
+    )
+    w_qkv, w_out, w_up, w_down, w_proj, w_conv = (weights[name] for name in WEIGHTS)
+    gain_one, bias_one, gain_two, bias_two = (vec[name] for name in VECTORS[2:])
 
     def chosen(pair):
         return jnp.where(borrowed, pair[1], pair[0])
 
-    stream = chosen(images).reshape(-1, width).astype(jnp.float32)
-    rows = stream.shape[0]
-
-    normed, scaled_one, factor_one = norm_rows(stream, gain_one, bias_one)
-    normed_low = normed.astype(low)
-    projected = jnp.dot(normed_low, w_qkv, preferred_element_type=jnp.float32).astype(low)
-    queries, pair_own = projected[:, :width], projected[:, width:]
-    pair_far = swap_cores(pair_own)
-    keys = jnp.concatenate([pair_own[:, :width], pair_far[:, :width]])
-    values = jnp.concatenate([pair_own[:, width:], pair_far[:, width:]])
-    attended_wide, logs = attend(queries, keys, values)
-    attended = attended_wide.astype(low)
-    after_attn = stream + jnp.dot(attended, w_out, preferred_element_type=jnp.float32)
-    normed_two, scaled_two, factor_two = norm_rows(after_attn, gain_two, bias_two)
-    normed_two_low = normed_two.astype(low)
-    hidden = jnp.dot(normed_two_low, w_up, preferred_element_type=jnp.float32) + b_up
-    hidden_low = jax.nn.gelu(hidden).astype(low)
-    after_mlp = after_attn + (
-        jnp.dot(hidden_low, w_down, preferred_element_type=jnp.float32) + b_down
-    )
-    tokens_low = after_mlp.astype(low)
+    rows = chips * tile
     tiles = (tile_rows, tile_cols)
-    feature = project(tokens_low, w_proj, tiles, cols)
-    beyond = swap_cores(feature[(half_rows - HALO) * all_cols :])
-    *saved, coarse = maps_forward(feature, beyond, w_conv, all_cols)
-
-    coarse = coarse.reshape(half_rows + 2, all_cols, feat)
+    tokens_low = saved["tokens_low"]
+
+    coarse = maps["coarse"].reshape(half_rows + 2, all_cols, feat)
     coarse = jnp.concatenate([coarse[:, :1], coarse, coarse[:, -1:]], 1)
     cuts = [
         coarse[
@@ -1424,9 +1591,18 @@
         wide[1], ((tile_rows, 0), (0, 0), (0, 0))
     )
     tall = tall.reshape(-1, feat)
-    grad_conv, proj_grad = maps_backward(tall, swap_cores(tall), saved, w_conv, tiles, cols)
+    grad_conv, proj_grad = maps_backward(
+        tall, swap_cores(tall), [maps[name] for name in MAPS[:-1]], w_conv, tiles, cols
+    )
     grad_conv = grad_conv.reshape(36, feat, feat)
 
+    normed, scaled_one, factor_one = norm_rows(saved["x"].astype(jnp.float32), gain_one, bias_one)
+    normed_low = normed.astype(low)
+    normed_two, scaled_two, factor_two = norm_rows(saved["after_attn"], gain_two, bias_two)
+    normed_two_low = normed_two.astype(low)
+    hidden = saved["hidden"]
+    hidden_low = jax.nn.gelu(hidden).astype(low)
+    attended = saved["o"].astype(low)
     grad_proj = outer_product(tokens_low, proj_grad)
     stream_grad = chosen(image_cots).reshape(rows, width).astype(jnp.float32)
     stream_grad = jnp.where(image_present > 0, stream_grad, 0.0) + back_product(proj_grad, w_proj)
@@ -1444,7 +1620,7 @@
     grad_out_w = outer_product(attended, branch_grad)
     attended_grad = back_product(branch_grad, w_out).astype(low)
     query_grad, key_grad, value_grad = attend_back(
-        queries, keys, values, attended_wide, logs, attended_grad
+        *(saved[name] for name in ("q", "k", "v", "o", "logs")), attended_grad
     )
     pair_grad = jnp.concatenate([key_grad, value_grad], 1)
     pair_grad = pair_grad[:rows] + swap_cores(pair_grad[rows:].astype(low)).astype(jnp.float32)
@@ -1489,7 +1665,7 @@
     sums = {name: value.astype(jnp.float32) for name, value in sums.items()}
     packed = sums["small"].reshape(-1)
     pieces, at = [], 0
-    for length in lengths:
+    for length in (v.shape[0] for v in vectors + (head_b, shift_row)):
         pieces.append(packed[at : at + length])
         at += length
     return (

time: 798 us -> 571 us (0.72)
  Pallas kernels: 613 us -> 429 us
  other arithmetic: 65.1 us -> 47.2 us
  matrix products: 61.6 us -> 45.6 us
    pallas_call x3 -> x2, Pallas kernels: 533 us -> 353 us  [the longest x1 217 us: bring_out(): pl.pallas_call(functools.partial(out_kernel, sizes, [TURNS[name] for name...]
    convert_element_type x16 -> x2, other arithmetic: 22.3 us -> 1.48 us  [the longest x1 0.91 us: on_chip(): w_head = both_halves(head_w.astype(low)).reshape(feat, feat)]
    dot_general x4 -> x0, matrix products: 15.1 us -> none  [the longest x1 5.65 us: on_chip(): jnp.dot(normed_two_low, w_up, preferred_element_type=jnp.float32) + b_up]
    pallas_call x3 -> x1, Pallas kernels: 33.4 us -> 19.1 us  [plain_call(): pl.pallas_call(kernel, out_shape=out_shape, in_specs=in_vmem(len(inputs))...]
    pallas_call x1, Pallas kernels: 27.9 us -> 38.7 us  [patches_out(): pl.pallas_call(functools.partial(patch_kernel, sizes), out_shape=jax.Shap...]
  transfers between devices with their start and end apart: 5 -> 4, of which waited for: 2 -> 0; matrix products, arithmetic and copies ran while one was open for 7% -> 5% of each run, Pallas kernels for 4% -> 0%
where the time goes in v2:
time: 571 us; the launch traced here: 567 us
  Pallas kernels  429 us (75%)
  other arithmetic  47.2 us (8%)
  matrix products  45.6 us (8%)
  local copies, waits for them, and re-layouts  36.2 us (6%)
    pallas_call x1, Pallas kernels, bring_out(): pl.pallas_call(functools.partial(out_kernel, sizes, [TURNS[name] for name...  217 us
    pallas_call x1, Pallas kernels, run_forward(): pl.pallas_call(functools.partial(forward_kernel, sizes, tiles), out_shape...  135 us
    pallas_call x1, Pallas kernels, patches_out(): pl.pallas_call(functools.partial(patch_kernel, sizes), out_shape=jax.Shap...  38.7 us
    dot_general x6, matrix products, back_product(): lax.dot_general(first_op, weight, (((1,), (1,)), ((), ())), preferred_ele...  25.2 us
    dot_general x6, matrix products, outer_product(): lax.dot_general(first_op, second_op, (((0,), (0,)), ((), ())), preferred_...  20 us
    pallas_call x1, Pallas kernels, plain_call(): pl.pallas_call(kernel, out_shape=out_shape, in_specs=in_vmem(len(inputs))...  19.1 us
    pallas_call x1, Pallas kernels, attend_back(): pl.pallas_call(attend_back_kernel, grid=(width // 128,), in_specs=[own, b...  19 us
    convert_element_type x8, other arithmetic, on_chip(): sums = {name: value.astype(jnp.float32) for name, value in sums.items()}  14.1 us
  transfers between devices with their start and end apart: 4, of which 0 were waited for; matrix products, arithmetic and copies ran while one was open for 5% of the time, Pallas kernels for 0%

profile of v2, /device:TPU:0, one launch (start us, length us, event | category | flops | bytes accessed | tf_op | source)
XLA Modules:
  0.0 566.8 jit_solution(1289208174423126956)
XLA Ops:
  1.4 2.9 collective-permute-start.3
  4.4 0.9 convert_element_type.276
  6.0 0.9 convert_bitcast_fusion.1
  8.7 1.2 broadcast_in_dim.87.refs_10_
  10.0 2.5 fusion.77
  20.2 0.9 pad.40.refs_2_
  21.6 135.4 %shard_map.340 = (bf16[2,8,64,768]{3,2,1,0:T(8,128)(2,1)}, bf16[2,8,112,256]{3,2,1,0:T(8,128)(2,1)}, bf16[768,2304]{1,0:T(8,128)(2,1)}, bf16[768,768]{1,0:T(8,12...) custom-call(bf16[10,64,768]{2,1,0:T(8,128)(2,1)} %bitcast.171, ...), custom_call_target="tpu_custom_call" | custom-call | tf_op jit(solution)/shard_map/pallas_call | solution.py:1412
  157.0 1.2 select_bitcast_fusion.2
  160.2 0.8 copy-done
  167.2 38.7 %shard_map.343 = bf16[10,112,256]{2,1,0:T(8,128)(2,1)} custom-call(bf16[8,112,256]{2,1,0:T(8,128)(2,1)} %pad.47.src), custom_call_target="tpu_custom_call" | custom-call | tf_op jit(solution)/shard_map/pallas_call | solution.py:704
  207.9 1.0 slice_convert_fusion.1
  209.0 1.3 reshape.383
  210.4 1.4 fusion.22
  212.1 2.4 copy.60
  214.6 2.4 reshape.368
  217.5 2.4 copy.61
  219.9 3.6 convert_element_type.301
  223.6 2.3 collective-permute-start.1
  226.0 1.6 convert_select_fusion
  228.9 1.9 multiply_convert_fusion.2
  230.8 1.2 fusion.42
  232.9 19.1 %shard_map.341 = (bf16[12,768,256]{2,1,0:T(8,128)(2,1)}, bf16[512,256]{1,0:T(8,128)(2,1)}) custom-call(f32[576,256]{1,0:T(8,128)} %bitcast.155, f32[576,256]{1,0:T(8,128)} %copy-done.26, f32[704,256]{1,0:T(8,128)} %get-tuple-element.62.f0_ref, f32[704,256]{1,0:T(8,128)} %get-tuple-element.63.first0_ref, f32[704,256]{1,0:T(8,128)} %get-tuple-element.64.f1_ref, ...), custom_call_target="tpu_custom_call" | custom-call | tf_op jit(solution)/shard_map/pallas_call | solution.py:1126
  251.9 1.5 convert_reduce_fusion.1
  253.6 10.6 %fusion.83 = (bf16[3072]{0:T(1024)(128)(2,1)S(1)}, bf16[512,3072]{1,0:T(8,128)(2,1)}) fusion(f32[512,3072]{1,0:T(8,128)} %get-tuple-element.71, bf16[3072,768]{1,0:T(8,128)(2,1)} %get-tuple-element.70, f32[512,768]{1,0:T(8,128)S(1)} %get-tuple-element.158), kind=kOutput, calls=%fused_computation.187 | convolution fusion | flops 2449339392 | bytes 15734784 | tf_op jit(solution)/shard_map/dot_general | solution.py:59
  264.2 7.4 %multiply_reduce_fusion.1 = (bf16[768]{0:T(1024)(128)(2,1)S(1)}, f32[512]{0:T(512)S(1)}, f32[512]{0:T(512)S(1)}, bf16[768]{0:T(1024)(128)(2,1)S(1)}, f32[512,768]{1,0:T(8,128)}) fusion(f32[512,768]{1,0:T(8,128)S(1)} %copy-done, f32[512]{0:T(512)S(1)} %copy-done.39, f32[512]{0:T(512)S(1)} %copy-done.35, f32[768]{0:T(1024)S(1)} %copy-done.37, ...), kind=kOutput, calls=%fused_computation.59 | convolution fusion | flops 2419455488 | bytes 11024384 | tf_op jit(solution)/shard_map/dot_general | solution.py:59
  271.7 1.2 convolution_convert_fusion.6
  273.0 2.0 multiply_add_fusion
  275.1 1.7 convolution_convert_fusion.5.g_ref
  276.8 1.9 convolution_convert_fusion.4
  278.6 19.0 %shard_map.342 = (f32[512,768]{1,0:T(8,128)}, f32[1024,768]{1,0:T(8,128)}, f32[1024,768]{1,0:T(8,128)}) custom-call(bf16[512,768]{1,0:T(8,128)(2,1)} %get-tuple-element.75.q_ref, bf16[1024,768]{1,0:T(8,128)(2,1)} %get-tuple-element.76.k_ref, bf16[1024,768]{1,0:T(8,128)(2,1)} %get-tuple-element.77.v_ref, f32[512,768]{1,0:T(8,128)} %get-tuple-element.78.o_ref, ...), custom_call_target="tpu_custom_call" | custom-call | tf_op jit(solution)/shard_map/pallas_call | solution.py:951
  297.6 1.5 convert.70
  299.1 2.6 constant_dynamic-update-slice_fusion.1
  303.1 1.0 copy-done.62
  304.1 4.9 convolution_convert_fusion.1
  309.1 5.1 convolution_convert_fusion.2
  315.3 1.7 copy-done.60
  317.0 3.4 fusion.30
  321.3 5.7 %convolution_convert_fusion = bf16[768,2304]{1,0:T(8,128)(2,1)} fusion(bf16[512,1536]{1,0:T(8,128)(2,1)} %copy-done.16, bf16[512,768]{1,0:T(8,128)(2,1)} %copy-done.25, bf16[512,768]{1,0:T(8,128)(2,1)S(1)} %copy-done.4, f32[768]{0:T(1024)S(1)} %copy-done.43, f32[768]{0:T(1024)S(1)} %copy-done.36, f32[512]{0:T(512)S(1)} %copy-done.38, f32[512]{0:T(512)S(1)} %copy-done.33), kind=kOutput, calls=%fused_computation.10 | convolution fusion | flops 1820786688 | bytes 6694912 | tf_op jit(solution)/shard_map/dot_general | solution.py:53
  327.0 1.4 fusion.27
  328.5 217.3 %shard_map.344 = (bf16[10,64,768]{2,1,0:T(8,128)(2,1)}, bf16[10,64,768]{2,1,0:T(8,128)(2,1)}, bf16[36,2,2,2,16,256]{5,4,3,2,1,0:T(8,128)(2,1)}, bf16[1,2,2,2,192...) custom-call(bf16[8,64,768]{2,1,0:T(8,128)(2,1)} %bitcast.173, ...), custom_call_target="tpu_custom_call" | custom-call | tf_op jit(solution)/shard_map/pallas_call | solution.py:859
  545.8 0.9 convert_element_type.338
  547.9 2.3 select_bitcast_fusion.1
  553.0 1.5 select_bitcast_fusion
  554.5 1.1 bitcast_convert_fusion.3
  555.6 2.1 bitcast_convert_fusion.2
  558.1 2.9 bitcast_convert_fusion.1
  561.1 2.7 bitcast_convert_fusion
  563.8 2.8 convert.93
  (241 shorter events, 31.6 us)
Async XLA Ops:
  0.7 11.8 %copy-start.51 = (f32[384]{0:T(512)S(1)}, f32[384]{0:T(512)}, u32[]{:S(2)}) copy-start(f32[384]{0:T(512)} %param.33) | copy-start | bytes 4612
  0.7 12.4 %copy-start.52 = (f32[384]{0:T(512)S(1)}, f32[384]{0:T(512)}, u32[]{:S(2)}) copy-start(f32[384]{0:T(512)} %param.34) | copy-start | bytes 4612
  0.7 12.9 %copy-start.53 = (f32[384]{0:T(512)S(1)}, f32[384]{0:T(512)}, u32[]{:S(2)}) copy-start(f32[384]{0:T(512)} %param.35) | copy-start | bytes 4612
  0.7 13.5 %copy-start.54 = (f32[384]{0:T(512)S(1)}, f32[384]{0:T(512)}, u32[]{:S(2)}) copy-start(f32[384]{0:T(512)} %param.36) | copy-start | bytes 4612
  0.7 14.1 %copy-start.40 = (f32[1536]{0:T(1024)S(1)}, f32[1536]{0:T(1024)}, u32[]{:S(2)}) copy-start(f32[1536]{0:T(1024)} %param.30) | copy-start | bytes 18436
  1.4 13.9 %collective-permute-start.3 = (bf16[2,128]{1,0:T(2,128)(2,1)S(1)}, bf16[2,128]{1,0:T(2,128)(2,1)S(1)}, u32[]{:S(2)}, u32[]{:S(2)}) collective-permute-start(bf16[2,128]{1,0:T(2,128)(2,1)S(1)} %get-tuple-element.150), channel_id=1, source_target_pairs={{0,16},{16,0},{1,17},{17,1},{2,18},{18,2},{3,19},{19,3},{4,20},{20... | collective-permute-start | bytes 1544 | tf_op jit(solution)/shard_map/ppermute | solution.py:1512
  5.3 10.7 %collective-permute-start = (bf16[128,256]{1,0:T(8,128)(2,1)S(1)}, bf16[128,256]{1,0:T(8,128)(2,1)S(1)}, u32[]{:S(2)}, u32[]{:S(2)}) collective-permute-start(bf16[128,256]{1,0:T(8,128)(2,1)S(1)} %convert_element_type.276), channel_id=1, source_target_pairs={{0,16},{16,0},{1,17},{17,1},{2,18},{18,2},{3,19},{19,3},{4,20},{20... | collective-permute-start | bytes 196616 | tf_op jit(solution)/shard_map/ppermute | solution.py:1512
  7.6 9.0 %copy-start.55 = (f32[10]{0:T(128)}, f32[10]{0:T(128)S(1)}, u32[]{:S(2)}) copy-start(f32[10]{0:T(128)S(1)} %multiply_add_fusion.1) | copy-start | bytes 124
  8.2 8.3 %copy-start.49 = (f32[10]{0:T(128)}, f32[10]{0:T(128)S(1)}, u32[]{:S(2)}) copy-start(f32[10]{0:T(128)S(1)} %convert_element_type.307) | copy-start | bytes 124
  8.7 7.9 %copy-start.57 = (f32[10]{0:T(128)}, f32[10]{0:T(128)S(1)}, u32[]{:S(2)}) copy-start(f32[10]{0:T(128)S(1)} %get-tuple-element.159) | copy-start | bytes 124
  12.5 3.6 copy-start.1
  161.2 2.7 copy-start.47
  161.3 3.3 copy-start.46
  161.3 3.9 copy-start.45
  161.3 4.5 copy-start.19
  162.4 3.9 copy-start.32
  219.9 3.7 copy-start.20
  223.6 4.6 copy-start.10
  223.6 4.0 copy-start.22
  223.6 4.0 copy-start.42
  223.6 8.4 %collective-permute-start.1 = (f32[576,256]{1,0:T(8,128)S(1)}, f32[576,256]{1,0:T(8,128)S(1)}, u32[]{:S(2)}, u32[]{:S(2)}) collective-permute-start(f32[576,256]{1,0:T(8,128)S(1)} %bitcast.154), channel_id=1, source_target_pairs={{0,4},{4,0},{8,12},{12,8},{1,5},{5,1},{9,13},{13,9},{2,6},{6,2},{1... | collective-permute-start | bytes 1769480 | tf_op jit(solution)/shard_map/ppermute | solution.py:1455
  232.9 19.1 %copy-start.28 = (bf16[768,256]{1,0:T(8,128)(2,1)S(1)}, bf16[768,256]{1,0:T(8,128)(2,1)}, u32[]{:S(2)}) copy-start(bf16[768,256]{1,0:T(8,128)(2,1)} %get-tuple-element.68) | copy-start | bytes 1179652
  253.5 10.6 %copy-start.6 = (f32[512,768]{1,0:T(8,128)}, f32[512,768]{1,0:T(8,128)S(1)}, u32[]{:S(2)}) copy-start(f32[512,768]{1,0:T(8,128)S(1)} %get-tuple-element.158) | copy-start | bytes 4718596
  253.5 10.6 %copy-start.35 = (f32[512]{0:T(512)S(1)}, f32[512]{0:T(512)}, u32[]{:S(2)}) copy-start(f32[512]{0:T(512)} %copy-done.34) | copy-start | bytes 6148
  253.5 10.6 %copy-start.37 = (f32[768]{0:T(1024)S(1)}, f32[768]{0:T(1024)}, u32[]{:S(2)}) copy-start(f32[768]{0:T(1024)} %reduce.5) | copy-start | bytes 9220
  253.5 10.6 %copy-start.39 = (f32[512]{0:T(512)S(1)}, f32[512]{0:T(512)}, u32[]{:S(2)}) copy-start(f32[512]{0:T(512)} %add_rsqrt_fusion.1) | copy-start | bytes 6148
  264.2 7.5 %copy-start.24 = (bf16[512,768]{1,0:T(8,128)(2,1)S(1)}, bf16[512,768]{1,0:T(8,128)(2,1)}, u32[]{:S(2)}) copy-start(bf16[512,768]{1,0:T(8,128)(2,1)} %get-tuple-element.59) | copy-start | bytes 2359300
  264.2 7.5 %copy-start.29 = (bf16[512,256]{1,0:T(8,128)(2,1)S(1)}, bf16[512,256]{1,0:T(8,128)(2,1)}, u32[]{:S(2)}) copy-start(bf16[512,256]{1,0:T(8,128)(2,1)} %get-tuple-element.67) | copy-start | bytes 786436
  299.1 15.6 %copy-start.25 = (bf16[512,768]{1,0:T(8,128)(2,1)}, bf16[512,768]{1,0:T(8,128)(2,1)S(1)}, u32[]{:S(2)}) copy-start(bf16[512,768]{1,0:T(8,128)(2,1)S(1)} %convert.70) | copy-start | bytes 2359300
  299.1 3.1 copy-start.9
  302.6 6.4 %slice-start = ((s8[6291456]{0:T(1024)(128)(4,1)}), s8[4194304]{0:T(1024)(128)(4,1)S(1)}, s32[]{:S(2)}) async-start(s8[6291456]{0:T(1024)(128)(4,1)} %bitcast.188), calls=%async_computation | async-start | bytes 8388608
  302.8 11.4 %collective-permute-start.2 = (bf16[512,1536]{1,0:T(8,128)(2,1)S(1)}, bf16[512,1536]{1,0:T(8,128)(2,1)S(1)}, u32[]{:S(2)}, u32[]{:S(2)}) collective-permute-start(bf16[512,1536]{1,0:T(8,128)(2,1)S(1)} %slice.300), channel_id=1, source_target_pairs={{0,4},{4,0},{8,12},{12,8},{1,5},{5,1},{9,13},{13,9},{2,6},{6,2},{1... | collective-permute-start | bytes 4718600 | tf_op jit(solution)/shard_map/ppermute | solution.py:1455
  304.1 5.0 copy-start.7
  304.1 5.0 slice-start.1
  314.2 2.8 copy-start.60
  314.7 5.8 %copy-start.16 = (bf16[512,1536]{1,0:T(8,128)(2,1)}, bf16[512,1536]{1,0:T(8,128)(2,1)S(1)}, u32[]{:S(2)}) copy-start(bf16[512,1536]{1,0:T(8,128)(2,1)S(1)} %fusion.7) | copy-start | bytes 4718596
  317.0 3.5 copy-start.59
  317.0 4.3 copy-start.43
  321.3 5.7 %copy-start.17 = (f32[512,768]{1,0:T(8,128)S(1)}, f32[512,768]{1,0:T(8,128)}, u32[]{:S(2)}) copy-start(f32[512,768]{1,0:T(8,128)} %get-tuple-element.154) | copy-start | bytes 4718596
  328.5 219.5 %copy-start.41 = (pred[10]{0:T(512)(128)(4,1)S(1)}, pred[10]{0:T(512)(128)(4,1)}, u32[]{:S(2)}) copy-start(pred[10]{0:T(512)(128)(4,1)} %get-tuple-element.160) | copy-start | bytes 34
  545.8 5.7 %copy-start.31 = (bf16[1,2,2,2,16,256]{5,4,3,2,1,0:T(8,128)(2,1)S(1)}, bf16[1,2,2,2,16,256]{5,4,3,2,1,0:T(8,128)(2,1)}, u32[]{:S(2)}) copy-start(bf16[1,2,2,2,16,256]{5,4,3,2,1,0:T(8,128)(2,1)} %get-tuple-element.99) | copy-start | bytes 196612
  545.8 6.4 %copy-start.30 = (bf16[1,2,2,2,48,256]{5,4,3,2,1,0:T(8,128)(2,1)S(1)}, bf16[1,2,2,2,48,256]{5,4,3,2,1,0:T(8,128)(2,1)}, u32[]{:S(2)}) copy-start(bf16[1,2,2,2,48,256]{5,4,3,2,1,0:T(8,128)(2,1)} %get-tuple-element.97) | copy-start | bytes 589828
  545.8 7.2 %copy-start.23 = (bf16[10,64,768]{2,1,0:T(8,128)(2,1)S(1)}, bf16[10,64,768]{2,1,0:T(8,128)(2,1)}, u32[]{:S(2)}) copy-start(bf16[10,64,768]{2,1,0:T(8,128)(2,1)} %get-tuple-element.91) | copy-start | bytes 2949124
  552.2 2.3 copy-start.27
  553.0 2.6 copy-start.15
  555.6 2.5 copy-start.13
  558.1 2.9 copy-start.12
  561.1 2.7 copy-start.11
  (21 other events, 29.6 us)

commit v3 on v2

--- a/solution.py
+++ b/solution.py
@@ -650,119 +650,97 @@
 
 
 class Gather:
-    def __init__(self, whole, send_sem, recv_sem, order):
-        self.whole, self.sems, self.order = whole, (send_sem, recv_sem), order + ("core",)
-        self.rows = whole.shape[-2] // 16
-        self.next, self.copy = 0, None
-
-    def at(self, step):
-        dp, core = bit_of("dp"), bit_of("core")
-        first, second = (bit_of(bit) for bit in self.order[:2])
-        start = (core * 4, core * 4 + second * 2, core * 4 + second * 2 + first)
-        if step == 0:
-            piece, size = dp * 8 + start[2], 1
+    def __init__(self, whole, send_sem, recv_sem, split):
+        self.whole, self.send_sem, self.recv_sem = whole, send_sem, recv_sem
+        if split:
+            self.orders = (("core", "y", "z1"), ("core", "z1", "y"))
         else:
-            piece, size = (1 - dp) * 8 + start[3 - step], 2 ** (step - 1)
-        rows = pl.ds(pl.multiple_of(piece * self.rows, 16), size * self.rows)
-        return self.whole.at[(slice(None),) * (len(self.whole.shape) - 2) + (rows,)]
+            self.orders = (("core", "y"),)
+        self.next, self.copies = 0, []
+
+    def at(self, step, side):
+        order = self.orders[side]
+        count = 2 ** len(order)
+        rows = self.whole.shape[-2] // (2 * count)
+        piece = 0
+        for i, bit in enumerate(order):
+            if i <= len(order) - max(step, 1):
+                piece = piece + bit_of(bit) * 2 ** (len(order) - 1 - i)
+        half = bit_of("dp") if step == 0 else 1 - bit_of("dp")
+        size = 1 if step == 0 else 2 ** (step - 1)
+        part = pl.ds(pl.multiple_of((half * count + piece) * rows, 16), size * rows)
+        width = self.whole.shape[-1] // len(self.orders)
+        return self.whole.at[
+            (slice(None),) * (len(self.whole.shape) - 2) + (part, pl.ds(side * width, width))
+        ]
 
     def tick(self):
-        if self.copy is not None:
-            self.copy.wait()
-            self.copy = None
-        if self.next < 4:
-            bit = (("dp",) + self.order)[self.next]
-            part = self.at(self.next)
-            self.copy = send(
-                part, part, self.sems[0].at[self.next], self.sems[1].at[self.next], *mate(bit)
-            )
-            self.copy.start()
+        while self.copies:
+            self.copies.pop().wait()
+        if self.next <= len(self.orders[0]):
+            for side, order in enumerate(self.orders):
+                bit = (("dp",) + order[::-1])[self.next]
+                part = self.at(self.next, side)
+                sems = (self.send_sem.at[side, self.next], self.recv_sem.at[side, self.next])
+                copy = send(part, part, *sems, *mate(bit))
+                copy.start()
+                self.copies.append(copy)
             self.next += 1
 
     def finish(self):
-        while self.copy is not None:
+        while self.copies:
             self.tick()
 
 
-def pipeline(jobs):
-    for slot in range(max(delay + steps for delay, steps, _, _ in jobs) + 1):
-        for delay, steps, start, wait in jobs:
-            step = slot - delay
-            if 0 < step <= steps:
-                wait(step - 1)
-            if 0 <= step < steps:
-                start(step)
-
-
-def patch_kernel(sizes, src, dst, send_sem, recv_sem):
-    to_tiles_start(src, dst, send_sem, recv_sem, sizes)
-    to_tiles_wait(src, dst, send_sem, recv_sem, sizes)
-
-
-def patches_out(patch, sizes):
-    chips, slots, cols = sizes
-    return pl.pallas_call(
-        functools.partial(patch_kernel, sizes),
-        out_shape=jax.ShapeDtypeStruct((slots,) + patch.shape[1:], patch.dtype),
-        in_specs=[pl.BlockSpec(memory_space=pltpu.HBM)],
-        out_specs=pl.BlockSpec(memory_space=pltpu.HBM),
-        scratch_shapes=[
-            pltpu.SemaphoreType.DMA((2 * chips,)),
-            pltpu.SemaphoreType.DMA((slots,)),
-        ],
-        compiler_params=pltpu.CompilerParams(
-            has_side_effects=True, vmem_limit_bytes=VMEM_LIMIT
-        ),
-    )(patch)
-
-
-SUM_ORDERS = (
-    ("dp", "y", "z1", "z2"),
-    ("y", "z1", "dp", "z2"),
-    ("z1", "dp", "y", "z2"),
-)
-BACK_ORDERS = (
-    ("z2", "z1", "y", "core"),
-    ("z2", "y", "z1", "core"),
-    ("z2", "z1", "y", "core"),
-)
 TURNS = {
-    "conv": (0, 0),
-    "fc2": (1, 0),
-    "fc1": (2, 0),
-    "qkv": (2, 1),
-    "out": (1, 1),
-    "proj": (0, 1),
-    "head": (0, 1),
-    "small": (0, 1),
+    "conv": ("dp", ("y", "z1", "z2"), ("z2", "z1", "y", "core")),
+    "fc2": ("y", ("z1", "dp", "z2"), ("z2", "y", "z1", "core")),
+    "fc1": ("z1", ("dp", "y", "z2"), ("z2", "y", "z1", "core")),
+    "out": (None, ("y", "z1", "dp", "z2"), ("z2", "y", "z1", "core")),
+    "proj": (None, ("y", "dp", "z1", "z2"), ("z2", "z1", "y", "core")),
+    "head": (None, ("y", "dp", "z1", "z2"), ("z2", "z1", "y", "core")),
+    "qkv": (None, ("dp", "y", "z1", "z2"), ("z2", "z1", "y", "core")),
+    "small": (None, ("z1", "dp", "y", "z2"), ("z2", "y", "z1", "core")),
 }
-
-
-def reduce_steps(grad, out, acc, recvs, sems, orders):
-    local_sem, send_sem, recv_sem = sems
-    sum_order, back_order = orders
-    half = grad.shape[-1] // 2
-    core = bit_of("core")
-    mine = pl.ds(pl.multiple_of(core * half, 128), half)
-    theirs = pl.ds(pl.multiple_of((1 - core) * half, 128), half)
-    kept = {bit: None for bit in BITS}
-    whole = slice(None)
-    copies = []
-    forward = 1 + len(sum_order)
-
-    def index():
-        return tuple(whole if kept[b] is None else kept[b] for b in BITS)
-
-    def add(recv):
-        free = [b for b in BITS if kept[b] is None]
+EARLY = ("conv", "fc2", "fc1")
+WHOLE = ("out", "proj", "head")
+
+
+class Reduce:
+    def __init__(self, turn, near, away, acc, recvs, out, sems):
+        self.gone, self.sum_order, self.back_order = turn
+        self.near, self.away, self.acc, self.recvs, self.out, self.sems = (
+            near,
+            away,
+            acc,
+            recvs,
+            out,
+            sems,
+        )
+        self.dims = [bit for bit in BITS if bit != self.gone]
+        self.kept = {bit: None for bit in BITS}
+        if self.gone is not None:
+            self.kept[self.gone] = bit_of(self.gone)
+        half = out.shape[-1] // 2
+        self.mine = pl.ds(pl.multiple_of(bit_of("core") * half, 128), half)
+        self.step, self.copies = 0, []
+        self.forward = 1 + len(self.sum_order)
+        self.last = self.forward + len(self.back_order)
+
+    def index(self):
+        free = slice(None)
+        return (free,) + tuple(free if self.kept[b] is None else self.kept[b] for b in self.dims)
+
+    def add(self, recv):
+        acc, kept, whole = self.acc, self.kept, slice(None)
+        free = [b for b in self.dims if kept[b] is None]
 
         def body(i, _):
             bits, left = {}, i
             for b in reversed(free):
                 bits[b] = lax.rem(left, 2)
                 left = lax.div(left, 2)
-            at = tuple(bits[b] if b in bits else kept[b] for b in BITS)
-            here = (whole,) + at
+            here = (whole,) + tuple(bits[b] if b in bits else kept[b] for b in self.dims)
             there = (whole,) + tuple(bits[b] for b in free)
             total = acc[here].astype(jnp.float32) + recv[there].astype(jnp.float32)
             acc[here] = total.astype(acc.dtype)
@@ -770,118 +748,63 @@
 
         lax.fori_loop(0, 2 ** len(free), body, 0)
 
-    def start(step):
-        if step == 0:
-            local = pltpu.make_async_copy(grad.at[..., mine], acc, local_sem.at[0])
-            local.start()
-            copies.append(local)
-            copy = send(
-                grad.at[..., theirs], recvs[0], send_sem.at[0], recv_sem.at[0], *mate("core")
+    def begin(self, copy):
+        copy.start()
+        self.copies.append(copy)
+
+    def travel(self, src, dst, step, bit):
+        _, send_sem, recv_sem = self.sems
+        self.begin(send(src, dst, send_sem.at[step], recv_sem.at[step], *mate(bit)))
+
+    def tick(self):
+        step, whole, kept = self.step, slice(None), self.kept
+        local_sem = self.sems[0]
+        while self.copies:
+            self.copies.pop().wait()
+        if 0 < step <= self.forward:
+            self.add(self.recvs[step - 1])
+        if step == self.forward:
+            kept["core"] = bit_of("core")
+            at = (whole,) + tuple(kept[b] for b in BITS[1:]) + (whole, self.mine)
+            self.begin(
+                pltpu.make_async_copy(self.acc.at[self.index()], self.out.at[at], local_sem.at[1])
             )
-        elif step < forward:
-            bit = sum_order[step - 1]
+        elif step == 0:
+            if self.near is not None:
+                self.begin(pltpu.make_async_copy(self.near, self.acc, local_sem.at[0]))
+            self.travel(self.away, self.recvs[0], 0, self.gone or "core")
+        elif step < self.forward:
+            bit = self.sum_order[step - 1]
             kept[bit] = 1 - bit_of(bit)
-            src = acc.at[(whole,) + index()]
+            src = self.acc.at[self.index()]
             kept[bit] = bit_of(bit)
-            copy = send(src, recvs[step], send_sem.at[step], recv_sem.at[step], *mate(bit))
-        elif step == forward:
-            at = (whole,) + index()[1:] + (whole, mine)
-            copy = pltpu.make_async_copy(acc.at[(whole,) + index()], out.at[at], local_sem.at[1])
-            kept.pop("dp")
-            kept["core"] = mine
-        else:
-            bit = back_order[step - forward - 1]
+            self.travel(src, self.recvs[step], step, bit)
+        elif step <= self.last:
+            if step > self.forward + 1:
+                kept[self.back_order[step - self.forward - 2]] = None
+            bit = self.back_order[step - self.forward - 1]
             at = (whole,) + tuple(whole if kept[b] is None else kept[b] for b in BITS[1:])
-            at = at + (whole, mine)
-            copy = send(
-                out.at[at], out.at[at], send_sem.at[step - 1], recv_sem.at[step - 1], *mate(bit)
-            )
-        copy.start()
-        copies.append(copy)
-
-    def wait(step):
-        while copies:
-            copies.pop().wait()
-        if step < forward:
-            add(recvs[step])
-        elif step > forward:
-            kept[back_order[step - forward - 1]] = None
-
-    return forward + 1 + len(back_order), start, wait
+            at = self.out.at[at + (whole, whole if kept["core"] is None else self.mine)]
+            self.travel(at, at, step - 1, bit)
+        self.step += 1
+
+    def busy(self):
+        return self.step <= self.last + 1
 
 
 def recv_shapes(shape):
-    lead, rows, width = shape[0], shape[5], shape[6]
-    return [(lead,) + (2,) * free + (rows, width // 2) for free in (4, 3, 2, 1, 0)]
-
-
-def out_kernel(sizes, turns, *refs):
-    n = len(turns)
-    tiles, refs = refs[:2], refs[2:]
-    grads, refs = refs[:n], refs[n:]
-    slots, refs = refs[:2], refs[2:]
-    outs, refs = refs[:n], refs[n:]
-    accs, refs = refs[:n], refs[n:]
-    recvs, refs = refs[: 5 * n], refs[5 * n :]
-    tile_send, tile_recv, local_sem, send_sem, recv_sem = refs
-    for i in range(2):
-        to_tiles_start(tiles[i], slots[i], tile_send.at[i], tile_recv.at[i], sizes)
-    jobs = []
-    for i in range(n):
-        steps, start, wait = reduce_steps(
-            grads[i],
-            outs[i],
-            accs[i],
-            recvs[5 * i : 5 * i + 5],
-            (local_sem.at[i], send_sem.at[i], recv_sem.at[i]),
-            (SUM_ORDERS[turns[i][0]], BACK_ORDERS[turns[i][0]]),
-        )
-        jobs.append((turns[i][1], steps, start, wait))
-    pipeline(jobs)
-    for i in range(2):
-        to_tiles_wait(tiles[i], slots[i], tile_send.at[i], tile_recv.at[i], sizes)
-
-
-def bring_out(tiles, grads, sizes):
-    chips, slots, cols = sizes
-    names = list(grads)
-    n = len(names)
-    cut = []
-    for name in names:
-        lead, rows, width = grads[name].shape
-        cut.append(grads[name].reshape(lead, 2, 2, 2, 2, rows // 16, width))
-    accs = [pltpu.VMEM(g.shape[:-1] + (g.shape[-1] // 2,), jnp.bfloat16) for g in cut]
-    recvs = [
-        pltpu.VMEM(shape, jnp.bfloat16)
-        for g in cut
-        for shape in recv_shapes(g.shape)
-    ]
-    outs = pl.pallas_call(
-        functools.partial(out_kernel, sizes, [TURNS[name] for name in names]),
-        out_shape=[
-            jax.ShapeDtypeStruct((slots,) + tile.shape[1:], tile.dtype) for tile in tiles
-        ]
-        + [jax.ShapeDtypeStruct(g.shape[:1] + g.shape[2:], jnp.bfloat16) for g in cut],
-        in_specs=[pl.BlockSpec(memory_space=pltpu.HBM)] * (2 + n),
-        out_specs=[pl.BlockSpec(memory_space=pltpu.HBM)] * (2 + n),
-        scratch_shapes=accs
-        + recvs
-        + [
-            pltpu.SemaphoreType.DMA((2, 2 * chips)),
-            pltpu.SemaphoreType.DMA((2, slots)),
-            pltpu.SemaphoreType.DMA((n, 2)),
-            pltpu.SemaphoreType.DMA((n, 9)),
-            pltpu.SemaphoreType.DMA((n, 9)),
-        ],
-        compiler_params=pltpu.CompilerParams(
-            has_side_effects=True, vmem_limit_bytes=VMEM_LIMIT
-        ),
-    )(*tiles, *cut)
-    sums = {}
-    for name, out in zip(names, outs[2:]):
-        lead, rows, width = grads[name].shape
-        sums[name] = out.reshape(lead, rows // 2, width)
-    return outs[:2], sums
+    free = len(shape) - 3
+    return [shape[:1] + (2,) * left + shape[-2:] for left in range(free, -1, -1)]
+
+
+def early_sum(near, other, bit):
+    lead, rows, width = near.shape
+    total = near.astype(jnp.float32) + swap_cores(other).astype(jnp.float32)
+    total = total.astype(jnp.bfloat16).reshape(lead, 2, 2, 2, 2, rows // 16, width)
+    axis, own = 1 + BITS.index(bit), bit_of(bit)
+    keep = lax.dynamic_index_in_dim(total, own, axis, keepdims=False)
+    away = lax.dynamic_index_in_dim(total, 1 - own, axis, keepdims=False)
+    return keep, away
 
 
 SCALE = HEAD_DIM**-0.5
@@ -908,12 +831,12 @@
     return out.T, logs
 
 
-def attend_back_kernel(q_ref, k_ref, v_ref, o_ref, log_ref, g_ref, dq_ref, dk_ref, dv_ref):
+def attend_pair_back(q, k, v, o, logs, g):
     lane = lax.broadcasted_iota(jnp.int32, (1, 128), 1)
     sub = lax.broadcasted_iota(jnp.int32, (128, 1), 0)
-    k, v, q, g = k_ref[...], v_ref[...], q_ref[...], g_ref[...]
-    product = (g.astype(jnp.float32) * o_ref[...]).T
+    product = (g.astype(jnp.float32) * o).T
     dq = jnp.zeros((128, q.shape[0]), jnp.float32)
+    dk = dv = 0.0
     for h in range(2):
         mine = (lane >= 64) == (h == 1)
         q_own, g_own = jnp.where(mine, q, 0), jnp.where(mine, g, 0)
@@ -921,7 +844,7 @@
         scores = lax.dot_general(
             k, q_own, (((1,), (1,)), ((), ())), preferred_element_type=jnp.float32
         )
-        p = jnp.exp2(scores * (SCALE * LOG2E) - log_ref[0, h : h + 1, :])
+        p = jnp.exp2(scores * (SCALE * LOG2E) - logs[h])
         dp = lax.dot_general(
             v, g_own, (((1,), (1,)), ((), ())), preferred_element_type=jnp.float32
         )
@@ -930,32 +853,181 @@
             k, ds, (((0,), (0,)), ((), ())), preferred_element_type=jnp.float32
         )
         dq = jnp.where((sub >= 64) == (h == 1), dq_own * SCALE, dq)
-        dk = jnp.dot(ds, q_own, preferred_element_type=jnp.float32) * SCALE
-        dv = jnp.dot(p.astype(jnp.bfloat16), g_own, preferred_element_type=jnp.float32)
-        if h == 0:
-            dk_ref[...], dv_ref[...] = dk, dv
+        dk = dk + jnp.dot(ds, q_own, preferred_element_type=jnp.float32) * SCALE
+        dv = dv + jnp.dot(p.astype(jnp.bfloat16), g_own, preferred_element_type=jnp.float32)
+    return dq.T, dk, dv
+
+
+BACK_INPUTS = ("q", "k", "v", "o", "logs", "g", "x", "stream", "w_qkv", "gain", "bias", "small")
+LN_ROWS = 8
+
+
+def backward_kernel(sizes, *refs):
+    refs = list(refs)
+
+    def take(names):
+        return {name: refs.pop(0) for name in names}
+
+    ref = take(BACK_INPUTS)
+    tiles = refs.pop(0)
+    near, away, grads = take(EARLY), take(EARLY), take(WHOLE)
+    slot_tokens, slot_grads = refs.pop(0), refs.pop(0)
+    outs = take(TURNS)
+    accs = take(TURNS)
+    recvs = {name: [refs.pop(0) for _ in range(4 if TURNS[name][0] else 5)] for name in TURNS}
+    mixed, far_out, far_in, own_pair, grad_tile, small_wide = (refs.pop(0) for _ in range(6))
+    outbox = take(("qkv", "small"))
+    tile_send, tile_recv, core_sem, local_sem, send_sem, recv_sem = refs
+    low, f32 = jnp.bfloat16, jnp.float32
+    core = bit_of("core")
+
+    jobs = {}
+    for i, name in enumerate(TURNS):
+        sems = (local_sem.at[i], send_sem.at[i], recv_sem.at[i])
+        if name in EARLY:
+            source = (near[name], away[name])
+        elif name in WHOLE:
+            half = grads[name].shape[-1] // 2
+            source = tuple(
+                grads[name].at[..., pl.ds(pl.multiple_of(side * half, 128), half)]
+                for side in (core, 1 - core)
+            )
         else:
-            dk_ref[...] += dk
-            dv_ref[...] += dv
-    dq_ref[...] = dq.T
-
-
-def pair_block(rows):
-    return pl.BlockSpec((rows, 128), lambda i: (0, i))
-
-
-def attend_back(q, k, v, o, logs, g):
-    rows, width = q.shape
-    keys = k.shape[0]
-    own, both = pair_block(rows), pair_block(keys)
-    return pl.pallas_call(
-        attend_back_kernel,
-        grid=(width // 128,),
-        in_specs=[own, both, both, own, pl.BlockSpec((1, 2, rows), lambda i: (i, 0, 0)), own],
-        out_specs=[own, both, both],
-        out_shape=[jax.ShapeDtypeStruct((n, width), jnp.float32) for n in (rows, keys, keys)],
-        compiler_params=pltpu.CompilerParams(vmem_limit_bytes=VMEM_LIMIT),
-    )(q, k, v, o, logs, g)
+            source = (None, outbox[name])
+        jobs[name] = Reduce(TURNS[name], *source, accs[name], recvs[name], outs[name], sems)
+
+    def tick(*names):
+        for name in names:
+            jobs[name].tick()
+
+    tick(*EARLY)
+    tick(*WHOLE)
+    to_tiles_start(tiles, slot_tokens, tile_send.at[0], tile_recv.at[0], sizes)
+    rows, width = ref["q"].shape
+    for pair in range(width // 128):
+        lanes = pl.ds(pair * 128, 128)
+        dq, dk, dv = attend_pair_back(
+            ref["q"][:, lanes],
+            ref["k"][:, lanes],
+            ref["v"][:, lanes],
+            ref["o"][:, lanes],
+            [ref["logs"][pair, h : h + 1, :] for h in range(2)],
+            ref["g"][:, lanes],
+        )
+        mixed[:, lanes] = dq.astype(low)
+        for i, value in enumerate((dk, dv)):
+            to = pl.ds(i * width + pair * 128, 128)
+            own_pair[:, to] = value[:rows]
+            far_out[:, to] = value[rows:].astype(low)
+        if pair == 2:
+            tick(*WHOLE)
+    pair_copy = send(far_out, far_in, core_sem.at[0], core_sem.at[1], *mate("core"))
+    pair_copy.start()
+    stream = ref["x"][...].astype(f32)
+    normed, scaled, factor = norm_rows(stream, ref["gain"][...], ref["bias"][...])
+    normed = normed.astype(low)
+    pair_copy.wait()
+    mixed[:, width:] = (own_pair[...] + far_in[...].astype(f32)).astype(low)
+
+    half = mixed.shape[1] // 2
+    for side, target in ((1 - core, outbox["qkv"]), (core, accs["qkv"])):
+        for c in range(0, half, 384):
+            part = mixed[:, pl.ds(pl.multiple_of(side * half + c, 128), 384)]
+            value = outer_product(normed, part).astype(low)
+            target[..., c : c + 384] = value.reshape(target.shape[:-1] + (384,))
+        if target is outbox["qkv"]:
+            tick(*EARLY)
+    tick("qkv")
+    tick(*WHOLE)
+    grad = back_product(mixed[...], ref["w_qkv"][...])
+    gained, grad_gain, grad_bias = norm_back(grad, scaled, factor, ref["gain"][...])
+    grad_tile[...] = (ref["stream"][...] + gained).astype(low).reshape(grad_tile.shape)
+
+    small_wide[...] = ref["small"][...]
+    for v, value in enumerate((grad_gain, grad_bias)):
+        value = value.reshape(1, width)
+        for j in range(width // 128):
+            side, at = divmod(j, width // 256)
+            row = side * (small_wide.shape[0] // 2) + LN_ROWS + 2 * v + at // 2
+            small_wide[row : row + 1, at % 2 * 128 : at % 2 * 128 + 128] = value[
+                :, j * 128 : (j + 1) * 128
+            ]
+    for side, target in ((core, accs["small"]), (1 - core, outbox["small"])):
+        part = small_wide[:, pl.ds(pl.multiple_of(side * 128, 128), 128)].astype(low)
+        target[...] = part.reshape(target.shape)
+    tick("small")
+    to_tiles_start(grad_tile, slot_grads, tile_send.at[1], tile_recv.at[1], sizes)
+    while any(job.busy() for job in jobs.values()):
+        for job in jobs.values():
+            if job.busy():
+                job.tick()
+    to_tiles_wait(tiles, slot_tokens, tile_send.at[0], tile_recv.at[0], sizes)
+    to_tiles_wait(grad_tile, slot_grads, tile_send.at[1], tile_recv.at[1], sizes)
+
+
+def run_backward(inputs, tiles, early, grads, sizes):
+    chips, slots, _ = sizes
+    low, f32 = jnp.bfloat16, jnp.float32
+    rows, width = inputs["q"].shape
+    cut, accs = {}, {}
+    for name in TURNS:
+        if name in EARLY:
+            accs[name] = early[name][0].shape
+            continue
+        if name in WHOLE:
+            lead, height, across = grads[name].shape
+            cut[name] = grads[name].reshape(lead, 2, 2, 2, 2, height // 16, across)
+        else:
+            lead = 1
+            height, across = (width, 3 * width) if name == "qkv" else inputs["small"].shape
+        accs[name] = (lead, 2, 2, 2, 2, height // 16, across // 2)
+    shape = jax.ShapeDtypeStruct
+    out_shape = [shape((slots,) + tiles.shape[1:], low)] * 2 + [
+        shape(acc[:1] + (2, 2, 2, acc[-2], 2 * acc[-1]), low) for acc in accs.values()
+    ]
+    recvs = [value for acc in accs.values() for value in recv_shapes(acc)]
+    hbm, vmem = pl.BlockSpec(memory_space=pltpu.HBM), pl.BlockSpec(memory_space=pltpu.VMEM)
+    n = len(TURNS)
+    slot_tokens, slot_grads, *sums = pl.pallas_call(
+        functools.partial(backward_kernel, sizes),
+        out_shape=out_shape,
+        in_specs=[vmem] * len(BACK_INPUTS) + [hbm] * (1 + 2 * len(EARLY) + len(WHOLE)),
+        out_specs=[hbm] * (2 + n),
+        scratch_shapes=[pltpu.VMEM(value, low) for value in list(accs.values()) + recvs]
+        + [
+            pltpu.VMEM((rows, 3 * width), low),
+            pltpu.VMEM((rows, 2 * width), low),
+            pltpu.VMEM((rows, 2 * width), low),
+            pltpu.VMEM((rows, 2 * width), f32),
+            pltpu.VMEM(tiles.shape, low),
+            pltpu.VMEM(inputs["small"].shape, f32),
+            pltpu.VMEM(accs["qkv"], low),
+            pltpu.VMEM(accs["small"], low),
+            pltpu.SemaphoreType.DMA((2, 2 * chips)),
+            pltpu.SemaphoreType.DMA((2, slots)),
+            pltpu.SemaphoreType.DMA((2,)),
+            pltpu.SemaphoreType.DMA((n, 2)),
+            pltpu.SemaphoreType.DMA((n, 9)),
+            pltpu.SemaphoreType.DMA((n, 9)),
+        ],
+        compiler_params=pltpu.CompilerParams(
+            has_side_effects=True, vmem_limit_bytes=VMEM_LIMIT
+        ),
+    )(
+        *(inputs[name] for name in BACK_INPUTS),
+        tiles,
+        *(early[name][0] for name in EARLY),
+        *(early[name][1] for name in EARLY),
+        *(cut[name] for name in WHOLE),
+    )
+    return (
+        slot_tokens,
+        slot_grads,
+        {
+            name: out.reshape(out.shape[0], 8 * out.shape[4], out.shape[5])
+            for name, out in zip(TURNS, sums)
+        },
+    )
 
 
 GELU_K, GELU_C = 0.7978845608028654, 0.044715
@@ -1030,9 +1102,13 @@
 def kernel_grads(wide, grad, out_ref, first, core, cols):
     own = grad.shape[0]
     for a in range(3):
-        out_ref[first + turned(core, a, 2)] = outer_product(
-            wide[a * cols : a * cols + own, :], grad
-        ).astype(out_ref.dtype)
+        value = outer_product(wide[a * cols : a * cols + own, :], grad)
+        half = value.shape[1] // 2
+        left, right = value[:, :half], value[:, half:]
+        at = first + turned(core, a, 2)
+        near, other = out_ref
+        near[at] = jnp.where(core == 0, left, right).astype(near.dtype)
+        other[at] = jnp.where(core == 0, right, left).astype(other.dtype)
 
 
 def conv_back_rows(src, w_ref, first, core, cols):
@@ -1058,13 +1134,22 @@
     f1_ref,
     first1_ref,
     w_ref,
-    g_ref,
+    patch_ref,
+    near_ref,
+    other_ref,
     out_ref,
+    slot_ref,
     wide,
     wide_g,
     total,
     parted,
+    tile_send,
+    tile_recv,
 ):
+    chips = patch_ref.shape[0]
+    sizes = (chips, slot_ref.shape[0], cols)
+    to_tiles_start(patch_ref, slot_ref, tile_send, tile_recv, sizes)
+    g_ref = (near_ref, other_ref)
     tile_rows, tile_cols = tiles
     core = place()[2]
     own_rows = 2 * tile_rows
@@ -1116,41 +1201,44 @@
                 block(row * cols + z, tile_cols), :
             ]
     out_ref[...] = parted[...].astype(out_ref.dtype)
+    to_tiles_wait(patch_ref, slot_ref, tile_send, tile_recv, sizes)
 
 
 def in_vmem(count):
     return [pl.BlockSpec(memory_space=pltpu.VMEM)] * count
 
 
-def plain_call(kernel, inputs, out_shape, scratch):
-    return pl.pallas_call(
-        kernel,
-        out_shape=out_shape,
-        in_specs=in_vmem(len(inputs)),
-        out_specs=in_vmem(len(out_shape)),
-        scratch_shapes=scratch,
-        compiler_params=pltpu.CompilerParams(vmem_limit_bytes=VMEM_LIMIT),
-    )(*inputs)
-
-
-def maps_backward(tall, far, saved, w_conv, tiles, cols):
+def maps_backward(tall, far, saved, w_conv, patch, slots, tiles, cols):
     rows, feat = saved[0].shape
     line = cols * tiles[1]
     own = 2 * tiles[0] * line
-    return plain_call(
+    low, f32 = jnp.bfloat16, jnp.float32
+    hbm = pl.BlockSpec(memory_space=pltpu.HBM)
+    half = jax.ShapeDtypeStruct((12, 3 * feat, feat // 2), low)
+    return pl.pallas_call(
         functools.partial(maps_back_kernel, tiles, cols),
-        (tall, far, *saved, w_conv),
-        [
-            jax.ShapeDtypeStruct((12, 3 * feat, feat), jnp.bfloat16),
-            jax.ShapeDtypeStruct((own, feat), jnp.bfloat16),
+        out_shape=[
+            half,
+            half,
+            jax.ShapeDtypeStruct((own, feat), low),
+            jax.ShapeDtypeStruct((slots,) + patch.shape[1:], low),
         ],
-        [pltpu.VMEM((rows + 2 * line, 3 * feat), jnp.bfloat16)] * 2
-        + [pltpu.VMEM((rows, feat), jnp.float32), pltpu.VMEM((own, feat), jnp.float32)],
-    )
+        in_specs=in_vmem(3 + len(saved)) + [hbm],
+        out_specs=in_vmem(3) + [hbm],
+        scratch_shapes=[pltpu.VMEM((rows + 2 * line, 3 * feat), low)] * 2
+        + [
+            pltpu.VMEM((rows, feat), f32),
+            pltpu.VMEM((own, feat), f32),
+            pltpu.SemaphoreType.DMA((2 * patch.shape[0],)),
+            pltpu.SemaphoreType.DMA((slots,)),
+        ],
+        compiler_params=pltpu.CompilerParams(
+            has_side_effects=True, vmem_limit_bytes=VMEM_LIMIT
+        ),
+    )(tall, far, *saved, w_conv, patch)
 
 
 WEIGHTS = ("qkv", "out", "fc1", "fc2", "proj", "conv")
-GATHER_ORDERS = (("z1", "y"), ("y", "z1"), ("z1", "y"), ("y", "z1"), ("z1", "y"), ("y", "z1"))
 VECTORS = ("fc1_b", "fc2_b", "ln1_gain", "ln1_bias", "ln2_gain", "ln2_bias")
 SAVED = ("x", "q", "k", "v", "o", "logs", "after_attn", "hidden", "tokens_low")
 MAPS = ("f0", "first0", "f1", "first1", "coarse")
@@ -1195,6 +1283,7 @@
     whole = take(WEIGHTS)
     far_vectors = take(VECTORS)
     keys, values, f0, hidden_low, flat, wide, stage = (refs.pop(0) for _ in range(7))
+    kept = take(("o", "after_attn", "hidden", "first0", "f1", "first1"))
     tile_send, tile_recv, gather_send, gather_recv, vec_send, vec_recv, stage_sem, core_sem, out_sem = refs
     dp, y, core, z = place()
     low, f32 = jnp.bfloat16, jnp.float32
@@ -1219,10 +1308,9 @@
             incoming[i].start()
 
     gathers = {
-        name: Gather(whole[name], gather_send.at[i], gather_recv.at[i], GATHER_ORDERS[i])
+        name: Gather(whole[name], gather_send.at[i], gather_recv.at[i], name in ("qkv", "out"))
         for i, name in enumerate(WEIGHTS)
     }
-    begun = []
     done = [0]
     for i in range(STAGES - 1):
         fetch(i)
@@ -1235,12 +1323,10 @@
             target = work[i][1][1]
             target[...] = stage[i % STAGES, : target.shape[0], : target.shape[1]].astype(low)
             done[0] += 1
-        gathers[name].tick()
-        begun.append(gathers[name])
-
-    def tick():
-        for gather in begun:
-            gather.tick()
+
+    def tick(*names):
+        for name in names:
+            gathers[name].tick()
 
     out_copies = []
 
@@ -1250,15 +1336,16 @@
         out_copies.append(copy)
 
     round_next("qkv")
+    tick("qkv")
     round_next("out")
+    tick("out")
     round_next("fc1")
-    tick()
+    tick("qkv", "fc1")
     round_next("fc2")
-    tick()
     round_next("proj")
-    gathers["qkv"].tick()
-    gathers["out"].tick()
+    tick("qkv")
     round_next("conv")
+    tick("out", "qkv", "fc1", "fc2")
     gathers["qkv"].finish()
     for copy in vector_copies:
         copy.wait()
@@ -1271,8 +1358,6 @@
         vec[name] = row.astype(low).astype(f32)
         vector_out[name][...] = vec[name]
     to_images_wait(tile_in["tokens"], image, tile_send.at[0], tile_recv.at[0], sizes)
-    to_images_start(tile_in["patches"], image_out["patches"], tile_send.at[1], tile_recv.at[1], sizes)
-    to_images_start(tile_in["cots"], image_out["cots"], tile_send.at[2], tile_recv.at[2], sizes)
 
     width = image.shape[3]
     x = jnp.where(flag[0:1, 0:1] > 0, image[1].astype(f32), image[0].astype(f32))
@@ -1296,9 +1381,11 @@
             )
             copy.start()
             core_copies.append(copy)
-    tick()
+    tick("out")
     for copy in core_copies:
         copy.wait()
+    tick("fc1", "fc2", "conv", "proj")
+    to_images_start(tile_in["patches"], image_out["patches"], tile_send.at[1], tile_recv.at[1], sizes)
     keep(keys, saved["k"])
     keep(values, saved["v"])
     for name in ("qkv",):
@@ -1307,30 +1394,36 @@
     for pair in range(width // 128):
         lanes = pl.ds(pair * 128, 128)
         out, logs = attend_pair(saved["q"][:, lanes], keys[:, lanes], values[:, lanes])
-        saved["o"][:, lanes] = out
+        kept["o"][:, lanes] = out
         for h in range(2):
             saved["logs"][pair, h : h + 1, :] = logs[h]
-        if pair % 2 == 1:
-            tick()
+        if pair == 1:
+            tick("out")
     gathers["out"].finish()
+    tick("fc2", "conv", "proj")
+    to_images_start(tile_in["cots"], image_out["cots"], tile_send.at[2], tile_recv.at[2], sizes)
     after_attn = saved["x"][...].astype(f32) + jnp.dot(
-        saved["o"][...].astype(low), whole["out"][...], preferred_element_type=f32
-    )
-    saved["after_attn"][...] = after_attn
+        kept["o"][...].astype(low), whole["out"][...], preferred_element_type=f32
+    )
+    kept["after_attn"][...] = after_attn
+    keep(kept["o"], saved["o"])
+    keep(kept["after_attn"], saved["after_attn"])
     normed_two = norm_rows(after_attn, vec["ln2_gain"], vec["ln2_bias"])[0].astype(low)
     gathers["fc1"].finish()
     for c in range(0, hidden_low.shape[1], width):
         part = pl.ds(c, width)
         hidden = jnp.dot(normed_two, whole["fc1"][:, part], preferred_element_type=f32)
         hidden = hidden + vec["fc1_b"][:, c : c + width]
-        saved["hidden"][:, part] = hidden
+        kept["hidden"][:, part] = hidden
         hidden_low[:, part] = jax.nn.gelu(hidden).astype(low)
+    keep(kept["hidden"], saved["hidden"])
     gathers["fc2"].finish()
-    after_mlp = saved["after_attn"][...] + (
+    after_mlp = kept["after_attn"][...] + (
         jnp.dot(hidden_low[...], whole["fc2"][...], preferred_element_type=f32) + vec["fc2_b"]
     )
     tokens_low = after_mlp.astype(low)
     saved["tokens_low"][...] = tokens_low
+    tick("conv")
     gathers["proj"].finish()
 
     flat[...] = jnp.dot(tokens_low, whole["proj"][...], preferred_element_type=f32)
@@ -1358,8 +1451,10 @@
         keep(whole[name], whole_out[name])
     keep(f0, maps["f0"])
     maps_forward(
-        line, rows, f0, maps["first0"], maps["f1"], maps["first1"], whole["conv"], maps["coarse"], wide
-    )
+        line, rows, f0, kept["first0"], kept["f1"], kept["first1"], whole["conv"], maps["coarse"], wide
+    )
+    for name in ("first0", "f1", "first1"):
+        keep(kept[name], maps[name])
     for copy in out_copies:
         copy.wait()
     to_images_wait(
@@ -1405,8 +1500,8 @@
     out_specs = (
         [hbm] * (2 + len(WEIGHTS))
         + [vmem] * len(VECTORS)
-        + [hbm if name in ("k", "v") else vmem for name in SAVED]
-        + [hbm if name == "f0" else vmem for name in MAPS]
+        + [hbm if name in ("k", "v", "o", "after_attn", "hidden") else vmem for name in SAVED]
+        + [vmem if name == "coarse" else hbm for name in MAPS]
     )
     n = len(WEIGHTS)
     outs = pl.pallas_call(
@@ -1425,15 +1520,21 @@
             pltpu.VMEM((rows, feat), f32),
             pltpu.VMEM((ext + 2 * line, 3 * feat), low),
             pltpu.VMEM((STAGES, 384, 768), f32),
+            pltpu.VMEM((rows, width), f32),
+            pltpu.VMEM((rows, width), f32),
+            pltpu.VMEM((rows, hidden), f32),
+            pltpu.VMEM((ext, feat), f32),
+            pltpu.VMEM((ext, feat), f32),
+            pltpu.VMEM((ext, feat), f32),
             pltpu.SemaphoreType.DMA((3, slots)),
             pltpu.SemaphoreType.DMA((3, 2 * chips)),
-            pltpu.SemaphoreType.DMA((n, 4)),
-            pltpu.SemaphoreType.DMA((n, 4)),
+            pltpu.SemaphoreType.DMA((n, 2, 4)),
+            pltpu.SemaphoreType.DMA((n, 2, 4)),
             pltpu.SemaphoreType.DMA((len(VECTORS),)),
             pltpu.SemaphoreType.DMA((len(VECTORS),)),
             pltpu.SemaphoreType.DMA((STAGES,)),
             pltpu.SemaphoreType.DMA((2, 3 + HALO)),
-            pltpu.SemaphoreType.DMA((n + 3,)),
+            pltpu.SemaphoreType.DMA((n + 9,)),
         ],
         compiler_params=pltpu.CompilerParams(
             has_side_effects=True, vmem_limit_bytes=VMEM_LIMIT
@@ -1565,7 +1666,25 @@
         for c in range(cols)
     ]
     patch = jnp.pad(jnp.stack(cuts), ((0, 0), (0, PATCH - cells), (0, 0)))
-    patch = patches_out(patch, sizes)[:, :cells]
+    parts = chosen(image_patches)[:, :cells].astype(jnp.float32)
+    parts = parts.reshape(2, cols, tile_rows + 2, tile_cols + 2, feat)
+    wide = sum(
+        jnp.pad(parts[:, c], ((0, 0), (0, 0), (c * tile_cols, (cols - 1 - c) * tile_cols), (0, 0)))
+        for c in range(cols)
+    )
+    wide = jnp.concatenate(
+        [wide[:, :, 1:2] + wide[:, :, :1], wide[:, :, 2:-2], wide[:, :, -2:-1] + wide[:, :, -1:]], 2
+    )
+    tall = jnp.pad(wide[0], ((0, tile_rows), (0, 0), (0, 0))) + jnp.pad(
+        wide[1], ((tile_rows, 0), (0, 0), (0, 0))
+    )
+    tall = tall.reshape(-1, feat)
+    *grad_conv, proj_grad, slot_patch = maps_backward(
+        tall, swap_cores(tall), [maps[name] for name in MAPS[:-1]], w_conv, patch, slots, tiles, cols
+    )
+    grad_conv = early_sum(*(g.reshape(36, feat, feat // 2) for g in grad_conv), TURNS["conv"][0])
+
+    patch = slot_patch[:, :cells]
     patch = patch.reshape(slots, tile_rows + 2, tile_cols + 2, feat).astype(jnp.float32)
     patch = jnp.where(present[:, None, None, None] > 0, patch, 0.0)
     upsampled = double_axis(double_axis(patch, 1), 2).astype(low)
@@ -1578,26 +1697,6 @@
     merged_out = merged.astype(low).reshape(cot_merged.shape)
     grad_head_w = outer_product(fine_rows, head_grad)
 
-    parts = chosen(image_patches)[:, :cells].astype(jnp.float32)
-    parts = parts.reshape(2, cols, tile_rows + 2, tile_cols + 2, feat)
-    wide = sum(
-        jnp.pad(parts[:, c], ((0, 0), (0, 0), (c * tile_cols, (cols - 1 - c) * tile_cols), (0, 0)))
-        for c in range(cols)
-    )
-    wide = jnp.concatenate(
-        [wide[:, :, 1:2] + wide[:, :, :1], wide[:, :, 2:-2], wide[:, :, -2:-1] + wide[:, :, -1:]], 2
-    )
-    tall = jnp.pad(wide[0], ((0, tile_rows), (0, 0), (0, 0))) + jnp.pad(
-        wide[1], ((tile_rows, 0), (0, 0), (0, 0))
-    )
-    tall = tall.reshape(-1, feat)
-    grad_conv, proj_grad = maps_backward(
-        tall, swap_cores(tall), [maps[name] for name in MAPS[:-1]], w_conv, tiles, cols
-    )
-    grad_conv = grad_conv.reshape(36, feat, feat)
-
-    normed, scaled_one, factor_one = norm_rows(saved["x"].astype(jnp.float32), gain_one, bias_one)
-    normed_low = normed.astype(low)
     normed_two, scaled_two, factor_two = norm_rows(saved["after_attn"], gain_two, bias_two)
     normed_two_low = normed_two.astype(low)
     hidden = saved["hidden"]
@@ -1608,10 +1707,20 @@
     stream_grad = jnp.where(image_present > 0, stream_grad, 0.0) + back_product(proj_grad, w_proj)
     down_grad = stream_grad.astype(low)
     grad_down_b = jnp.sum(down_grad.astype(jnp.float32), 0)
-    grad_down_w = outer_product(hidden_low, down_grad)
+
+    def halves_of(first_op, second_op):
+        half = second_op.shape[1] // 2
+        return [
+            outer_product(
+                first_op, lax.dynamic_slice_in_dim(second_op, side * half, half, 1)
+            ).astype(low)[None]
+            for side in (core, 1 - core)
+        ]
+
+    grad_down_w = early_sum(*halves_of(hidden_low, down_grad), TURNS["fc2"][0])
     up_grad = gelu_grad(hidden, back_product(down_grad, w_down)).astype(low)
     grad_up_b = jnp.sum(up_grad.astype(jnp.float32), 0)
-    grad_up_w = outer_product(normed_two_low, up_grad)
+    grad_up_w = early_sum(*halves_of(normed_two_low, up_grad), TURNS["fc1"][0])
     norm_grad, grad_gain_two, grad_bias_two = norm_back(
         back_product(up_grad, w_up), scaled_two, factor_two, gain_two
     )
@@ -1619,44 +1728,36 @@
     branch_grad = stream_grad.astype(low)
     grad_out_w = outer_product(attended, branch_grad)
     attended_grad = back_product(branch_grad, w_out).astype(low)
-    query_grad, key_grad, value_grad = attend_back(
-        *(saved[name] for name in ("q", "k", "v", "o", "logs")), attended_grad
-    )
-    pair_grad = jnp.concatenate([key_grad, value_grad], 1)
-    pair_grad = pair_grad[:rows] + swap_cores(pair_grad[rows:].astype(low)).astype(jnp.float32)
-    mixed_grad = jnp.concatenate([query_grad, pair_grad], 1).astype(low)
-    grad_qkv = outer_product(normed_low, mixed_grad)
-    norm_grad, grad_gain_one, grad_bias_one = norm_back(
-        back_product(mixed_grad, w_qkv), scaled_one, factor_one, gain_one
-    )
-    input_grad = (stream_grad + norm_grad).astype(low)
-
-    vector_grads = (
-        grad_up_b,
-        grad_down_b,
-        grad_gain_one,
-        grad_bias_one,
-        grad_gain_two,
-        grad_bias_two,
-        grad_head_b,
-        grad_shift,
-    )
-    packed = jnp.concatenate([v.reshape(2, -1) for v in vector_grads], 1).astype(low)
-    room = 128 * feat
-    packed = jnp.pad(packed, ((0, 0), (0, room - packed.shape[1]))).reshape(256, feat)
-    grads = {
-        "conv": grad_conv,
-        "fc2": grad_down_w.astype(low)[None],
-        "fc1": grad_up_w.astype(low)[None],
-        "qkv": grad_qkv.astype(low)[None],
-        "out": grad_out_w.astype(low)[None],
-        "proj": grad_proj.astype(low)[None],
-        "head": grad_head_w.astype(low)[None],
-        "small": packed[None],
-    }
-    (slot_tokens, slot_grads), sums = bring_out(
-        (tokens_low.reshape(chips, tile, width), input_grad.reshape(chips, tile, width)),
-        grads,
+    blank = jnp.zeros((2, (width // 2 + feat - 1) // feat * feat), jnp.float32)
+    packed = []
+    for v in (grad_up_b, grad_down_b, None, None, grad_gain_two, grad_bias_two, grad_head_b, grad_shift):
+        if v is None:
+            packed.append(blank)
+            continue
+        v = v.reshape(2, -1)
+        packed.append(jnp.pad(v, ((0, 0), (0, -v.shape[1] % feat))))
+    starts, at = [], 0
+    for v in packed:
+        starts.append(at)
+        at += v.shape[1]
+    packed = jnp.pad(jnp.concatenate(packed, 1), ((0, 0), (0, 128 * feat - at)))
+    slot_tokens, slot_grads, sums = run_backward(
+        {
+            **{name: saved[name] for name in ("q", "k", "v", "o", "logs", "x")},
+            "g": attended_grad,
+            "stream": stream_grad,
+            "w_qkv": w_qkv,
+            "gain": gain_one,
+            "bias": bias_one,
+            "small": packed.reshape(256, feat),
+        },
+        tokens_low.reshape(chips, tile, width),
+        {"conv": grad_conv, "fc2": grad_down_w, "fc1": grad_up_w},
+        {
+            "out": grad_out_w.astype(low)[None],
+            "proj": grad_proj.astype(low)[None],
+            "head": grad_head_w.astype(low)[None],
+        },
         sizes,
     )
     here = present[:, None, None] > 0
@@ -1664,10 +1765,9 @@
     grad_tokens = jnp.where(here, slot_grads.astype(jnp.float32), 0.0).reshape(tokens.shape)
     sums = {name: value.astype(jnp.float32) for name, value in sums.items()}
     packed = sums["small"].reshape(-1)
-    pieces, at = [], 0
-    for length in (v.shape[0] for v in vectors + (head_b, shift_row)):
-        pieces.append(packed[at : at + length])
-        at += length
+    pieces = [
+        packed[at : at + v.shape[0]] for at, v in zip(starts, vectors + (head_b, shift_row))
+    ]
     return (
         tokens_out,
         merged_out,

time: 571 us -> 521 us (0.912)
  Pallas kernels: 429 us -> 380 us
  local copies, waits for them, and re-layouts: 36.2 us -> 44.2 us
  other arithmetic: 47.2 us -> 41.3 us
    pallas_call x4 -> x2, Pallas kernels: 294 us -> 269 us  [the longest x1 219 us: run_backward(): pl.pallas_call(functools.partial(backward_kernel, sizes), out_shape=out_s...]
    pallas_call x1, Pallas kernels: 135 us -> 111 us  [run_forward(): pl.pallas_call(functools.partial(forward_kernel, sizes, tiles), out_shape...]
    dot_general x6 -> x5, matrix products: 25.2 us -> 18.9 us  [back_product(): lax.dot_general(first_op, weight, (((1,), (1,)), ((), ())), preferred_ele...]
    unnamed x153 -> x94, local copies, waits for them, and re-layouts: 11.8 us -> 7.71 us
    dot_general x6 -> x7, matrix products: 20 us -> 22.4 us  [outer_product(): lax.dot_general(first_op, second_op, (((0,), (0,)), ((), ())), preferred_...]
  transfers between devices with their start and end apart: 4 -> 6, of which waited for: 0 -> 0; matrix products, arithmetic and copies ran while one was open for 5% -> 9% of each run, Pallas kernels for 0% -> 0%
where the time goes in v3:
time: 521 us; the launch traced here: 516 us
  Pallas kernels  380 us (73%)
  local copies, waits for them, and re-layouts  44.2 us (8%)
  matrix products  41.8 us (8%)
  other arithmetic  41.3 us (8%)
  starting transfers between devices  6.04 us (1%)
    pallas_call x1, Pallas kernels, run_backward(): pl.pallas_call(functools.partial(backward_kernel, sizes), out_shape=out_s...  219 us
    pallas_call x1, Pallas kernels, run_forward(): pl.pallas_call(functools.partial(forward_kernel, sizes, tiles), out_shape...  111 us
    pallas_call x1, Pallas kernels, maps_backward(): pl.pallas_call(functools.partial(maps_back_kernel, tiles, cols), out_shap...  49.9 us
    dot_general x7, matrix products, outer_product(): lax.dot_general(first_op, second_op, (((0,), (0,)), ((), ())), preferred_...  22.4 us
    dot_general x5, matrix products, back_product(): lax.dot_general(first_op, weight, (((1,), (1,)), ((), ())), preferred_ele...  18.9 us
    convert_element_type x8, other arithmetic, on_chip(): sums = {name: value.astype(jnp.float32) for name, value in sums.items()}  15.6 us
  transfers between devices with their start and end apart: 6, of which 0 were waited for; matrix products, arithmetic and copies ran while one was open for 9% of the time, Pallas kernels for 0%

profile of v3, /device:TPU:0, one launch (start us, length us, event | category | flops | bytes accessed | tf_op | source)
XLA Modules:
  0.0 516.2 jit_solution(8840498409977818297)
XLA Ops:
  0.7 0.9 convert_element_type.307
  1.6 3.0 collective-permute-start
  5.3 0.9 convert_bitcast_fusion.1
  8.2 1.3 broadcast_in_dim.90.refs_9_
  9.5 1.2 broadcast_in_dim.91.refs_10_
  10.8 1.2 broadcast_in_dim.92.refs_11_
  12.0 1.2 broadcast_in_dim.93.refs_12_
  13.2 1.2 broadcast_in_dim.94.refs_13_
  14.5 1.2 broadcast_in_dim.95.refs_14_
  15.7 2.2 convert_reduce_fusion.1
  23.7 111.3 %shard_map.340 = (bf16[2,8,64,768]{3,2,1,0:T(8,128)(2,1)}, bf16[2,8,112,256]{3,2,1,0:T(8,128)(2,1)}, bf16[768,2304]{1,0:T(8,128)(2,1)}, bf16[768,768]{1,0:T(8,12...) custom-call(bf16[10,64,768]{2,1,0:T(8,128)(2,1)} %bitcast.199, ...), custom_call_target="tpu_custom_call" | custom-call | tf_op jit(solution)/shard_map/pallas_call | solution.py:1507
  135.0 1.2 select_bitcast_fusion.2
  147.2 2.7 convert_select_fusion
  150.8 49.9 %shard_map.341 = (bf16[12,768,128]{2,1,0:T(8,128)(2,1)}, bf16[12,768,128]{2,1,0:T(8,128)(2,1)}, bf16[512,256]{1,0:T(8,128)(2,1)}, bf16[10,112,256]{2,1,0:T(8,128)(2,1)}) custom-call(f32[576,256]{1,0:T(8,128)} %bitcast.180, f32[576,256]{1,0:T(8,128)} %copy-done.18, f32[704,256]{1,0:T(8,128)} %get-tuple-element.65.f0_ref, ...), custom_call_target="tpu_custom_call" | custom-call | tf_op jit(solution)/shard_map/pallas_call | solution.py:1218
  200.7 2.1 slice_convert_fusion
  202.8 1.5 reshape.373
  205.5 2.4 copy.72
  208.0 2.4 reshape.363
  210.9 2.4 copy.73
  213.3 3.2 convert_element_type.345
  216.6 2.5 convolution_convert_fusion.7
  219.0 2.7 convert_reduce_fusion.2
  221.7 10.0 %convert_reduce_fusion = (f32[3072]{0:T(1024)S(1)}, bf16[512,3072]{1,0:T(8,128)(2,1)S(1)}) fusion(f32[512,3072]{1,0:T(8,128)} %get-tuple-element.75, bf16[512,768]{1,0:T(8,128)(2,1)S(1)} %get-tuple-element.105, bf16[3072,768]{1,0:T(8,128)(2,1)} %get-tuple-element.74), kind=kOutput, calls=%fused_computation.10 | convolution fusion | flops 2450519040 | bytes 14954496 | tf_op jit(solution)/shard_map/dot_general | solution.py:59
  231.8 4.0 multiply_reduce_fusion.1
  235.8 3.1 fusion.13
  238.9 2.3 collective-permute-start.4
  241.2 3.8 fusion.11
  245.8 0.9 reshape.357.refs_11_
  247.3 1.5 multiply_convert_fusion.1
  251.0 1.7 convolution_convert_fusion.6.refs_5_
  252.7 1.8 convolution_convert_fusion.5
  254.5 1.2 fusion.30
  255.8 6.6 %fusion.8 = bf16[1,3072,384]{2,1,0:T(8,128)(2,1)S(1)} fusion(bf16[1,3072,384]{2,1,0:T(8,128)(2,1)} %collective-permute-done.3, bf16[512,768]{1,0:T(8,128)(2,1)S(1)} %copy-done.17, s32[]{:T(128)S(6)} %select_n.124, f32[512,3072]{1,0:T(8,128)} %get-tuple-element.75), kind=kOutput, calls=%fused_computation.14 | convolution fusion | flops 1228013568 | bytes 11403268 | tf_op jit(solution)/shard_map/dot_general | solution.py:53
  262.3 1.7 dynamic-slice_bitcast_fusion.1
  264.0 1.0 copy-done.32
  265.1 3.4 fusion.7
  268.4 1.6 dynamic-slice_bitcast_fusion
  270.0 0.9 copy-done.8
  271.0 2.7 fusion.9
  273.7 2.3 dynamic-slice_bitcast_fusion.2
  276.0 219.2 %shard_map.342 = (bf16[10,64,768]{2,1,0:T(8,128)(2,1)}, bf16[10,64,768]{2,1,0:T(8,128)(2,1)}, bf16[36,2,2,2,16,256]{5,4,3,2,1,0:T(8,128)(2,1)}, bf16[1,2,2,2,192...) custom-call(bf16[512,768]{1,0:T(8,128)(2,1)} %get-tuple-element.58.r, ...), custom_call_target="tpu_custom_call" | custom-call | tf_op jit(solution)/shard_map/pallas_call | solution.py:991
  497.2 4.4 bitcast_convert_fusion
  501.6 2.9 bitcast_convert_fusion.1
  504.5 2.8 convert.44
  507.3 2.1 bitcast_convert_fusion.2
  509.4 1.5 select_bitcast_fusion
  511.0 1.1 bitcast_convert_fusion.3
  512.1 1.1 select_bitcast_fusion.1
  (175 shorter events, 29.0 us)
Async XLA Ops:
  1.6 16.6 %collective-permute-start = (bf16[128,256]{1,0:T(8,128)(2,1)S(1)}, bf16[128,256]{1,0:T(8,128)(2,1)S(1)}, u32[]{:S(2)}, u32[]{:S(2)}) collective-permute-start(bf16[128,256]{1,0:T(8,128)(2,1)S(1)} %convert_element_type.307), channel_id=1, source_target_pairs={{0,16},{16,0},{1,17},{17,1},{2,18},{18,2},{3,19},{19,3},{4,20},{20... | collective-permute-start | bytes 196616 | tf_op jit(solution)/shard_map/ppermute | solution.py:1613
  5.2 12.8 %collective-permute-start.5 = (bf16[2,128]{1,0:T(2,128)(2,1)S(1)}, bf16[2,128]{1,0:T(2,128)(2,1)S(1)}, u32[]{:S(2)}, u32[]{:S(2)}) collective-permute-start(bf16[2,128]{1,0:T(2,128)(2,1)S(1)} %get-tuple-element.155), channel_id=1, source_target_pairs={{0,16},{16,0},{1,17},{17,1},{2,18},{18,2},{3,19},{19,3},{4,20},{20... | collective-permute-start | bytes 1544 | tf_op jit(solution)/shard_map/ppermute | solution.py:1613
  8.2 9.8 %copy-start.28 = (f32[10]{0:T(128)}, f32[10]{0:T(128)S(1)}, u32[]{:S(2)}) copy-start(f32[10]{0:T(128)S(1)} %multiply_add_fusion.1) | copy-start | bytes 124
  18.0 1.1 copy-start.2
  137.6 1.0 copy-start.13
  142.7 1.4 copy-start
  143.5 2.8 copy-start.7
  143.5 6.5 %collective-permute-start.1 = (f32[576,256]{1,0:T(8,128)S(1)}, f32[576,256]{1,0:T(8,128)S(1)}, u32[]{:S(2)}, u32[]{:S(2)}) collective-permute-start(f32[576,256]{1,0:T(8,128)S(1)} %bitcast.179), channel_id=1, source_target_pairs={{0,4},{4,0},{8,12},{12,8},{1,5},{5,1},{9,13},{13,9},{2,6},{6,2},{1... | collective-permute-start | bytes 1769480 | tf_op jit(solution)/shard_map/ppermute | solution.py:1556
  144.1 2.2 copy-start.21
  144.3 2.0 copy-start.23
  144.3 2.0 copy-start.22
  144.3 2.9 copy-start.27
  144.3 2.9 copy-start.26
  150.0 0.8 copy-start.18
  213.3 5.7 %copy-start.20 = (bf16[768,256]{1,0:T(8,128)(2,1)S(1)}, bf16[768,256]{1,0:T(8,128)(2,1)}, u32[]{:S(2)}) copy-start(bf16[768,256]{1,0:T(8,128)(2,1)} %get-tuple-element.72) | copy-start | bytes 1179652
  216.5 2.5 copy-start.5
  219.0 12.7 %slice-start.2 = ((s8[4718592]{0:T(1024)(128)(4,1)}), s8[4194304]{0:T(1024)(128)(4,1)S(1)}, s32[]{:S(2)}) async-start(s8[4718592]{0:T(1024)(128)(4,1)} %bitcast.218), calls=%async_computation.2 | async-start | bytes 8388608
  219.0 22.2 %slice-start = ((s8[6291456]{0:T(1024)(128)(4,1)}), s8[4194304]{0:T(1024)(128)(4,1)S(1)}, s32[]{:S(2)}) async-start(s8[6291456]{0:T(1024)(128)(4,1)} %bitcast.216), calls=%async_computation | async-start | bytes 8388608
  221.7 19.5 %copy-start.16 = (bf16[512,768]{1,0:T(8,128)(2,1)}, bf16[512,768]{1,0:T(8,128)(2,1)S(1)}, u32[]{:S(2)}) copy-start(bf16[512,768]{1,0:T(8,128)(2,1)S(1)} %get-tuple-element.105) | copy-start | bytes 2359300
  221.7 10.1 %slice-start.3 = ((s8[4718592]{0:T(1024)(128)(4,1)}), s8[524288]{0:T(1024)(128)(4,1)S(1)}, s32[]{:S(2)}) async-start(s8[4718592]{0:T(1024)(128)(4,1)} %bitcast.218), calls=%async_computation.3 | async-start | bytes 1048576
  221.7 19.5 %slice-start.1 = ((s8[6291456]{0:T(1024)(128)(4,1)}), s8[2097152]{0:T(1024)(128)(4,1)S(1)}, s32[]{:S(2)}) async-start(s8[6291456]{0:T(1024)(128)(4,1)} %bitcast.216), calls=%async_computation.1 | async-start | bytes 4194304
  231.7 4.1 copy-start.31
  238.9 25.1 %collective-permute-start.4 = (bf16[1,768,1536]{2,1,0:T(8,128)(2,1)}, bf16[1,768,1536]{2,1,0:T(8,128)(2,1)}, u32[]{:S(2)}, u32[]{:S(2)}) collective-permute-start(bf16[1,768,1536]{2,1,0:T(8,128)(2,1)} %fusion.13), channel_id=1, source_target_pairs={{0,4},{4,0},{8,12},{12,8},{1,5},{5,1},{9,13},{13,9},{2,6},{6,2},{1... | collective-permute-start | bytes 7077896 | tf_op jit(solution)/shard_map/ppermute | solution.py:1556
  245.0 10.7 %collective-permute-start.3 = (bf16[1,3072,384]{2,1,0:T(8,128)(2,1)}, bf16[1,3072,384]{2,1,0:T(8,128)(2,1)}, u32[]{:S(2)}, u32[]{:S(2)}) collective-permute-start(bf16[1,3072,384]{2,1,0:T(8,128)(2,1)} %fusion.11), channel_id=1, source_target_pairs={{0,4},{4,0},{8,12},{12,8},{1,5},{5,1},{9,13},{13,9},{2,6},{6,2},{1... | collective-permute-start | bytes 7077896 | tf_op jit(solution)/shard_map/ppermute | solution.py:1556
  245.1 25.0 %collective-permute-start.2 = (bf16[36,256,128]{2,1,0:T(8,128)(2,1)}, bf16[36,256,128]{2,1,0:T(8,128)(2,1)}, u32[]{:S(2)}, u32[]{:S(2)}) collective-permute-start(bf16[36,256,128]{2,1,0:T(8,128)(2,1)} %bitcast.25), channel_id=1, source_target_pairs={{0,4},{4,0},{8,12},{12,8},{1,5},{5,1},{9,13},{13,9},{2,6},{6,2},{1... | collective-permute-start | bytes 7077896 | tf_op jit(solution)/shard_map/ppermute | solution.py:1556
  246.7 0.7 copy-start.29
  247.3 1.5 copy-start.6
  247.3 2.4 copy-start.12
  249.7 1.3 copy-start.30
  250.2 2.4 copy-start.1
  251.0 1.7 copy-start.4
  252.7 1.9 copy-start.3
  254.5 1.2 copy-start.17
  262.3 2.7 copy-start.32
  268.4 2.5 copy-start.8
  497.2 4.4 copy-start.10
  501.6 2.9 copy-start.9
  504.5 2.8 copy-start.11
  507.3 2.1 copy-start.15
  509.4 1.5 copy-start.19
  509.4 2.7 copy-start.14
  511.0 2.2 copy-start.24
  512.1 1.9 copy-start.25

commit v4 on v3

--- a/solution.py
+++ b/solution.py
@@ -498,8 +498,13 @@
     return dp, lax.div(row, 2), lax.rem(row, 2), col
 
 
-def flip(bit):
-    return 1 - bit
+def slot_of(y, z, cols):
+    return 2 * lax.rem(z + cols + cols // 2 - y, cols) + y
+
+
+def chip_of(slot, cols):
+    y = slot % 2
+    return y, (slot // 2 + cols // 2 + y) % cols
 
 
 def send(src, dst, send_sem, recv_sem, dp, y, core, z):
@@ -524,7 +529,7 @@
     for step in range(chips):
         far_y = lax.rem(y + step // cols, 2)
         far_z = lax.rem(z + step % cols, cols)
-        slot = far_y * cols + far_z
+        slot = slot_of(far_y, far_z, cols)
         copy = send(
             src.at[slot], dst.at[0, own], send_sem.at[step], recv_sem.at[own], dp, far_y, y, far_z
         )
@@ -535,16 +540,16 @@
         else:
             copy.start()
     for extra in range(slots - chips):
-        chip = 2 * chips - slots + extra
+        to_y, to_z = chip_of(2 * chips - slots + extra, cols)
         send(
             src.at[chips + extra],
             dst.at[1, own],
             send_sem.at[chips + extra],
             recv_sem.at[chips + own],
             1 - dp,
-            chip // cols,
+            to_y,
             y,
-            chip % cols,
+            to_z,
         ).start()
 
 
@@ -560,7 +565,7 @@
     for tile in range(chips):
         landed(dst.at[0, tile], recv_sem.at[tile]).wait()
 
-    @pl.when(y * cols + z >= 2 * chips - slots)
+    @pl.when(slot_of(y, z, cols) >= 2 * chips - slots)
     def _():
         for tile in range(chips):
             landed(dst.at[1, tile], recv_sem.at[chips + tile]).wait()
@@ -569,7 +574,7 @@
 def to_tiles_start(src, dst, send_sem, recv_sem, sizes):
     chips, slots, cols = sizes
     dp, y, core, z = place()
-    slot = y * cols + z
+    slot = slot_of(y, z, cols)
     for step in range(chips):
         far_core = lax.rem(core + step // cols, 2)
         far_z = lax.rem(z + step % cols, cols)
@@ -612,7 +617,7 @@
         else:
             left.wait()
 
-    @pl.when(y * cols + z >= 2 * chips - slots)
+    @pl.when(slot_of(y, z, cols) >= 2 * chips - slots)
     def _():
         for step in range(chips):
             landed(src.at[0], send_sem.at[chips + step]).wait()
@@ -693,21 +698,23 @@
 
 
 TURNS = {
-    "conv": ("dp", ("y", "z1", "z2"), ("z2", "z1", "y", "core")),
-    "fc2": ("y", ("z1", "dp", "z2"), ("z2", "y", "z1", "core")),
-    "fc1": ("z1", ("dp", "y", "z2"), ("z2", "y", "z1", "core")),
-    "out": (None, ("y", "z1", "dp", "z2"), ("z2", "y", "z1", "core")),
-    "proj": (None, ("y", "dp", "z1", "z2"), ("z2", "z1", "y", "core")),
-    "head": (None, ("y", "dp", "z1", "z2"), ("z2", "z1", "y", "core")),
-    "qkv": (None, ("dp", "y", "z1", "z2"), ("z2", "z1", "y", "core")),
-    "small": (None, ("z1", "dp", "y", "z2"), ("z2", "y", "z1", "core")),
+    "conv": ("z1", ("dp", "z2", "y"), ("z2", "z1", "y", "core")),
+    "small": (None, ("dp", "y", "z1", "z2"), ("y", "z1", "z2", "core")),
+    "fc1": ("z1", ("y", "dp", "z2"), ("z2", "y", "z1", "core")),
+    "proj": (None, ("dp", "z2", "z1", "y"), ("z1", "y", "z2", "core")),
+    "head": (None, ("dp", "y", "z2", "z1"), ("y", "z2", "z1", "core")),
+    "fc2": ("y", ("dp", "z1", "z2"), ("z2", "z1", "y", "core")),
+    "qkv": (None, ("dp", "y", "z1", "z2"), ("z2", "y", "z1", "core")),
+    "out": (None, ("dp", "y", "z1", "z2"), ("y", "z2", "z1", "core")),
 }
 EARLY = ("conv", "fc2", "fc1")
+ARRIVED = ("conv",)
 WHOLE = ("out", "proj", "head")
 
 
 class Reduce:
-    def __init__(self, turn, near, away, acc, recvs, out, sems):
+    def __init__(self, turn, near, away, acc, recvs, out, sems, arrived=False):
+        self.arrived = arrived
         self.gone, self.sum_order, self.back_order = turn
         self.near, self.away, self.acc, self.recvs, self.out, self.sems = (
             near,
@@ -772,7 +779,10 @@
         elif step == 0:
             if self.near is not None:
                 self.begin(pltpu.make_async_copy(self.near, self.acc, local_sem.at[0]))
-            self.travel(self.away, self.recvs[0], 0, self.gone or "core")
+            if self.arrived:
+                self.begin(pltpu.make_async_copy(self.away, self.recvs[0], local_sem.at[1]))
+            else:
+                self.travel(self.away, self.recvs[0], 0, self.gone or "core")
         elif step < self.forward:
             bit = self.sum_order[step - 1]
             kept[bit] = 1 - bit_of(bit)
@@ -790,6 +800,14 @@
 
     def busy(self):
         return self.step <= self.last + 1
+
+
+def across(value, bit):
+    if bit == "dp":
+        return lax.ppermute(value, "dp", [(0, 1), (1, 0)])
+    if bit == "y":
+        return lax.ppermute(value, "row", [(0, 2), (1, 3), (2, 0), (3, 1)])
+    return lax.ppermute(value, "col", [(i, i + 1 - 2 * (i % 2)) for i in range(4)])
 
 
 def recv_shapes(shape):
@@ -860,6 +878,17 @@
 
 BACK_INPUTS = ("q", "k", "v", "o", "logs", "g", "x", "stream", "w_qkv", "gain", "bias", "small")
 LN_ROWS = 8
+PLAN = (
+    ("fc1", "head", "proj"),
+    ("fc2", "out", "conv"),
+    ("proj", "out", "conv"),
+    (),
+    ("head", "conv", "out"),
+    (),
+    ("out", "proj"),
+    (),
+    ("fc2", "out", "conv"),
+)
 
 
 def backward_kernel(sizes, *refs):
@@ -894,14 +923,15 @@
             )
         else:
             source = (None, outbox[name])
-        jobs[name] = Reduce(TURNS[name], *source, accs[name], recvs[name], outs[name], sems)
+        jobs[name] = Reduce(
+            TURNS[name], *source, accs[name], recvs[name], outs[name], sems, name in ARRIVED
+        )
 
     def tick(*names):
         for name in names:
             jobs[name].tick()
 
-    tick(*EARLY)
-    tick(*WHOLE)
+    tick(*PLAN[0])
     to_tiles_start(tiles, slot_tokens, tile_send.at[0], tile_recv.at[0], sizes)
     rows, width = ref["q"].shape
     for pair in range(width // 128):
@@ -919,8 +949,7 @@
             to = pl.ds(i * width + pair * 128, 128)
             own_pair[:, to] = value[:rows]
             far_out[:, to] = value[rows:].astype(low)
-        if pair == 2:
-            tick(*WHOLE)
+        tick(*PLAN[1 + pair])
     pair_copy = send(far_out, far_in, core_sem.at[0], core_sem.at[1], *mate("core"))
     pair_copy.start()
     stream = ref["x"][...].astype(f32)
@@ -936,9 +965,9 @@
             value = outer_product(normed, part).astype(low)
             target[..., c : c + 384] = value.reshape(target.shape[:-1] + (384,))
         if target is outbox["qkv"]:
-            tick(*EARLY)
+            tick(*PLAN[7])
     tick("qkv")
-    tick(*WHOLE)
+    tick(*PLAN[8])
     grad = back_product(mixed[...], ref["w_qkv"][...])
     gained, grad_gain, grad_bias = norm_back(grad, scaled, factor, ref["gain"][...])
     grad_tile[...] = (ref["stream"][...] + gained).astype(low).reshape(grad_tile.shape)
@@ -1261,7 +1290,7 @@
     return out
 
 
-def forward_kernel(sizes, tiles, *refs):
+def forward_kernel(sizes, tiles, lengths, *refs):
     chips, slots, cols = sizes
     tile_rows, tile_cols = tiles
     refs = list(refs)
@@ -1272,16 +1301,16 @@
 
     tile_in = take(("tokens", "cots", "patches"))
     masters = take(WEIGHTS)
-    vectors = take(VECTORS)
+    vectors = refs.pop(0)
     flag = refs.pop(0)
     image_out = take(("cots", "patches"))
     whole_out = take(WEIGHTS)
-    vector_out = take(VECTORS)
+    vector_out = refs.pop(0)
     saved = take(SAVED)
     maps = take(MAPS)
     image = refs.pop(0)
     whole = take(WEIGHTS)
-    far_vectors = take(VECTORS)
+    far_vectors = refs.pop(0)
     keys, values, f0, hidden_low, flat, wide, stage = (refs.pop(0) for _ in range(7))
     kept = take(("o", "after_attn", "hidden", "first0", "f1", "first1"))
     tile_send, tile_recv, gather_send, gather_recv, vec_send, vec_recv, stage_sem, core_sem, out_sem = refs
@@ -1289,13 +1318,8 @@
     low, f32 = jnp.bfloat16, jnp.float32
 
     to_images_start(tile_in["tokens"], image, tile_send.at[0], tile_recv.at[0], sizes)
-    vector_copies = []
-    for i, name in enumerate(VECTORS):
-        copy = send(
-            vectors[name], far_vectors[name], vec_send.at[i], vec_recv.at[i], *mate("dp")
-        )
-        copy.start()
-        vector_copies.append(copy)
+    vector_copy = send(vectors, far_vectors, vec_send, vec_recv, *mate("dp"))
+    vector_copy.start()
 
     work = [(name, c) for name in WEIGHTS for c in chunks_of(name, masters[name], whole[name], dp)]
     incoming = {}
@@ -1347,16 +1371,17 @@
     round_next("conv")
     tick("out", "qkv", "fc1", "fc2")
     gathers["qkv"].finish()
-    for copy in vector_copies:
-        copy.wait()
-    vec = {}
-    for name in VECTORS:
-        own, far = vectors[name][...], far_vectors[name][...]
+    vector_copy.wait()
+    own, far = vectors[...], far_vectors[...]
+    vec, at = {}, 0
+    for name, length in zip(VECTORS, lengths):
+        part = slice(at, at + length)
         row = jnp.concatenate(
-            [jnp.where(dp == 0, own, far), jnp.where(dp == 0, far, own)], axis=1
+            [jnp.where(dp == 0, own, far)[:, part], jnp.where(dp == 0, far, own)[:, part]], axis=1
         )
         vec[name] = row.astype(low).astype(f32)
-        vector_out[name][...] = vec[name]
+        vector_out[:, 2 * at : 2 * (at + length)] = vec[name]
+        at += length
     to_images_wait(tile_in["tokens"], image, tile_send.at[0], tile_recv.at[0], sizes)
 
     width = image.shape[3]
@@ -1470,6 +1495,7 @@
     tile, width = tile_in[0].shape[1:]
     feat = masters["proj"].shape[1]
     hidden = masters["fc1"].shape[1]
+    lengths = [v.shape[0] for v in vectors]
     rows, line = chips * tile, cols * tiles[1]
     ext = rows + HALO * line
     wholes = {
@@ -1493,25 +1519,25 @@
     out_shape = (
         far[1:]
         + [wholes[name] for name in WEIGHTS]
-        + [shape((1, 2 * vectors[name].shape[1]), f32) for name in VECTORS]
+        + [shape((1, 2 * sum(lengths)), f32)]
         + [saved[name] for name in SAVED]
         + [maps[name] for name in MAPS]
     )
     out_specs = (
         [hbm] * (2 + len(WEIGHTS))
-        + [vmem] * len(VECTORS)
+        + [vmem]
         + [hbm if name in ("k", "v", "o", "after_attn", "hidden") else vmem for name in SAVED]
         + [vmem if name == "coarse" else hbm for name in MAPS]
     )
     n = len(WEIGHTS)
     outs = pl.pallas_call(
-        functools.partial(forward_kernel, sizes, tiles),
+        functools.partial(forward_kernel, sizes, tiles, lengths),
         out_shape=out_shape,
-        in_specs=[hbm] * (3 + n) + [vmem] * (len(VECTORS) + 1),
+        in_specs=[hbm] * (3 + n) + [vmem] * 2,
         out_specs=out_specs,
         scratch_shapes=[pltpu.VMEM(far[0].shape, low)]
         + [pltpu.VMEM(wholes[name].shape, low) for name in WEIGHTS]
-        + [pltpu.VMEM(vectors[name].shape, f32) for name in VECTORS]
+        + [pltpu.VMEM((1, sum(lengths)), f32)]
         + [
             pltpu.VMEM((2 * rows, width), low),
             pltpu.VMEM((2 * rows, width), low),
@@ -1530,8 +1556,8 @@
             pltpu.SemaphoreType.DMA((3, 2 * chips)),
             pltpu.SemaphoreType.DMA((n, 2, 4)),
             pltpu.SemaphoreType.DMA((n, 2, 4)),
-            pltpu.SemaphoreType.DMA((len(VECTORS),)),
-            pltpu.SemaphoreType.DMA((len(VECTORS),)),
+            pltpu.SemaphoreType.DMA,
+            pltpu.SemaphoreType.DMA,
             pltpu.SemaphoreType.DMA((STAGES,)),
             pltpu.SemaphoreType.DMA((2, 3 + HALO)),
             pltpu.SemaphoreType.DMA((n + 9,)),
@@ -1542,13 +1568,18 @@
     )(
         *tile_in,
         *(masters[name] for name in WEIGHTS),
-        *(vectors[name] for name in VECTORS),
+        jnp.concatenate(vectors)[None],
         flag,
     )
     outs = list(outs)
     images = [outs.pop(0) for _ in range(2)]
-    return (images,) + tuple(
-        {name: outs.pop(0) for name in names} for names in (WEIGHTS, VECTORS, SAVED, MAPS)
+    weights = {name: outs.pop(0) for name in WEIGHTS}
+    joined, vec, at = outs.pop(0), {}, 0
+    for name, length in zip(VECTORS, lengths):
+        vec[name] = joined[:, 2 * at : 2 * (at + length)]
+        at += length
+    return (images, weights, vec) + tuple(
+        {name: outs.pop(0) for name in names} for names in (SAVED, MAPS)
     )
 
 
@@ -1603,7 +1634,7 @@
     factor = 0.5 + 0.5 * scale_flags.astype(jnp.float32)
     shift_sign = shift_flags.astype(jnp.float32)
     full_group = count == slots
-    chip = y * cols + z
+    chip = slot_of(y, z, cols)
     borrowed = jnp.logical_and(jnp.logical_not(full_group), chip >= 2 * chips - slots)
     image_present = jnp.where(
         jnp.logical_or(jnp.logical_or(full_group, borrowed), chip < count), 1.0, 0.0
@@ -1641,7 +1672,7 @@
             "proj": proj_w,
             "conv": conv_w.reshape((36,) + conv_w.shape[3:]),
         },
-        {name: v[None] for name, v in zip(VECTORS, vectors)},
+        vectors,
         jnp.full((8, 128), borrowed.astype(jnp.float32)),
         sizes,
         (tile_rows, tile_cols),
@@ -1705,6 +1736,8 @@
     grad_proj = outer_product(tokens_low, proj_grad)
     stream_grad = chosen(image_cots).reshape(rows, width).astype(jnp.float32)
     stream_grad = jnp.where(image_present > 0, stream_grad, 0.0) + back_product(proj_grad, w_proj)
+    grad_conv, stream_grad = lax.optimization_barrier((grad_conv, stream_grad))
+    grad_conv = (grad_conv[0], across(grad_conv[1], TURNS["conv"][0]))
     down_grad = stream_grad.astype(low)
     grad_down_b = jnp.sum(down_grad.astype(jnp.float32), 0)
 

time: 521 us -> 471 us (0.904)
  Pallas kernels: 380 us -> 329 us
  waiting for transfers between devices: 0.02 us -> 6.33 us
    pallas_call x1, Pallas kernels: 219 us -> 172 us  [run_backward(): pl.pallas_call(functools.partial(backward_kernel, sizes), out_shape=out_s...]
    broadcast_in_dim x6 -> x1, local copies, waits for them, and re-layouts: 7.52 us -> 0.61 us  [run_forward(): jnp.concatenate(vectors)[None]]
    ppermute x0 -> x1, waiting for transfers between devices: none -> 6.31 us  [across(): lax.ppermute(value, 'col', [(i, i + 1 - 2 * (i % 2)) for i in range(4)])]
    unnamed x94 -> x99, local copies, waits for them, and re-layouts: 7.71 us -> 10.7 us
  transfers between devices with their start and end apart: 6 -> 7, of which waited for: 0 -> 1; matrix products, arithmetic and copies ran while one was open for 9% -> 12% of each run, Pallas kernels for 0% -> 0%
where the time goes in v4:
time: 471 us; the launch traced here: 466 us
  Pallas kernels  329 us (70%)
  other arithmetic  41.8 us (9%)
  matrix products  39.8 us (8%)
  local copies, waits for them, and re-layouts  39.3 us (8%)
  starting transfers between devices  7.46 us (2%)
  waiting for transfers between devices  6.33 us (1%)
    pallas_call x1, Pallas kernels, run_backward(): pl.pallas_call(functools.partial(backward_kernel, sizes), out_shape=out_s...  172 us
    pallas_call x1, Pallas kernels, run_forward(): pl.pallas_call(functools.partial(forward_kernel, sizes, tiles, lengths),...  111 us
    pallas_call x1, Pallas kernels, maps_backward(): pl.pallas_call(functools.partial(maps_back_kernel, tiles, cols), out_shap...  46 us
    dot_general x7, matrix products, outer_product(): lax.dot_general(first_op, second_op, (((0,), (0,)), ((), ())), preferred_...  22.8 us
    dot_general x5, matrix products, back_product(): lax.dot_general(first_op, weight, (((1,), (1,)), ((), ())), preferred_ele...  16.5 us
    convert_element_type x8, other arithmetic, on_chip(): sums = {name: value.astype(jnp.float32) for name, value in sums.items()}  15.6 us
    unnamed x99, local copies, waits for them, and re-layouts  10.7 us
  transfers between devices with their start and end apart: 7, of which 1 were waited for; matrix products, arithmetic and copies ran while one was open for 12% of the time, Pallas kernels for 0%

profile of v4, /device:TPU:0, one launch (start us, length us, event | category | flops | bytes accessed | tf_op | source)
XLA Modules:
  0.0 466.0 jit_solution(15327476777354446608)
XLA Ops:
  0.7 0.9 convert_element_type.307
  1.6 3.0 collective-permute-start
  5.3 0.9 convert_bitcast_fusion.1
  13.0 2.2 convert_reduce_fusion.1
  19.5 0.9 pad.57.refs_2_
  20.9 110.8 %shard_map.340 = (bf16[2,8,64,768]{3,2,1,0:T(8,128)(2,1)}, bf16[2,8,112,256]{3,2,1,0:T(8,128)(2,1)}, bf16[768,2304]{1,0:T(8,128)(2,1)}, bf16[768,768]{1,0:T(8,12...) custom-call(bf16[10,64,768]{2,1,0:T(8,128)(2,1)} %bitcast.194, ...), custom_call_target="tpu_custom_call" | custom-call | tf_op jit(solution)/shard_map/pallas_call | solution.py:1533
  131.8 1.2 select_bitcast_fusion.2
  141.4 1.0 constant_dynamic-update-slice_fusion.7
  144.1 1.3 fusion.57
  145.4 1.4 convert_select_fusion
  147.6 46.0 %shard_map.341 = (bf16[12,768,128]{2,1,0:T(8,128)(2,1)}, bf16[12,768,128]{2,1,0:T(8,128)(2,1)}, bf16[512,256]{1,0:T(8,128)(2,1)}, bf16[10,112,256]{2,1,0:T(8,128)(2,1)}) custom-call(f32[576,256]{1,0:T(8,128)} %bitcast.179, f32[576,256]{1,0:T(8,128)} %copy-done.19, f32[704,256]{1,0:T(8,128)} %get-tuple-element.64.f0_ref, ...), custom_call_target="tpu_custom_call" | custom-call | tf_op jit(solution)/shard_map/pallas_call | solution.py:1247
  193.6 2.1 slice_convert_fusion
  195.7 1.5 reshape.373
  198.4 2.3 collective-permute-start.2
  200.8 2.4 copy.72
  203.3 2.4 reshape.363
  206.2 1.4 copy.73
  207.6 1.4 convert_element_type.345
  208.9 2.4 convolution_convert_fusion.7
  211.3 1.6 bitcast_add_fusion
  213.6 1.5 multiply_convert_fusion.1
  215.2 1.2 fusion.30
  216.9 3.0 fusion.9
  219.9 2.1 dynamic-slice_bitcast_fusion.4
  222.1 8.6 %convert_reduce_fusion = (f32[3072]{0:T(1024)S(1)}, bf16[512,3072]{1,0:T(8,128)(2,1)S(1)}) fusion(f32[512,3072]{1,0:T(8,128)S(1)} %bitcast.212, bf16[512,768]{1,0:T(8,128)(2,1)S(1)} %get-tuple-element.107, bf16[3072,768]{1,0:T(8,128)(2,1)} %get-tuple-element.77), kind=kOutput, calls=%fused_computation.10 | convolution fusion | flops 2450519040 | bytes 14954496 | tf_op jit(solution)/shard_map/dot_general | solution.py:59
  230.8 4.0 multiply_reduce_fusion.1
  234.8 3.0 fusion.13
  237.9 4.3 fusion.11
  242.9 0.9 reshape.359.refs_11_
  243.8 1.3 collective-permute-start.5
  245.2 2.0 multiply_add_fusion.refs_7_
  247.2 1.7 convolution_convert_fusion.6.refs_5_
  249.5 1.9 convolution_convert_fusion.5
  251.4 6.6 %fusion.8 = bf16[1,3072,384]{2,1,0:T(8,128)(2,1)S(1)} fusion(bf16[1,3072,384]{2,1,0:T(8,128)(2,1)} %collective-permute-done.3, bf16[512,768]{1,0:T(8,128)(2,1)S(1)} %copy-done.18, s32[]{:T(128)S(6)} %select_n.121, f32[512,3072]{1,0:T(8,128)} %get-tuple-element.78), kind=kOutput, calls=%fused_computation.14 | convolution fusion | flops 1228013568 | bytes 11403268 | tf_op jit(solution)/shard_map/dot_general | solution.py:53
  258.0 1.7 dynamic-slice_bitcast_fusion.1
  259.7 1.0 copy-done.33
  260.7 3.4 fusion.7
  264.1 1.6 dynamic-slice_bitcast_fusion
  265.6 6.3 %collective-permute-done.5.refs_16_ = bf16[36,2,2,2,16,128]{5,4,3,2,1,0:T(8,128)(2,1)S(1)} collective-permute-done((bf16[36,2,2,2,16,128]{5,4,3,2,1,0:T(8,128)(2,1)}, bf16[36,2,2,2,16,128]{5,4,3,2,1,0:T(8,128)(2,1)S(1)}, u32[]{:S(2)}, u32[]{:S(2)}) %collective-permute-start.5) | collective-permute-done | bytes 1179680 | tf_op jit(solution)/shard_map/ppermute | solution.py:810
  272.0 1.0 copy-done.14
  273.0 172.0 %shard_map.342 = (bf16[10,64,768]{2,1,0:T(8,128)(2,1)}, bf16[10,64,768]{2,1,0:T(8,128)(2,1)}, bf16[36,2,2,2,16,256]{5,4,3,2,1,0:T(8,128)(2,1)}, bf16[1,2,2,2,16,...) custom-call(bf16[512,768]{1,0:T(8,128)(2,1)} %get-tuple-element.58.r, ...), custom_call_target="tpu_custom_call" | custom-call | tf_op jit(solution)/shard_map/pallas_call | solution.py:1020
  447.0 4.4 bitcast_convert_fusion
  451.4 2.9 bitcast_convert_fusion.1
  454.3 2.8 convert.44
  457.1 2.1 bitcast_convert_fusion.2
  459.2 1.5 select_bitcast_fusion
  460.7 1.1 bitcast_convert_fusion.3
  461.9 1.1 select_bitcast_fusion.1
  (181 shorter events, 31.3 us)
Async XLA Ops:
  1.6 13.8 %collective-permute-start = (bf16[128,256]{1,0:T(8,128)(2,1)S(1)}, bf16[128,256]{1,0:T(8,128)(2,1)S(1)}, u32[]{:S(2)}, u32[]{:S(2)}) collective-permute-start(bf16[128,256]{1,0:T(8,128)(2,1)S(1)} %convert_element_type.307), channel_id=1, source_target_pairs={{0,16},{16,0},{1,17},{17,1},{2,18},{18,2},{3,19},{19,3},{4,20},{20... | collective-permute-start | bytes 196616 | tf_op jit(solution)/shard_map/ppermute | solution.py:1644
  5.2 10.0 %collective-permute-start.6 = (bf16[2,128]{1,0:T(2,128)(2,1)S(1)}, bf16[2,128]{1,0:T(2,128)(2,1)S(1)}, u32[]{:S(2)}, u32[]{:S(2)}) collective-permute-start(bf16[2,128]{1,0:T(2,128)(2,1)S(1)} %get-tuple-element.161), channel_id=1, source_target_pairs={{0,16},{16,0},{1,17},{17,1},{2,18},{18,2},{3,19},{19,3},{4,20},{20... | collective-permute-start | bytes 1544 | tf_op jit(solution)/shard_map/ppermute | solution.py:1644
  6.9 9.0 %copy-start.27 = (f32[10]{0:T(128)}, f32[10]{0:T(128)S(1)}, u32[]{:S(2)}) copy-start(f32[10]{0:T(128)S(1)} %compare_convert_fusion) | copy-start | bytes 124
  8.2 7.7 %copy-start.29 = (f32[10]{0:T(128)}, f32[10]{0:T(128)S(1)}, u32[]{:S(2)}) copy-start(f32[10]{0:T(128)S(1)} %multiply_add_fusion.1) | copy-start | bytes 124
  15.2 1.1 copy-start.2
  134.4 1.0 copy-start.13
  139.5 1.4 copy-start
  140.3 2.9 copy-start.7
  140.3 6.5 %collective-permute-start.1 = (f32[576,256]{1,0:T(8,128)S(1)}, f32[576,256]{1,0:T(8,128)S(1)}, u32[]{:S(2)}, u32[]{:S(2)}) collective-permute-start(f32[576,256]{1,0:T(8,128)S(1)} %bitcast.178), channel_id=1, source_target_pairs={{0,4},{4,0},{8,12},{12,8},{1,5},{5,1},{9,13},{13,9},{2,6},{6,2},{1... | collective-permute-start | bytes 1769480 | tf_op jit(solution)/shard_map/ppermute | solution.py:1587
  140.9 2.3 copy-start.22
  141.1 2.1 copy-start.24
  141.1 2.2 copy-start.23
  141.1 4.3 copy-start.12
  146.8 0.8 copy-start.19
  198.4 18.0 %collective-permute-start.2 = (bf16[36,256,128]{2,1,0:T(8,128)(2,1)}, bf16[36,256,128]{2,1,0:T(8,128)(2,1)}, u32[]{:S(2)}, u32[]{:S(2)}) collective-permute-start(bf16[36,256,128]{2,1,0:T(8,128)(2,1)} %bitcast.21), channel_id=1, source_target_pairs={{0,4},{4,0},{8,12},{12,8},{1,5},{5,1},{9,13},{13,9},{2,6},{6,2},{1... | collective-permute-start | bytes 7077896 | tf_op jit(solution)/shard_map/ppermute | solution.py:1587
  207.5 1.4 copy-start.21
  208.9 2.4 copy-start.6
  211.3 1.6 copy-start.4
  212.9 0.7 copy-start.28
  212.9 0.7 copy-start.30
  213.6 1.5 copy-start.3
  215.2 1.7 copy-start.8
  215.2 6.9 %slice-start = ((s8[6291456]{0:T(1024)(128)(4,1)}), s8[4194304]{0:T(1024)(128)(4,1)S(1)}, s32[]{:S(2)}) async-start(s8[6291456]{0:T(1024)(128)(4,1)} %bitcast.211), calls=%async_computation | async-start | bytes 8388608
  216.9 5.2 %slice-start.1 = ((s8[6291456]{0:T(1024)(128)(4,1)}), s8[2097152]{0:T(1024)(128)(4,1)S(1)}, s32[]{:S(2)}) async-start(s8[6291456]{0:T(1024)(128)(4,1)} %bitcast.211), calls=%async_computation.1 | async-start | bytes 4194304
  221.9 8.8 %slice-start.2 = ((s8[4718592]{0:T(1024)(128)(4,1)}), s8[4194304]{0:T(1024)(128)(4,1)S(1)}, s32[]{:S(2)}) async-start(s8[4718592]{0:T(1024)(128)(4,1)} %bitcast.213), calls=%async_computation.2 | async-start | bytes 8388608
  222.1 15.8 %copy-start.17 = (bf16[512,768]{1,0:T(8,128)(2,1)}, bf16[512,768]{1,0:T(8,128)(2,1)S(1)}, u32[]{:S(2)}) copy-start(bf16[512,768]{1,0:T(8,128)(2,1)S(1)} %get-tuple-element.107) | copy-start | bytes 2359300
  222.1 8.6 %slice-start.3 = ((s8[4718592]{0:T(1024)(128)(4,1)}), s8[524288]{0:T(1024)(128)(4,1)S(1)}, s32[]{:S(2)}) async-start(s8[4718592]{0:T(1024)(128)(4,1)} %bitcast.213), calls=%async_computation.3 | async-start | bytes 1048576
  230.7 4.1 copy-start.32
  237.9 21.8 %collective-permute-start.4 = (bf16[1,768,1536]{2,1,0:T(8,128)(2,1)}, bf16[1,768,1536]{2,1,0:T(8,128)(2,1)}, u32[]{:S(2)}, u32[]{:S(2)}) collective-permute-start(bf16[1,768,1536]{2,1,0:T(8,128)(2,1)} %fusion.13), channel_id=1, source_target_pairs={{0,4},{4,0},{8,12},{12,8},{1,5},{5,1},{9,13},{13,9},{2,6},{6,2},{1... | collective-permute-start | bytes 7077896 | tf_op jit(solution)/shard_map/ppermute | solution.py:1587
  242.2 9.2 %collective-permute-start.3 = (bf16[1,3072,384]{2,1,0:T(8,128)(2,1)}, bf16[1,3072,384]{2,1,0:T(8,128)(2,1)}, u32[]{:S(2)}, u32[]{:S(2)}) collective-permute-start(bf16[1,3072,384]{2,1,0:T(8,128)(2,1)} %fusion.11), channel_id=1, source_target_pairs={{0,4},{4,0},{8,12},{12,8},{1,5},{5,1},{9,13},{13,9},{2,6},{6,2},{1... | collective-permute-start | bytes 7077896 | tf_op jit(solution)/shard_map/ppermute | solution.py:1587
  243.8 28.1 %collective-permute-start.5 = (bf16[36,2,2,2,16,128]{5,4,3,2,1,0:T(8,128)(2,1)}, bf16[36,2,2,2,16,128]{5,4,3,2,1,0:T(8,128)(2,1)S(1)}, u32[]{:S(2)}, u32[]{:S(2)}) collective-permute-start(bf16[36,2,2,2,16,128]{5,4,3,2,1,0:T(8,128)(2,1)} %get-tuple-element.86), channel_id=1, source_target_pairs={{0,1},{1,0},{2,3},{3,2},{4,5},{5,4},{6,7},{7,6},{8,9},{9,8},{10,11... | collective-permute-start | bytes 3538952 | tf_op jit(solution)/shard_map/ppermute | solution.py:810
  245.2 2.0 copy-start.31
  247.2 1.7 copy-start.1
  247.2 2.3 copy-start.5
  249.5 2.0 copy-start.18
  258.0 2.7 copy-start.33
  272.0 1.0 copy-start.14
  447.0 4.4 copy-start.10
  451.4 2.9 copy-start.9
  454.3 2.8 copy-start.11
  457.1 2.1 copy-start.16
  459.2 1.5 copy-start.20
  459.2 2.7 copy-start.15
  460.7 2.2 copy-start.25
  461.9 1.9 copy-start.26

commit v5 on v4

--- a/solution.py
+++ b/solution.py
@@ -660,7 +660,7 @@
         if split:
             self.orders = (("core", "y", "z1"), ("core", "z1", "y"))
         else:
-            self.orders = (("core", "y"),)
+            self.orders = (("core", "y"), ("core", "z1"))
         self.next, self.copies = 0, []
 
     def at(self, step, side):
@@ -1424,6 +1424,8 @@
             saved["logs"][pair, h : h + 1, :] = logs[h]
         if pair == 1:
             tick("out")
+        if pair == 3:
+            tick("fc2")
     gathers["out"].finish()
     tick("fc2", "conv", "proj")
     to_images_start(tile_in["cots"], image_out["cots"], tile_send.at[2], tile_recv.at[2], sizes)
@@ -1441,6 +1443,8 @@
         hidden = hidden + vec["fc1_b"][:, c : c + width]
         kept["hidden"][:, part] = hidden
         hidden_low[:, part] = jax.nn.gelu(hidden).astype(low)
+        if c == width:
+            tick("conv", "proj")
     keep(kept["hidden"], saved["hidden"])
     gathers["fc2"].finish()
     after_mlp = kept["after_attn"][...] + (
@@ -1448,7 +1452,6 @@
     )
     tokens_low = after_mlp.astype(low)
     saved["tokens_low"][...] = tokens_low
-    tick("conv")
     gathers["proj"].finish()
 
     flat[...] = jnp.dot(tokens_low, whole["proj"][...], preferred_element_type=f32)
@@ -1715,6 +1718,40 @@
     )
     grad_conv = early_sum(*(g.reshape(36, feat, feat // 2) for g in grad_conv), TURNS["conv"][0])
 
+    normed_two, scaled_two, factor_two = norm_rows(saved["after_attn"], gain_two, bias_two)
+    normed_two_low = normed_two.astype(low)
+    hidden = saved["hidden"]
+    hidden_low = jax.nn.gelu(hidden).astype(low)
+    attended = saved["o"].astype(low)
+    grad_proj = outer_product(tokens_low, proj_grad)
+    stream_grad = chosen(image_cots).reshape(rows, width).astype(jnp.float32)
+    stream_grad = jnp.where(image_present > 0, stream_grad, 0.0) + back_product(proj_grad, w_proj)
+    grad_conv, stream_grad = lax.optimization_barrier((grad_conv, stream_grad))
+    grad_conv = (grad_conv[0], across(grad_conv[1], TURNS["conv"][0]))
+    down_grad = stream_grad.astype(low)
+    grad_down_b = jnp.sum(down_grad.astype(jnp.float32), 0)
+
+    def halves_of(first_op, second_op):
+        half = second_op.shape[1] // 2
+        return [
+            outer_product(
+                first_op, lax.dynamic_slice_in_dim(second_op, side * half, half, 1)
+            ).astype(low)[None]
+            for side in (core, 1 - core)
+        ]
+
+    grad_down_w = early_sum(*halves_of(hidden_low, down_grad), TURNS["fc2"][0])
+    up_grad = gelu_grad(hidden, back_product(down_grad, w_down)).astype(low)
+    grad_up_b = jnp.sum(up_grad.astype(jnp.float32), 0)
+    grad_up_w = early_sum(*halves_of(normed_two_low, up_grad), TURNS["fc1"][0])
+    norm_grad, grad_gain_two, grad_bias_two = norm_back(
+        back_product(up_grad, w_up), scaled_two, factor_two, gain_two
+    )
+    stream_grad = stream_grad + norm_grad
+    branch_grad = stream_grad.astype(low)
+    grad_out_w = outer_product(attended, branch_grad)
+    attended_grad = back_product(branch_grad, w_out).astype(low)
+    slot_patch, grad_up_b = lax.optimization_barrier((slot_patch, grad_up_b))
     patch = slot_patch[:, :cells]
     patch = patch.reshape(slots, tile_rows + 2, tile_cols + 2, feat).astype(jnp.float32)
     patch = jnp.where(present[:, None, None, None] > 0, patch, 0.0)
@@ -1728,39 +1765,6 @@
     merged_out = merged.astype(low).reshape(cot_merged.shape)
     grad_head_w = outer_product(fine_rows, head_grad)
 
-    normed_two, scaled_two, factor_two = norm_rows(saved["after_attn"], gain_two, bias_two)
-    normed_two_low = normed_two.astype(low)
-    hidden = saved["hidden"]
-    hidden_low = jax.nn.gelu(hidden).astype(low)
-    attended = saved["o"].astype(low)
-    grad_proj = outer_product(tokens_low, proj_grad)
-    stream_grad = chosen(image_cots).reshape(rows, width).astype(jnp.float32)
-    stream_grad = jnp.where(image_present > 0, stream_grad, 0.0) + back_product(proj_grad, w_proj)
-    grad_conv, stream_grad = lax.optimization_barrier((grad_conv, stream_grad))
-    grad_conv = (grad_conv[0], across(grad_conv[1], TURNS["conv"][0]))
-    down_grad = stream_grad.astype(low)
-    grad_down_b = jnp.sum(down_grad.astype(jnp.float32), 0)
-
-    def halves_of(first_op, second_op):
-        half = second_op.shape[1] // 2
-        return [
-            outer_product(
-                first_op, lax.dynamic_slice_in_dim(second_op, side * half, half, 1)
-            ).astype(low)[None]
-            for side in (core, 1 - core)
-        ]
-
-    grad_down_w = early_sum(*halves_of(hidden_low, down_grad), TURNS["fc2"][0])
-    up_grad = gelu_grad(hidden, back_product(down_grad, w_down)).astype(low)
-    grad_up_b = jnp.sum(up_grad.astype(jnp.float32), 0)
-    grad_up_w = early_sum(*halves_of(normed_two_low, up_grad), TURNS["fc1"][0])
-    norm_grad, grad_gain_two, grad_bias_two = norm_back(
-        back_product(up_grad, w_up), scaled_two, factor_two, gain_two
-    )
-    stream_grad = stream_grad + norm_grad
-    branch_grad = stream_grad.astype(low)
-    grad_out_w = outer_product(attended, branch_grad)
-    attended_grad = back_product(branch_grad, w_out).astype(low)
     blank = jnp.zeros((2, (width // 2 + feat - 1) // feat * feat), jnp.float32)
     packed = []
     for v in (grad_up_b, grad_down_b, None, None, grad_gain_two, grad_bias_two, grad_head_b, grad_shift):

time: 471 us -> 455 us (0.966)
  Pallas kernels: 329 us -> 316 us
    pallas_call x1, Pallas kernels: 46 us -> 39.2 us  [maps_backward(): pl.pallas_call(functools.partial(maps_back_kernel, tiles, cols), out_shap...]
    pallas_call x1, Pallas kernels: 111 us -> 104 us  [run_forward(): pl.pallas_call(functools.partial(forward_kernel, sizes, tiles, lengths),...]
    unnamed x99 -> x101, local copies, waits for them, and re-layouts: 10.7 us -> 9.95 us
  transfers between devices with their start and end apart: 7 -> 7, of which waited for: 1 -> 3; matrix products, arithmetic and copies ran while one was open for 12% -> 12% of each run, Pallas kernels for 0% -> 32%
where the time goes in v5:
time: 455 us; the launch traced here: 450 us
  Pallas kernels  316 us (69%)
  matrix products  42.8 us (9%)
  other arithmetic  39.1 us (9%)
  local copies, waits for them, and re-layouts  37.8 us (8%)
  starting transfers between devices  7.63 us (2%)
  waiting for transfers between devices  4.59 us (1%)
    pallas_call x1, Pallas kernels, run_backward(): pl.pallas_call(functools.partial(backward_kernel, sizes), out_shape=out_s...  172 us
    pallas_call x1, Pallas kernels, run_forward(): pl.pallas_call(functools.partial(forward_kernel, sizes, tiles, lengths),...  104 us
    pallas_call x1, Pallas kernels, maps_backward(): pl.pallas_call(functools.partial(maps_back_kernel, tiles, cols), out_shap...  39.2 us
    dot_general x7, matrix products, outer_product(): lax.dot_general(first_op, second_op, (((0,), (0,)), ((), ())), preferred_...  24.5 us
    dot_general x5, matrix products, back_product(): lax.dot_general(first_op, weight, (((1,), (1,)), ((), ())), preferred_ele...  17.7 us
    convert_element_type x8, other arithmetic, on_chip(): sums = {name: value.astype(jnp.float32) for name, value in sums.items()}  15.6 us
    unnamed x101, local copies, waits for them, and re-layouts  9.95 us
  transfers between devices with their start and end apart: 7, of which 3 were waited for; matrix products, arithmetic and copies ran while one was open for 12% of the time, Pallas kernels for 32%

profile of v5, /device:TPU:0, one launch (start us, length us, event | category | flops | bytes accessed | tf_op | source)
XLA Modules:
  0.0 449.9 jit_solution(8175079193625581396)
XLA Ops:
  0.7 0.9 convert_element_type.307
  1.6 3.0 collective-permute-start
  5.3 0.9 convert_bitcast_fusion.1
  11.7 2.2 convert_reduce_fusion.1
  18.7 0.9 pad.57.refs_2_
  20.2 104.1 %shard_map.340 = (bf16[2,8,64,768]{3,2,1,0:T(8,128)(2,1)}, bf16[2,8,112,256]{3,2,1,0:T(8,128)(2,1)}, bf16[768,2304]{1,0:T(8,128)(2,1)}, bf16[768,768]{1,0:T(8,12...) custom-call(bf16[10,64,768]{2,1,0:T(8,128)(2,1)} %bitcast.194, ...), custom_call_target="tpu_custom_call" | custom-call | tf_op jit(solution)/shard_map/pallas_call | solution.py:1536
  124.3 1.2 select_bitcast_fusion.2
  131.6 0.8 copy-done.24
  132.5 39.2 %shard_map.341 = (bf16[12,768,128]{2,1,0:T(8,128)(2,1)}, bf16[12,768,128]{2,1,0:T(8,128)(2,1)}, bf16[512,256]{1,0:T(8,128)(2,1)}, bf16[10,112,256]{2,1,0:T(8,128)(2,1)}) custom-call(f32[576,256]{1,0:T(8,128)} %bitcast.179, f32[576,256]{1,0:T(8,128)} %copy-done.24, f32[704,256]{1,0:T(8,128)} %get-tuple-element.66.f0_ref, ...), custom_call_target="tpu_custom_call" | custom-call | tf_op jit(solution)/shard_map/pallas_call | solution.py:1247
  171.7 2.3 collective-permute-start.2
  174.6 1.4 fusion.57
  176.3 1.2 convolution_convert_fusion.7
  178.5 1.1 copy-done.10
  179.7 3.9 fusion.9
  183.6 2.1 dynamic-slice_bitcast_fusion.4
  185.9 7.3 %convert_reduce_fusion = (f32[3072]{0:T(1024)S(1)}, bf16[512,3072]{1,0:T(8,128)(2,1)}) fusion(f32[512,3072]{1,0:T(8,128)S(1)} %bitcast.212, bf16[512,768]{1,0:T(8,128)(2,1)S(1)} %get-tuple-element.111, bf16[3072,768]{1,0:T(8,128)(2,1)S(1)} %bitcast.214), kind=kOutput, calls=%fused_computation.10 | convolution fusion | flops 2450519040 | bytes 14954496 | tf_op jit(solution)/shard_map/dot_general | solution.py:59
  193.2 1.0 slice_convert_fusion
  194.2 1.3 reshape.373
  195.6 0.8 fusion.18
  196.8 2.4 copy.72
  199.2 2.4 reshape.363
  202.1 2.4 copy.73
  204.5 3.4 convert_element_type.345
  207.9 7.8 %multiply_reduce_fusion.1 = (f32[768]{0:T(1024)S(1)}, f32[512]{0:T(512)S(1)}, f32[512]{0:T(512)S(1)}, f32[768]{0:T(1024)S(1)}, f32[512,768]{1,0:T(8,128)}) fusion(f32[512,768]{1,0:T(8,128)S(1)} %copy-done, f32[512]{0:T(512)S(1)} %add_rsqrt_fusion, f32[512]{0:T(512)S(1)} %broadcast_multiply_fusion.5, f32[768]{0:T(1024)S(1)} %get-tuple-element.160, ...), kind=kOutput, calls=%fused_computation.50 | convolution fusion | flops 2419455488 | bytes 11027456 | tf_op jit(solution)/shard_map/dot_general | solution.py:59
  215.7 3.1 fusion.13
  218.9 7.0 %fusion.11 = bf16[1,3072,384]{2,1,0:T(8,128)(2,1)} fusion(bf16[512,768]{1,0:T(8,128)(2,1)S(1)} %copy-done.22, s32[]{:T(128)S(6)} %select_n.122, f32[512,3072]{1,0:T(8,128)} %get-tuple-element.80), kind=kOutput, calls=%fused_computation.21 | convolution fusion | flops 1223294976 | bytes 9043972 | tf_op jit(solution)/shard_map/dot_general | solution.py:53
  226.5 0.9 reshape.359.refs_11_
  227.4 1.3 collective-permute-start.5
  229.3 1.6 multiply_convert_fusion.1
  232.9 1.7 convolution_convert_fusion.6.refs_5_
  234.6 2.0 convolution_convert_fusion.5
  236.6 1.2 fusion.30
  237.8 6.8 %fusion.8 = bf16[1,3072,384]{2,1,0:T(8,128)(2,1)S(1)} fusion(bf16[1,3072,384]{2,1,0:T(8,128)(2,1)} %collective-permute-done.3, bf16[512,768]{1,0:T(8,128)(2,1)S(1)} %copy-done.23, s32[]{:T(128)S(6)} %select_n.121, f32[512,3072]{1,0:T(8,128)} %get-tuple-element.80), kind=kOutput, calls=%fused_computation.14 | convolution fusion | flops 1228013568 | bytes 11403268 | tf_op jit(solution)/shard_map/dot_general | solution.py:53
  244.6 1.7 dynamic-slice_bitcast_fusion.1
  246.3 1.0 copy-done.34
  247.3 3.4 fusion.7
  250.7 1.6 dynamic-slice_bitcast_fusion
  252.3 3.3 collective-permute-done.5.refs_16_
  255.6 1.0 copy-done.17
  256.6 172.4 %shard_map.342 = (bf16[10,64,768]{2,1,0:T(8,128)(2,1)}, bf16[10,64,768]{2,1,0:T(8,128)(2,1)}, bf16[36,2,2,2,16,256]{5,4,3,2,1,0:T(8,128)(2,1)}, bf16[1,2,2,2,16,...) custom-call(bf16[512,768]{1,0:T(8,128)(2,1)} %get-tuple-element.60.r, ...), custom_call_target="tpu_custom_call" | custom-call | tf_op jit(solution)/shard_map/pallas_call | solution.py:1020
  429.0 0.9 convert_element_type.381
  431.1 4.4 bitcast_convert_fusion
  435.4 2.9 bitcast_convert_fusion.1
  438.3 2.8 convert.44
  441.1 2.1 bitcast_convert_fusion.2
  443.3 1.5 select_bitcast_fusion
  444.8 1.1 bitcast_convert_fusion.3
  445.9 1.1 select_bitcast_fusion.1
  (183 shorter events, 26.7 us)
Async XLA Ops:
  0.7 13.3 %copy-start.31 = (f32[384]{0:T(512)S(1)}, f32[384]{0:T(512)}, u32[]{:S(2)}) copy-start(f32[384]{0:T(512)} %param.36) | copy-start | bytes 4612
  1.6 13.0 %collective-permute-start = (bf16[128,256]{1,0:T(8,128)(2,1)S(1)}, bf16[128,256]{1,0:T(8,128)(2,1)S(1)}, u32[]{:S(2)}, u32[]{:S(2)}) collective-permute-start(bf16[128,256]{1,0:T(8,128)(2,1)S(1)} %convert_element_type.307), channel_id=1, source_target_pairs={{0,16},{16,0},{1,17},{17,1},{2,18},{18,2},{3,19},{19,3},{4,20},{20... | collective-permute-start | bytes 196616 | tf_op jit(solution)/shard_map/ppermute | solution.py:1647
  5.3 168.8 %collective-permute-start.6 = (bf16[2,128]{1,0:T(2,128)(2,1)S(1)}, bf16[2,128]{1,0:T(2,128)(2,1)S(1)}, u32[]{:S(2)}, u32[]{:S(2)}) collective-permute-start(bf16[2,128]{1,0:T(2,128)(2,1)S(1)} %get-tuple-element.165), channel_id=1, source_target_pairs={{0,16},{16,0},{1,17},{17,1},{2,18},{18,2},{3,19},{19,3},{4,20},{20... | collective-permute-start | bytes 1544 | tf_op jit(solution)/shard_map/ppermute | solution.py:1647
  13.9 1.6 copy-start.4
  126.9 1.0 copy-start.16
  129.6 2.1 copy-start.9
  129.6 2.1 collective-permute-start.1
  131.6 0.8 copy-start.24
  132.5 41.7 %copy-start = (f32[512,768]{1,0:T(8,128)S(1)}, f32[512,768]{1,0:T(8,128)}, u32[]{:S(2)}) copy-start(f32[512,768]{1,0:T(8,128)} %get-tuple-element.78) | copy-start | bytes 4718596
  171.7 4.3 copy-start.14
  171.7 6.8 %collective-permute-start.2 = (bf16[36,256,128]{2,1,0:T(8,128)(2,1)}, bf16[36,256,128]{2,1,0:T(8,128)(2,1)}, u32[]{:S(2)}, u32[]{:S(2)}) collective-permute-start(bf16[36,256,128]{2,1,0:T(8,128)(2,1)} %bitcast.215), channel_id=1, source_target_pairs={{0,4},{4,0},{8,12},{12,8},{1,5},{5,1},{9,13},{13,9},{2,6},{6,2},{1... | collective-permute-start | bytes 7077896 | tf_op jit(solution)/shard_map/ppermute | solution.py:1590
  174.6 1.6 copy-start.20
  174.6 1.6 copy-start.28
  176.2 1.2 copy-start.27
  177.4 2.2 copy-start.10
  177.4 8.4 %slice-start = ((s8[6291456]{0:T(1024)(128)(4,1)}), s8[4194304]{0:T(1024)(128)(4,1)S(1)}, s32[]{:S(2)}) async-start(s8[6291456]{0:T(1024)(128)(4,1)} %bitcast.211), calls=%async_computation | async-start | bytes 8388608
  177.4 8.4 %slice-start.2 = ((s8[4718592]{0:T(1024)(128)(4,1)}), s8[4194304]{0:T(1024)(128)(4,1)S(1)}, s32[]{:S(2)}) async-start(s8[4718592]{0:T(1024)(128)(4,1)} %bitcast.213), calls=%async_computation.2 | async-start | bytes 8388608
  177.8 7.8 %copy-start.2 = (f32[512,768]{1,0:T(8,128)}, f32[512,768]{1,0:T(8,128)S(1)}, u32[]{:S(2)}) copy-start(f32[512,768]{1,0:T(8,128)S(1)} %bitcast_add_fusion) | copy-start | bytes 4718596
  179.7 6.2 %slice-start.1 = ((s8[6291456]{0:T(1024)(128)(4,1)}), s8[2097152]{0:T(1024)(128)(4,1)S(1)}, s32[]{:S(2)}) async-start(s8[6291456]{0:T(1024)(128)(4,1)} %bitcast.211), calls=%async_computation.1 | async-start | bytes 4194304
  179.7 6.2 %slice-start.3 = ((s8[4718592]{0:T(1024)(128)(4,1)}), s8[524288]{0:T(1024)(128)(4,1)S(1)}, s32[]{:S(2)}) async-start(s8[4718592]{0:T(1024)(128)(4,1)} %bitcast.213), calls=%async_computation.3 | async-start | bytes 1048576
  185.8 7.4 %copy-start.21 = (bf16[512,768]{1,0:T(8,128)(2,1)}, bf16[512,768]{1,0:T(8,128)(2,1)S(1)}, u32[]{:S(2)}) copy-start(bf16[512,768]{1,0:T(8,128)(2,1)S(1)} %get-tuple-element.111) | copy-start | bytes 2359300
  185.9 7.3 %copy-start.26 = (bf16[10,112,256]{2,1,0:T(8,128)(2,1)S(1)}, bf16[10,112,256]{2,1,0:T(8,128)(2,1)}, u32[]{:S(2)}) copy-start(bf16[10,112,256]{2,1,0:T(8,128)(2,1)} %get-tuple-element.91) | copy-start | bytes 1720324
  207.9 20.8 %copy-start.6 = (bf16[16,10,16,256]{3,0,2,1:T(8,128)(2,1)}, bf16[16,10,16,256]{3,0,2,1:T(8,128)(2,1)S(1)}, u32[]{:S(2)}) copy-start(bf16[16,10,16,256]{3,0,2,1:T(8,128)(2,1)S(1)} %convert_element_type.345) | copy-start | bytes 3932164
  207.9 7.8 %copy-start.33 = (bf16[512,3072]{1,0:T(8,128)(2,1)S(1)}, bf16[512,3072]{1,0:T(8,128)(2,1)}, u32[]{:S(2)}) copy-start(bf16[512,3072]{1,0:T(8,128)(2,1)} %get-tuple-element.113) | copy-start | bytes 9437188
  215.7 3.2 copy-start.22
  218.8 27.5 %collective-permute-start.4 = (bf16[1,768,1536]{2,1,0:T(8,128)(2,1)}, bf16[1,768,1536]{2,1,0:T(8,128)(2,1)}, u32[]{:S(2)}, u32[]{:S(2)}) collective-permute-start(bf16[1,768,1536]{2,1,0:T(8,128)(2,1)} %fusion.13), channel_id=1, source_target_pairs={{0,4},{4,0},{8,12},{12,8},{1,5},{5,1},{9,13},{13,9},{2,6},{6,2},{1... | collective-permute-start | bytes 7077896 | tf_op jit(solution)/shard_map/ppermute | solution.py:1590
  225.9 11.9 %collective-permute-start.3 = (bf16[1,3072,384]{2,1,0:T(8,128)(2,1)}, bf16[1,3072,384]{2,1,0:T(8,128)(2,1)}, u32[]{:S(2)}, u32[]{:S(2)}) collective-permute-start(bf16[1,3072,384]{2,1,0:T(8,128)(2,1)} %fusion.11), channel_id=1, source_target_pairs={{0,4},{4,0},{8,12},{12,8},{1,5},{5,1},{9,13},{13,9},{2,6},{6,2},{1... | collective-permute-start | bytes 7077896 | tf_op jit(solution)/shard_map/ppermute | solution.py:1590
  227.4 28.2 %collective-permute-start.5 = (bf16[36,2,2,2,16,128]{5,4,3,2,1,0:T(8,128)(2,1)}, bf16[36,2,2,2,16,128]{5,4,3,2,1,0:T(8,128)(2,1)S(1)}, u32[]{:S(2)}, u32[]{:S(2)}) collective-permute-start(bf16[36,2,2,2,16,128]{5,4,3,2,1,0:T(8,128)(2,1)} %get-tuple-element.90), channel_id=1, source_target_pairs={{0,1},{1,0},{2,3},{3,2},{4,5},{5,4},{6,7},{7,6},{8,9},{9,8},{10,11... | collective-permute-start | bytes 3538952 | tf_op jit(solution)/shard_map/ppermute | solution.py:810
  229.3 1.6 copy-start.3
  229.3 2.3 copy-start.15
  231.6 1.3 copy-start.32
  232.2 2.4 copy-start.1
  232.9 1.7 copy-start.8
  234.6 2.0 copy-start.5
  234.6 2.0 copy-start.7
  236.6 1.2 copy-start.23
  244.6 2.7 copy-start.34
  255.6 1.0 copy-start.17
  431.1 4.4 copy-start.12
  435.4 2.9 copy-start.11
  438.3 2.8 copy-start.13
  441.1 2.1 copy-start.19
  443.3 1.5 copy-start.25
  443.3 2.7 copy-start.18
  444.8 2.2 copy-start.29
  445.9 1.9 copy-start.30

commit v6 on v5

--- a/solution.py
+++ b/solution.py
@@ -1383,6 +1383,7 @@
         vector_out[:, 2 * at : 2 * (at + length)] = vec[name]
         at += length
     to_images_wait(tile_in["tokens"], image, tile_send.at[0], tile_recv.at[0], sizes)
+    to_images_start(tile_in["patches"], image_out["patches"], tile_send.at[1], tile_recv.at[1], sizes)
 
     width = image.shape[3]
     x = jnp.where(flag[0:1, 0:1] > 0, image[1].astype(f32), image[0].astype(f32))
@@ -1410,7 +1411,6 @@
     for copy in core_copies:
         copy.wait()
     tick("fc1", "fc2", "conv", "proj")
-    to_images_start(tile_in["patches"], image_out["patches"], tile_send.at[1], tile_recv.at[1], sizes)
     keep(keys, saved["k"])
     keep(values, saved["v"])
     for name in ("qkv",):

time: 455 us -> 455 us (level)
    pallas_call x1, Pallas kernels: 39.2 us -> 31.5 us  [maps_backward(): pl.pallas_call(functools.partial(maps_back_kernel, tiles, cols), out_shap...]
    pallas_call x1, Pallas kernels: 104 us -> 109 us  [run_forward(): pl.pallas_call(functools.partial(forward_kernel, sizes, tiles, lengths),...]
  transfers between devices with their start and end apart: 7 -> 7, of which waited for: 3 -> 3; matrix products, arithmetic and copies ran while one was open for 12% -> 12% of each run, Pallas kernels for 32% -> 31%
where the time goes in v6:
time: 455 us; the launch traced here: 447 us
  Pallas kernels  313 us (69%)
  matrix products  42.7 us (9%)
  other arithmetic  39.1 us (9%)
  local copies, waits for them, and re-layouts  37.8 us (8%)
  starting transfers between devices  7.64 us (2%)
  waiting for transfers between devices  4.59 us (1%)
    pallas_call x1, Pallas kernels, run_backward(): pl.pallas_call(functools.partial(backward_kernel, sizes), out_shape=out_s...  172 us
    pallas_call x1, Pallas kernels, run_forward(): pl.pallas_call(functools.partial(forward_kernel, sizes, tiles, lengths),...  109 us
    pallas_call x1, Pallas kernels, maps_backward(): pl.pallas_call(functools.partial(maps_back_kernel, tiles, cols), out_shap...  31.5 us
    dot_general x7, matrix products, outer_product(): lax.dot_general(first_op, second_op, (((0,), (0,)), ((), ())), preferred_...  24.5 us
    dot_general x5, matrix products, back_product(): lax.dot_general(first_op, weight, (((1,), (1,)), ((), ())), preferred_ele...  17.7 us
    convert_element_type x8, other arithmetic, on_chip(): sums = {name: value.astype(jnp.float32) for name, value in sums.items()}  15.6 us
    unnamed x101, local copies, waits for them, and re-layouts  9.95 us
  transfers between devices with their start and end apart: 7, of which 3 were waited for; matrix products, arithmetic and copies ran while one was open for 12% of the time, Pallas kernels for 31%

profile of v6, /device:TPU:0, one launch (start us, length us, event | category | flops | bytes accessed | tf_op | source)
XLA Modules:
  0.0 447.5 jit_solution(7444696473670825043)
XLA Ops:
  0.7 0.9 convert_element_type.307
  1.6 3.0 collective-permute-start
  5.3 0.9 convert_bitcast_fusion.1
  11.7 2.2 convert_reduce_fusion.1
  18.7 0.9 pad.57.refs_2_
  20.2 109.4 %shard_map.340 = (bf16[2,8,64,768]{3,2,1,0:T(8,128)(2,1)}, bf16[2,8,112,256]{3,2,1,0:T(8,128)(2,1)}, bf16[768,2304]{1,0:T(8,128)(2,1)}, bf16[768,768]{1,0:T(8,12...) custom-call(bf16[10,64,768]{2,1,0:T(8,128)(2,1)} %bitcast.194, ...), custom_call_target="tpu_custom_call" | custom-call | tf_op jit(solution)/shard_map/pallas_call | solution.py:1536
  129.6 1.2 select_bitcast_fusion.2
  136.9 0.8 copy-done.24
  137.7 31.5 %shard_map.341 = (bf16[12,768,128]{2,1,0:T(8,128)(2,1)}, bf16[12,768,128]{2,1,0:T(8,128)(2,1)}, bf16[512,256]{1,0:T(8,128)(2,1)}, bf16[10,112,256]{2,1,0:T(8,128)(2,1)}) custom-call(f32[576,256]{1,0:T(8,128)} %bitcast.179, f32[576,256]{1,0:T(8,128)} %copy-done.24, f32[704,256]{1,0:T(8,128)} %get-tuple-element.66.f0_ref, ...), custom_call_target="tpu_custom_call" | custom-call | tf_op jit(solution)/shard_map/pallas_call | solution.py:1247
  169.3 2.3 collective-permute-start.2
  172.2 1.4 fusion.57
  173.8 1.2 convolution_convert_fusion.7
  176.1 1.1 copy-done.10
  177.3 3.9 fusion.9
  181.2 2.1 dynamic-slice_bitcast_fusion.4
  183.4 7.3 %convert_reduce_fusion = (f32[3072]{0:T(1024)S(1)}, bf16[512,3072]{1,0:T(8,128)(2,1)}) fusion(f32[512,3072]{1,0:T(8,128)S(1)} %bitcast.212, bf16[512,768]{1,0:T(8,128)(2,1)S(1)} %get-tuple-element.111, bf16[3072,768]{1,0:T(8,128)(2,1)S(1)} %bitcast.214), kind=kOutput, calls=%fused_computation.10 | convolution fusion | flops 2450519040 | bytes 14954496 | tf_op jit(solution)/shard_map/dot_general | solution.py:59
  190.7 1.0 slice_convert_fusion
  191.8 1.3 reshape.373
  193.1 0.8 fusion.18
  194.4 2.4 copy.72
  196.8 2.4 reshape.363
  199.7 2.4 copy.73
  202.1 3.4 convert_element_type.345
  205.5 7.8 %multiply_reduce_fusion.1 = (f32[768]{0:T(1024)S(1)}, f32[512]{0:T(512)S(1)}, f32[512]{0:T(512)S(1)}, f32[768]{0:T(1024)S(1)}, f32[512,768]{1,0:T(8,128)}) fusion(f32[512,768]{1,0:T(8,128)S(1)} %copy-done, f32[512]{0:T(512)S(1)} %add_rsqrt_fusion, f32[512]{0:T(512)S(1)} %broadcast_multiply_fusion.5, f32[768]{0:T(1024)S(1)} %get-tuple-element.160, ...), kind=kOutput, calls=%fused_computation.50 | convolution fusion | flops 2419455488 | bytes 11027456 | tf_op jit(solution)/shard_map/dot_general | solution.py:59
  213.3 3.1 fusion.13
  216.5 7.0 %fusion.11 = bf16[1,3072,384]{2,1,0:T(8,128)(2,1)} fusion(bf16[512,768]{1,0:T(8,128)(2,1)S(1)} %copy-done.22, s32[]{:T(128)S(6)} %select_n.122, f32[512,3072]{1,0:T(8,128)} %get-tuple-element.80), kind=kOutput, calls=%fused_computation.21 | convolution fusion | flops 1223294976 | bytes 9043972 | tf_op jit(solution)/shard_map/dot_general | solution.py:53
  224.1 0.9 reshape.359.refs_11_
  225.0 1.3 collective-permute-start.5
  226.9 1.6 multiply_convert_fusion.1
  230.5 1.7 convolution_convert_fusion.6.refs_5_
  232.2 2.0 convolution_convert_fusion.5
  234.2 1.2 fusion.30
  235.4 6.8 %fusion.8 = bf16[1,3072,384]{2,1,0:T(8,128)(2,1)S(1)} fusion(bf16[1,3072,384]{2,1,0:T(8,128)(2,1)} %collective-permute-done.3, bf16[512,768]{1,0:T(8,128)(2,1)S(1)} %copy-done.23, s32[]{:T(128)S(6)} %select_n.121, f32[512,3072]{1,0:T(8,128)} %get-tuple-element.80), kind=kOutput, calls=%fused_computation.14 | convolution fusion | flops 1228013568 | bytes 11403268 | tf_op jit(solution)/shard_map/dot_general | solution.py:53
  242.2 1.7 dynamic-slice_bitcast_fusion.1
  243.9 1.0 copy-done.34
  244.9 3.4 fusion.7
  248.3 1.6 dynamic-slice_bitcast_fusion
  249.9 3.3 collective-permute-done.5.refs_16_
  253.2 1.0 copy-done.17
  254.2 172.4 %shard_map.342 = (bf16[10,64,768]{2,1,0:T(8,128)(2,1)}, bf16[10,64,768]{2,1,0:T(8,128)(2,1)}, bf16[36,2,2,2,16,256]{5,4,3,2,1,0:T(8,128)(2,1)}, bf16[1,2,2,2,16,...) custom-call(bf16[512,768]{1,0:T(8,128)(2,1)} %get-tuple-element.60.r, ...), custom_call_target="tpu_custom_call" | custom-call | tf_op jit(solution)/shard_map/pallas_call | solution.py:1020
  426.6 0.9 convert_element_type.381
  428.6 4.4 bitcast_convert_fusion
  433.0 2.9 bitcast_convert_fusion.1
  435.9 2.8 convert.44
  438.7 2.1 bitcast_convert_fusion.2
  440.8 1.5 select_bitcast_fusion
  442.3 1.1 bitcast_convert_fusion.3
  443.5 1.1 select_bitcast_fusion.1
  (183 shorter events, 26.8 us)
Async XLA Ops:
  0.7 13.3 %copy-start.31 = (f32[384]{0:T(512)S(1)}, f32[384]{0:T(512)}, u32[]{:S(2)}) copy-start(f32[384]{0:T(512)} %param.36) | copy-start | bytes 4612
  1.6 13.0 %collective-permute-start = (bf16[128,256]{1,0:T(8,128)(2,1)S(1)}, bf16[128,256]{1,0:T(8,128)(2,1)S(1)}, u32[]{:S(2)}, u32[]{:S(2)}) collective-permute-start(bf16[128,256]{1,0:T(8,128)(2,1)S(1)} %convert_element_type.307), channel_id=1, source_target_pairs={{0,16},{16,0},{1,17},{17,1},{2,18},{18,2},{3,19},{19,3},{4,20},{20... | collective-permute-start | bytes 196616 | tf_op jit(solution)/shard_map/ppermute | solution.py:1647
  5.3 166.4 %collective-permute-start.6 = (bf16[2,128]{1,0:T(2,128)(2,1)S(1)}, bf16[2,128]{1,0:T(2,128)(2,1)S(1)}, u32[]{:S(2)}, u32[]{:S(2)}) collective-permute-start(bf16[2,128]{1,0:T(2,128)(2,1)S(1)} %get-tuple-element.165), channel_id=1, source_target_pairs={{0,16},{16,0},{1,17},{17,1},{2,18},{18,2},{3,19},{19,3},{4,20},{20... | collective-permute-start | bytes 1544 | tf_op jit(solution)/shard_map/ppermute | solution.py:1647
  13.9 1.6 copy-start.4
  132.2 1.0 copy-start.16
  134.8 2.1 copy-start.9
  134.8 2.1 collective-permute-start.1
  136.9 0.8 copy-start.24
  137.7 34.0 %copy-start = (f32[512,768]{1,0:T(8,128)S(1)}, f32[512,768]{1,0:T(8,128)}, u32[]{:S(2)}) copy-start(f32[512,768]{1,0:T(8,128)} %get-tuple-element.78) | copy-start | bytes 4718596
  169.3 4.3 copy-start.14
  169.3 6.8 %collective-permute-start.2 = (bf16[36,256,128]{2,1,0:T(8,128)(2,1)}, bf16[36,256,128]{2,1,0:T(8,128)(2,1)}, u32[]{:S(2)}, u32[]{:S(2)}) collective-permute-start(bf16[36,256,128]{2,1,0:T(8,128)(2,1)} %bitcast.215), channel_id=1, source_target_pairs={{0,4},{4,0},{8,12},{12,8},{1,5},{5,1},{9,13},{13,9},{2,6},{6,2},{1... | collective-permute-start | bytes 7077896 | tf_op jit(solution)/shard_map/ppermute | solution.py:1590
  172.2 1.6 copy-start.20
  172.2 1.6 copy-start.28
  173.8 1.2 copy-start.27
  175.0 2.2 copy-start.10
  175.0 8.4 %slice-start = ((s8[6291456]{0:T(1024)(128)(4,1)}), s8[4194304]{0:T(1024)(128)(4,1)S(1)}, s32[]{:S(2)}) async-start(s8[6291456]{0:T(1024)(128)(4,1)} %bitcast.211), calls=%async_computation | async-start | bytes 8388608
  175.0 8.4 %slice-start.2 = ((s8[4718592]{0:T(1024)(128)(4,1)}), s8[4194304]{0:T(1024)(128)(4,1)S(1)}, s32[]{:S(2)}) async-start(s8[4718592]{0:T(1024)(128)(4,1)} %bitcast.213), calls=%async_computation.2 | async-start | bytes 8388608
  175.4 7.8 %copy-start.2 = (f32[512,768]{1,0:T(8,128)}, f32[512,768]{1,0:T(8,128)S(1)}, u32[]{:S(2)}) copy-start(f32[512,768]{1,0:T(8,128)S(1)} %bitcast_add_fusion) | copy-start | bytes 4718596
  177.2 6.2 %slice-start.1 = ((s8[6291456]{0:T(1024)(128)(4,1)}), s8[2097152]{0:T(1024)(128)(4,1)S(1)}, s32[]{:S(2)}) async-start(s8[6291456]{0:T(1024)(128)(4,1)} %bitcast.211), calls=%async_computation.1 | async-start | bytes 4194304
  177.3 6.2 %slice-start.3 = ((s8[4718592]{0:T(1024)(128)(4,1)}), s8[524288]{0:T(1024)(128)(4,1)S(1)}, s32[]{:S(2)}) async-start(s8[4718592]{0:T(1024)(128)(4,1)} %bitcast.213), calls=%async_computation.3 | async-start | bytes 1048576
  183.4 7.4 %copy-start.21 = (bf16[512,768]{1,0:T(8,128)(2,1)}, bf16[512,768]{1,0:T(8,128)(2,1)S(1)}, u32[]{:S(2)}) copy-start(bf16[512,768]{1,0:T(8,128)(2,1)S(1)} %get-tuple-element.111) | copy-start | bytes 2359300
  183.4 7.3 %copy-start.26 = (bf16[10,112,256]{2,1,0:T(8,128)(2,1)S(1)}, bf16[10,112,256]{2,1,0:T(8,128)(2,1)}, u32[]{:S(2)}) copy-start(bf16[10,112,256]{2,1,0:T(8,128)(2,1)} %get-tuple-element.91) | copy-start | bytes 1720324
  205.5 20.9 %copy-start.6 = (bf16[16,10,16,256]{3,0,2,1:T(8,128)(2,1)}, bf16[16,10,16,256]{3,0,2,1:T(8,128)(2,1)S(1)}, u32[]{:S(2)}) copy-start(bf16[16,10,16,256]{3,0,2,1:T(8,128)(2,1)S(1)} %convert_element_type.345) | copy-start | bytes 3932164
  205.5 7.8 %copy-start.33 = (bf16[512,3072]{1,0:T(8,128)(2,1)S(1)}, bf16[512,3072]{1,0:T(8,128)(2,1)}, u32[]{:S(2)}) copy-start(bf16[512,3072]{1,0:T(8,128)(2,1)} %get-tuple-element.113) | copy-start | bytes 9437188
  213.3 3.2 copy-start.22
  216.4 27.5 %collective-permute-start.4 = (bf16[1,768,1536]{2,1,0:T(8,128)(2,1)}, bf16[1,768,1536]{2,1,0:T(8,128)(2,1)}, u32[]{:S(2)}, u32[]{:S(2)}) collective-permute-start(bf16[1,768,1536]{2,1,0:T(8,128)(2,1)} %fusion.13), channel_id=1, source_target_pairs={{0,4},{4,0},{8,12},{12,8},{1,5},{5,1},{9,13},{13,9},{2,6},{6,2},{1... | collective-permute-start | bytes 7077896 | tf_op jit(solution)/shard_map/ppermute | solution.py:1590
  223.5 11.9 %collective-permute-start.3 = (bf16[1,3072,384]{2,1,0:T(8,128)(2,1)}, bf16[1,3072,384]{2,1,0:T(8,128)(2,1)}, u32[]{:S(2)}, u32[]{:S(2)}) collective-permute-start(bf16[1,3072,384]{2,1,0:T(8,128)(2,1)} %fusion.11), channel_id=1, source_target_pairs={{0,4},{4,0},{8,12},{12,8},{1,5},{5,1},{9,13},{13,9},{2,6},{6,2},{1... | collective-permute-start | bytes 7077896 | tf_op jit(solution)/shard_map/ppermute | solution.py:1590
  225.0 28.2 %collective-permute-start.5 = (bf16[36,2,2,2,16,128]{5,4,3,2,1,0:T(8,128)(2,1)}, bf16[36,2,2,2,16,128]{5,4,3,2,1,0:T(8,128)(2,1)S(1)}, u32[]{:S(2)}, u32[]{:S(2)}) collective-permute-start(bf16[36,2,2,2,16,128]{5,4,3,2,1,0:T(8,128)(2,1)} %get-tuple-element.90), channel_id=1, source_target_pairs={{0,1},{1,0},{2,3},{3,2},{4,5},{5,4},{6,7},{7,6},{8,9},{9,8},{10,11... | collective-permute-start | bytes 3538952 | tf_op jit(solution)/shard_map/ppermute | solution.py:810
  226.8 1.6 copy-start.3
  226.9 2.3 copy-start.15
  229.2 1.3 copy-start.32
  229.8 2.4 copy-start.1
  230.5 1.7 copy-start.8
  232.2 2.0 copy-start.5
  232.2 2.0 copy-start.7
  234.2 1.2 copy-start.23
  242.2 2.7 copy-start.34
  253.2 1.0 copy-start.17
  428.6 4.4 copy-start.12
  433.0 2.9 copy-start.11
  435.9 2.8 copy-start.13
  438.7 2.1 copy-start.19
  440.8 1.5 copy-start.25
  440.8 2.7 copy-start.18
  442.3 2.2 copy-start.29
  443.5 1.9 copy-start.30
